TPU v7x, 512 devices: a whole 4x4x16 slice. The times are simulated.
512 devices in a mesh: dom: 256 (over x, z, y), band: 2 (over core).
Axes of the slice: x: 4, y: 4, z: 16, core: 2. Of those that a mesh axis runs over, the one named last changes fastest.
Arguments:
- block: bfloat16 [128, 262144], P('band', 'dom')
- cell_nodes: int32 [8192, 125], P('dom'), may hold values from 0 to 1535, as said below
- send_lists: int32 [256, 2, 256], P('dom'), may hold values from 0 to 1023, as said below
- cell_matrix: bfloat16 [125, 125], replicated
- cell_scale: float32 [8192], P('dom'), may hold values from 0.5 to 2
- potential: float32 [262144], P('dom'), may hold values from -1 to 0.5
Outputs:
- ortho_block: float32 [128, 262144], P(None, ('dom', 'band'))
- projected: float32 [128, 128], replicated
Inputs may be any that keep to these rules, and one draw needn't show every extreme that they name: `cell_nodes`: entries below 1024 name the partition's own nodes, from 1024 to 1279 the ghost slots filled by the left neighbour, and the rest those filled by the right neighbour. The first partition's cells use no left slots and the last partition's no right slots; how many slots are used differs from partition to partition. `send_lists`: node indices in the numbering of the sending partition; a node may stand in a list more than once.
All inputs are finite; a program needn't handle non-finite values.
Results may differ from a plain program's by a relative error of at most 0.013.
Values may be sent and summed in bfloat16 or wider, within the bound.
No kernel may reach another device: no remote copies, remote signals or barrier semaphores. Data moves between devices by JAX's collectives and lax.ppermute only.
A program may use at most 64 MiB of HBM per device.

v0:
```python
import jax
import jax.numpy as jnp
from jax import lax
from jax.sharding import PartitionSpec as P


def from_behind(x, axis, by):
    devices = lax.axis_size(axis)
    pairs = [(i, i + by) for i in range(devices) if 0 <= i + by < devices]
    return lax.ppermute(x, axis, pairs)


def lower_solve(factor, right_hand):
    return lax.linalg.triangular_solve(factor, right_hand, left_side=True, lower=True)


def shards(block, cell_nodes, send_lists, cell_matrix, cell_scale, potential):
    cell_grid = cell_nodes.T
    ghost_lists = send_lists[0]
    own_count = block.shape[1]
    slot_count = ghost_lists.shape[1]

    def operate(states_in):
        to_right = states_in[:, ghost_lists[1]]
        to_left = states_in[:, ghost_lists[0]]
        from_left = from_behind(to_right, "dom", 1)
        from_right = from_behind(to_left, "dom", -1)
        extended = jnp.concatenate([states_in, from_left, from_right], axis=1)
        gathered = extended[:, cell_grid]
        product = (
            jnp.einsum("ij,sjc->sic", cell_matrix, gathered, preferred_element_type=jnp.float32)
            * cell_scale[None, None, :]
        )
        summed = (
            jnp.zeros((states_in.shape[0], extended.shape[1]), jnp.float32)
            .at[:, cell_grid]
            .add(product)
        )
        left_slots = summed[:, own_count : own_count + slot_count]
        right_slots = summed[:, own_count + slot_count :]
        incoming_right = from_behind(left_slots, "dom", -1)
        incoming_left = from_behind(right_slots, "dom", 1)
        owned_sum = summed[:, :own_count].at[:, ghost_lists[1]].add(incoming_right)
        owned_sum = owned_sum.at[:, ghost_lists[0]].add(incoming_left)
        return owned_sum + potential[None, :] * states_in.astype(jnp.float32)

    filter_one = operate(block).astype(jnp.bfloat16)
    filter_two = (2.0 * operate(filter_one) - block.astype(jnp.float32)).astype(jnp.bfloat16)
    filtered_local = (2.0 * operate(filter_two) - filter_one.astype(jnp.float32)).astype(
        jnp.bfloat16
    )
    filtered = lax.all_gather(filtered_local, "band", axis=0, tiled=True)
    half_nodes = filtered.shape[1] // lax.axis_size("band")
    own_part = lax.dynamic_slice_in_dim(
        filtered, lax.axis_index("band") * half_nodes, half_nodes, 1
    )
    gram_local = jnp.dot(filtered, filtered.T, preferred_element_type=jnp.float32)
    gram_total = lax.psum(gram_local, "dom")
    image_local = operate(filtered_local).astype(jnp.bfloat16)
    image_cols = lax.all_gather(image_local, "band", axis=0, tiled=True)
    hamil_local = jnp.dot(filtered, image_cols.T, preferred_element_type=jnp.float32)
    hamil_total = lax.psum(hamil_local, "dom")
    node_total = block.shape[1] * lax.axis_size("dom")
    gram = gram_total / node_total
    hamiltonian = hamil_total / node_total
    factor = jnp.linalg.cholesky(gram)
    ortho_block = lower_solve(factor, own_part.astype(jnp.float32))
    half_solved = lower_solve(factor, hamiltonian)
    projected = lower_solve(factor, half_solved.T).T
    return (ortho_block, projected)


def solution(mesh):
    return jax.shard_map(
        shards,
        mesh=mesh,
        in_specs=(P("band", "dom"), P("dom", None), P("dom", None, None), P(), P("dom"), P("dom")),
        out_specs=(P(None, ("dom", "band")), P()),
        check_vma=False,
    )
```

profile of v0, /device:TPU:6, one launch (start us, length us, event | category | flops | bytes accessed | tf_op | source)
XLA Modules:
  0.0 730.5 jit_solution(10926154680158833223)
XLA Ops:
  8.0 1.1 copy.57
  9.1 0.9 gather_fusion
  9.9 3.5 collective-permute-start
  13.4 0.9 gather_fusion.1
  14.3 12.5 %collective-permute-start.1 = (bf16[64,256]{0,1:T(8,128)(2,1)S(1)}, bf16[64,256]{0,1:T(8,128)(2,1)S(1)}, u32[]{:S(2)}, u32[]{:S(2)}) collective-permute-start(bf16[64,256]{0,1:T(8,128)(2,1)S(1)} %bitcast.114), channel_id=1, source_target_pairs={{2,0},{4,2},{6,4},{8,6},{10,8},{12,10},{14,12},{16,14},{18,16},{20... | collective-permute-start | bytes 98312 | tf_op jit(solution)/shard_map/ppermute | solution.py:10
  27.8 0.9 collective-permute-done.1
  28.8 12.3 %gather_fusion.2 = bf16[4000,64]{1,0:T(8,128)(2,1)S(1)} fusion(bf16[64,1536]{0,1:T(8,128)(2,1)S(1)} %pad_maximum_fusion, s32[4096]{0:T(1024)S(1)} %pad_clamp_fusion), kind=kCustom, calls=%fused_computation.2 | custom fusion | bytes 1040000 | tf_op jit(solution)/shard_map/gather | solution.py:29
  41.2 1.2 copy.58
  42.7 2.8 copy.59
  45.5 22.9 %scatter_custom_fusion = f32[64,1536]{0,1:T(8,128)S(1)} fusion(s32[4000]{0:T(1024)S(1)} %reshape.229, f32[4000,64]{1,0:T(8,128)} %bitcast.108, f32[]{:T(128)} %constant.55.clone.1), kind=kCustom, calls=%fused_computation.58 | custom fusion | flops 256000 | bytes 393728 | tf_op jit(solution)/shard_map/scatter-add | solution.py:37
  68.4 8.5 %collective-permute-start.2 = (f32[64,256]{0,1:T(8,128)S(1)}, f32[64,256]{0,1:T(8,128)S(1)}, u32[]{:S(2)}, u32[]{:S(2)}) collective-permute-start(f32[64,256]{0,1:T(8,128)S(1)} %get-tuple-element.20), channel_id=1, source_target_pairs={{2,0},{4,2},{6,4},{8,6},{10,8},{12,10},{14,12},{16,14},{18,16},{20... | collective-permute-start | bytes 196616 | tf_op jit(solution)/shard_map/ppermute | solution.py:10
  76.9 1.9 collective-permute-start.3
  79.4 2.1 scatter_custom_fusion.1
  81.6 6.4 collective-permute-done.3
  88.0 2.1 scatter_custom_fusion.2
  90.2 0.9 gather_fusion.3
  91.0 0.9 gather_fusion.4
  91.9 1.9 collective-permute-start.4
  93.8 8.4 %collective-permute-start.5 = (bf16[64,256]{0,1:T(8,128)(2,1)S(1)}, bf16[64,256]{0,1:T(8,128)(2,1)S(1)}, u32[]{:S(2)}, u32[]{:S(2)}) collective-permute-start(bf16[64,256]{0,1:T(8,128)(2,1)S(1)} %bitcast.115), channel_id=1, source_target_pairs={{2,0},{4,2},{6,4},{8,6},{10,8},{12,10},{14,12},{16,14},{18,16},{20... | collective-permute-start | bytes 98312 | tf_op jit(solution)/shard_map/ppermute | solution.py:10
  102.3 1.6 collective-permute-done.5
  103.9 12.3 %gather_fusion.5 = bf16[4000,64]{1,0:T(8,128)(2,1)S(1)} fusion(bf16[64,1536]{0,1:T(8,128)(2,1)S(1)} %pad_maximum_fusion.1, s32[4096]{0:T(1024)S(1)} %pad_clamp_fusion), kind=kCustom, calls=%fused_computation.5 | custom fusion | bytes 1040000 | tf_op jit(solution)/shard_map/gather | solution.py:29
  116.3 1.2 copy.61
  117.8 2.8 copy.62
  120.6 22.9 %scatter_custom_fusion.3 = f32[64,1536]{0,1:T(8,128)S(1)} fusion(s32[4000]{0:T(1024)S(1)} %reshape.229, f32[4000,64]{1,0:T(8,128)} %bitcast.109, f32[]{:T(128)} %constant.55.clone.1), kind=kCustom, calls=%fused_computation.56 | custom fusion | flops 256000 | bytes 393728 | tf_op jit(solution)/shard_map/scatter-add | solution.py:37
  143.5 8.5 %collective-permute-start.6 = (f32[64,256]{0,1:T(8,128)S(1)}, f32[64,256]{0,1:T(8,128)S(1)}, u32[]{:S(2)}, u32[]{:S(2)}) collective-permute-start(f32[64,256]{0,1:T(8,128)S(1)} %get-tuple-element.18), channel_id=1, source_target_pairs={{2,0},{4,2},{6,4},{8,6},{10,8},{12,10},{14,12},{16,14},{18,16},{20... | collective-permute-start | bytes 196616 | tf_op jit(solution)/shard_map/ppermute | solution.py:10
  152.0 1.9 collective-permute-start.7
  154.5 2.1 scatter_custom_fusion.4
  156.7 6.4 collective-permute-done.7
  163.1 2.1 scatter_custom_fusion.5
  165.3 0.9 gather_fusion.6
  167.0 1.9 collective-permute-start.8
  168.9 8.7 %collective-permute-start.9 = (bf16[64,256]{0,1:T(8,128)(2,1)S(1)}, bf16[64,256]{0,1:T(8,128)(2,1)S(1)}, u32[]{:S(2)}, u32[]{:S(2)}) collective-permute-start(bf16[64,256]{0,1:T(8,128)(2,1)S(1)} %bitcast.116), channel_id=1, source_target_pairs={{2,0},{4,2},{6,4},{8,6},{10,8},{12,10},{14,12},{16,14},{18,16},{20... | collective-permute-start | bytes 98312 | tf_op jit(solution)/shard_map/ppermute | solution.py:10
  177.6 1.3 collective-permute-done.9
  179.1 12.3 %gather_fusion.8 = bf16[4000,64]{1,0:T(8,128)(2,1)S(1)} fusion(bf16[64,1536]{0,1:T(8,128)(2,1)S(1)} %pad_maximum_fusion.2, s32[4096]{0:T(1024)S(1)} %pad_clamp_fusion), kind=kCustom, calls=%fused_computation.8 | custom fusion | bytes 1040000 | tf_op jit(solution)/shard_map/gather | solution.py:29
  191.4 1.2 copy.63
  192.9 2.8 copy.64
  195.7 22.9 %scatter_custom_fusion.6 = f32[64,1536]{0,1:T(8,128)S(1)} fusion(s32[4000]{0:T(1024)S(1)} %reshape.229, f32[4000,64]{1,0:T(8,128)} %bitcast.110, f32[]{:T(128)} %constant.55.clone.1), kind=kCustom, calls=%fused_computation.54 | custom fusion | flops 256000 | bytes 393728 | tf_op jit(solution)/shard_map/scatter-add | solution.py:37
  218.6 8.5 %collective-permute-start.10 = (f32[64,256]{0,1:T(8,128)S(1)}, f32[64,256]{0,1:T(8,128)S(1)}, u32[]{:S(2)}, u32[]{:S(2)}) collective-permute-start(f32[64,256]{0,1:T(8,128)S(1)} %get-tuple-element.16), channel_id=1, source_target_pairs={{2,0},{4,2},{6,4},{8,6},{10,8},{12,10},{14,12},{16,14},{18,16},{20... | collective-permute-start | bytes 196616 | tf_op jit(solution)/shard_map/ppermute | solution.py:10
  227.1 1.9 collective-permute-start.11
  229.6 2.1 scatter_custom_fusion.7
  231.8 6.4 collective-permute-done.11
  238.2 2.1 scatter_custom_fusion.8
  240.4 0.9 gather_fusion.9
  242.3 1.9 collective-permute-start.12
  244.2 8.1 %collective-permute-start.13 = (bf16[64,256]{0,1:T(8,128)(2,1)S(1)}, bf16[64,256]{0,1:T(8,128)(2,1)S(1)}, u32[]{:S(2)}, u32[]{:S(2)}) collective-permute-start(bf16[64,256]{0,1:T(8,128)(2,1)S(1)} %bitcast.112), channel_id=1, source_target_pairs={{2,0},{4,2},{6,4},{8,6},{10,8},{12,10},{14,12},{16,14},{18,16},{20... | collective-permute-start | bytes 98312 | tf_op jit(solution)/shard_map/ppermute | solution.py:10
  252.4 2.2 all_gather.6
  254.5 0.9 fusion.55
  255.5 12.3 %gather_fusion.11 = bf16[4000,64]{1,0:T(8,128)(2,1)S(1)} fusion(bf16[64,1536]{0,1:T(8,128)(2,1)S(1)} %pad_maximum_fusion.3, s32[4096]{0:T(1024)S(1)} %pad_clamp_fusion), kind=kCustom, calls=%fused_computation.11 | custom fusion | bytes 1040000 | tf_op jit(solution)/shard_map/gather | solution.py:29
  267.8 1.2 copy.68
  269.3 2.8 copy.69
  272.1 22.9 %scatter_custom_fusion.9 = f32[64,1536]{0,1:T(8,128)S(1)} fusion(s32[4000]{0:T(1024)S(1)} %reshape.229, f32[4000,64]{1,0:T(8,128)} %bitcast.107, f32[]{:T(128)} %constant.55.clone.1), kind=kCustom, calls=%fused_computation.52 | custom fusion | flops 256000 | bytes 393728 | tf_op jit(solution)/shard_map/scatter-add | solution.py:37
  295.1 7.3 %collective-permute-start.14 = (f32[64,256]{0,1:T(8,128)S(1)}, f32[64,256]{0,1:T(8,128)S(1)}, u32[]{:S(2)}, u32[]{:S(2)}) collective-permute-start(f32[64,256]{0,1:T(8,128)S(1)} %get-tuple-element.14), channel_id=1, source_target_pairs={{2,0},{4,2},{6,4},{8,6},{10,8},{12,10},{14,12},{16,14},{18,16},{20... | collective-permute-start | bytes 196616 | tf_op jit(solution)/shard_map/ppermute | solution.py:10
  302.4 1.9 collective-permute-start.15
  304.9 2.1 scatter_custom_fusion.10
  307.0 6.4 collective-permute-done.15
  313.5 2.1 scatter_custom_fusion.11
  315.8 2.2 all_gather.7
  318.0 0.9 fusion.56
  318.9 376.7 %all-reduce.3.cloned.1.call-done = (f32[128,128]{0,1:T(8,128)}, f32[128,128]{0,1:T(8,128)}) async-done(((f32[128,128]{0,1:T(8,128)}, f32[128,128]{0,1:T(8,128)}), (f32[128,128]{0,1:T(8,128)}, f32[128,128]{0,1:T(8,128)})) %all-reduce.3.cloned.1.call-update) | async-done | bytes 131088 | tf_op jit(solution)/shard_map/psum | solution.py:58
  696.5 0.9 fusion.42
  697.4 11.7 %cholesky.16 = f32[128,128]{1,0:T(8,128)S(1)} custom-call(f32[128,128]{1,0:T(8,128)S(1)} %fusion.42), custom_call_target="Cholesky" | custom-call | tf_op jit(solution)/shard_map/jit(cholesky)/cholesky | solution.py:66
  710.4 9.8 %custom-call.9 = f32[1,128,128]{1,2,0:T(8,128)S(1)} custom-call(f32[1,128,128]{2,1,0:T(8,128)S(1)} %fusion.38), custom_call_target="InvertDiagBlocksLowerTriangular" | custom-call | tf_op jit(solution)/shard_map/triangular_solve | solution.py:14
  720.2 1.1 convolution_bitcast_fusion.1
  722.4 1.0 fusion.36
  (54 shorter events, 11.1 us)
Async XLA Ops:
  7.2 35.2 %copy-start = (bf16[125,125]{1,0:T(8,128)(2,1)S(1)}, bf16[125,125]{1,0:T(8,128)(2,1)}, u32[]{:S(2)}) copy-start(bf16[125,125]{1,0:T(8,128)(2,1)} %param.11) | copy-start | bytes 93754
  7.2 688.4 %all-reduce.3.cloned.1.call-start = ((), (), s32[]{:S(2)}) async-start(), calls=%async_computation | async-start | bytes 262144 | tf_op jit(solution)/shard_map/psum | solution.py:58
  9.9 17.8 %collective-permute-start = (bf16[64,256]{0,1:T(8,128)(2,1)S(1)}, bf16[64,256]{0,1:T(8,128)(2,1)S(1)}, u32[]{:S(2)}, u32[]{:S(2)}) collective-permute-start(bf16[64,256]{0,1:T(8,128)(2,1)S(1)} %bitcast.111), channel_id=1, source_target_pairs={{0,2},{2,4},{4,6},{6,8},{8,10},{10,12},{12,14},{14,16},{16,18},{18... | collective-permute-start | bytes 98312 | tf_op jit(solution)/shard_map/ppermute | solution.py:10
  14.3 14.4 %collective-permute-start.1 = (bf16[64,256]{0,1:T(8,128)(2,1)S(1)}, bf16[64,256]{0,1:T(8,128)(2,1)S(1)}, u32[]{:S(2)}, u32[]{:S(2)}) collective-permute-start(bf16[64,256]{0,1:T(8,128)(2,1)S(1)} %bitcast.114), channel_id=1, source_target_pairs={{2,0},{4,2},{6,4},{8,6},{10,8},{12,10},{14,12},{16,14},{18,16},{20... | collective-permute-start | bytes 98312 | tf_op jit(solution)/shard_map/ppermute | solution.py:10
  28.8 13.5 %copy-start.2 = (f32[32]{0:T(128)S(1)}, f32[32]{0:T(128)}, u32[]{:S(2)}) copy-start(f32[32]{0:T(128)} %param.12) | copy-start | bytes 388
  42.7 36.2 %copy-start.1 = (f32[1024]{0:T(1024)S(1)}, f32[1024]{0:T(1024)}, u32[]{:S(2)}) copy-start(f32[1024]{0:T(1024)} %param.13) | copy-start | bytes 12292
  68.4 11.0 %collective-permute-start.2 = (f32[64,256]{0,1:T(8,128)S(1)}, f32[64,256]{0,1:T(8,128)S(1)}, u32[]{:S(2)}, u32[]{:S(2)}) collective-permute-start(f32[64,256]{0,1:T(8,128)S(1)} %get-tuple-element.20), channel_id=1, source_target_pairs={{2,0},{4,2},{6,4},{8,6},{10,8},{12,10},{14,12},{16,14},{18,16},{20... | collective-permute-start | bytes 196616 | tf_op jit(solution)/shard_map/ppermute | solution.py:10
  76.9 11.1 %collective-permute-start.3 = (f32[64,256]{0,1:T(8,128)S(1)}, f32[64,256]{0,1:T(8,128)S(1)}, u32[]{:S(2)}, u32[]{:S(2)}) collective-permute-start(f32[64,256]{0,1:T(8,128)S(1)} %get-tuple-element.19), channel_id=1, source_target_pairs={{0,2},{2,4},{4,6},{6,8},{8,10},{10,12},{12,14},{14,16},{16,18},{18... | collective-permute-start | bytes 196616 | tf_op jit(solution)/shard_map/ppermute | solution.py:10
  91.9 10.4 %collective-permute-start.4 = (bf16[64,256]{0,1:T(8,128)(2,1)S(1)}, bf16[64,256]{0,1:T(8,128)(2,1)S(1)}, u32[]{:S(2)}, u32[]{:S(2)}) collective-permute-start(bf16[64,256]{0,1:T(8,128)(2,1)S(1)} %bitcast.117), channel_id=1, source_target_pairs={{0,2},{2,4},{4,6},{6,8},{8,10},{10,12},{12,14},{14,16},{16,18},{18... | collective-permute-start | bytes 98312 | tf_op jit(solution)/shard_map/ppermute | solution.py:10
  93.8 10.0 %collective-permute-start.5 = (bf16[64,256]{0,1:T(8,128)(2,1)S(1)}, bf16[64,256]{0,1:T(8,128)(2,1)S(1)}, u32[]{:S(2)}, u32[]{:S(2)}) collective-permute-start(bf16[64,256]{0,1:T(8,128)(2,1)S(1)} %bitcast.115), channel_id=1, source_target_pairs={{2,0},{4,2},{6,4},{8,6},{10,8},{12,10},{14,12},{16,14},{18,16},{20... | collective-permute-start | bytes 98312 | tf_op jit(solution)/shard_map/ppermute | solution.py:10
  143.5 11.0 %collective-permute-start.6 = (f32[64,256]{0,1:T(8,128)S(1)}, f32[64,256]{0,1:T(8,128)S(1)}, u32[]{:S(2)}, u32[]{:S(2)}) collective-permute-start(f32[64,256]{0,1:T(8,128)S(1)} %get-tuple-element.18), channel_id=1, source_target_pairs={{2,0},{4,2},{6,4},{8,6},{10,8},{12,10},{14,12},{16,14},{18,16},{20... | collective-permute-start | bytes 196616 | tf_op jit(solution)/shard_map/ppermute | solution.py:10
  152.0 11.1 %collective-permute-start.7 = (f32[64,256]{0,1:T(8,128)S(1)}, f32[64,256]{0,1:T(8,128)S(1)}, u32[]{:S(2)}, u32[]{:S(2)}) collective-permute-start(f32[64,256]{0,1:T(8,128)S(1)} %get-tuple-element.17), channel_id=1, source_target_pairs={{0,2},{2,4},{4,6},{6,8},{8,10},{10,12},{12,14},{14,16},{16,18},{18... | collective-permute-start | bytes 196616 | tf_op jit(solution)/shard_map/ppermute | solution.py:10
  167.0 10.6 %collective-permute-start.8 = (bf16[64,256]{0,1:T(8,128)(2,1)S(1)}, bf16[64,256]{0,1:T(8,128)(2,1)S(1)}, u32[]{:S(2)}, u32[]{:S(2)}) collective-permute-start(bf16[64,256]{0,1:T(8,128)(2,1)S(1)} %bitcast.118), channel_id=1, source_target_pairs={{0,2},{2,4},{4,6},{6,8},{8,10},{10,12},{12,14},{14,16},{16,18},{18... | collective-permute-start | bytes 98312 | tf_op jit(solution)/shard_map/ppermute | solution.py:10
  168.9 10.0 %collective-permute-start.9 = (bf16[64,256]{0,1:T(8,128)(2,1)S(1)}, bf16[64,256]{0,1:T(8,128)(2,1)S(1)}, u32[]{:S(2)}, u32[]{:S(2)}) collective-permute-start(bf16[64,256]{0,1:T(8,128)(2,1)S(1)} %bitcast.116), channel_id=1, source_target_pairs={{2,0},{4,2},{6,4},{8,6},{10,8},{12,10},{14,12},{16,14},{18,16},{20... | collective-permute-start | bytes 98312 | tf_op jit(solution)/shard_map/ppermute | solution.py:10
  218.6 11.0 %collective-permute-start.10 = (f32[64,256]{0,1:T(8,128)S(1)}, f32[64,256]{0,1:T(8,128)S(1)}, u32[]{:S(2)}, u32[]{:S(2)}) collective-permute-start(f32[64,256]{0,1:T(8,128)S(1)} %get-tuple-element.16), channel_id=1, source_target_pairs={{2,0},{4,2},{6,4},{8,6},{10,8},{12,10},{14,12},{16,14},{18,16},{20... | collective-permute-start | bytes 196616 | tf_op jit(solution)/shard_map/ppermute | solution.py:10
  227.1 11.1 %collective-permute-start.11 = (f32[64,256]{0,1:T(8,128)S(1)}, f32[64,256]{0,1:T(8,128)S(1)}, u32[]{:S(2)}, u32[]{:S(2)}) collective-permute-start(f32[64,256]{0,1:T(8,128)S(1)} %get-tuple-element.15), channel_id=1, source_target_pairs={{0,2},{2,4},{4,6},{6,8},{8,10},{10,12},{12,14},{14,16},{16,18},{18... | collective-permute-start | bytes 196616 | tf_op jit(solution)/shard_map/ppermute | solution.py:10
  242.3 13.1 %collective-permute-start.12 = (bf16[64,256]{0,1:T(8,128)(2,1)S(1)}, bf16[64,256]{0,1:T(8,128)(2,1)S(1)}, u32[]{:S(2)}, u32[]{:S(2)}) collective-permute-start(bf16[64,256]{0,1:T(8,128)(2,1)S(1)} %bitcast.113), channel_id=1, source_target_pairs={{0,2},{2,4},{4,6},{6,8},{8,10},{10,12},{12,14},{14,16},{16,18},{18... | collective-permute-start | bytes 98312 | tf_op jit(solution)/shard_map/ppermute | solution.py:10
  244.2 11.2 %collective-permute-start.13 = (bf16[64,256]{0,1:T(8,128)(2,1)S(1)}, bf16[64,256]{0,1:T(8,128)(2,1)S(1)}, u32[]{:S(2)}, u32[]{:S(2)}) collective-permute-start(bf16[64,256]{0,1:T(8,128)(2,1)S(1)} %bitcast.112), channel_id=1, source_target_pairs={{2,0},{4,2},{6,4},{8,6},{10,8},{12,10},{14,12},{16,14},{18,16},{20... | collective-permute-start | bytes 98312 | tf_op jit(solution)/shard_map/ppermute | solution.py:10
  295.1 9.8 %collective-permute-start.14 = (f32[64,256]{0,1:T(8,128)S(1)}, f32[64,256]{0,1:T(8,128)S(1)}, u32[]{:S(2)}, u32[]{:S(2)}) collective-permute-start(f32[64,256]{0,1:T(8,128)S(1)} %get-tuple-element.14), channel_id=1, source_target_pairs={{2,0},{4,2},{6,4},{8,6},{10,8},{12,10},{14,12},{16,14},{18,16},{20... | collective-permute-start | bytes 196616 | tf_op jit(solution)/shard_map/ppermute | solution.py:10
  302.4 11.1 %collective-permute-start.15 = (f32[64,256]{0,1:T(8,128)S(1)}, f32[64,256]{0,1:T(8,128)S(1)}, u32[]{:S(2)}, u32[]{:S(2)}) collective-permute-start(f32[64,256]{0,1:T(8,128)S(1)} %get-tuple-element.13), channel_id=1, source_target_pairs={{0,2},{2,4},{4,6},{6,8},{8,10},{10,12},{12,14},{14,16},{16,18},{18... | collective-permute-start | bytes 196616 | tf_op jit(solution)/shard_map/ppermute | solution.py:10
Sparse Core Ops, SparseCore 0:
  319.0 376.5 all-reduce.2
where the time goes:
time: 739 us; the launch traced here: 730 us
  waiting for transfers between devices  408 us (55%)
  other arithmetic  136 us (18%)
  starting transfers between devices  87.5 us (12%)
  local copies, waits for them, and re-layouts  74.5 us (10%)
  between operations  14.8 us (2%)
    psum x1, waiting for transfers between devices, shards(): gram_total = lax.psum(gram_local, 'dom')  377 us
    scatter-add x4, other arithmetic, operate(): summed = jnp.zeros((states_in.shape[0], extended.shape[1]), jnp.float32)....  91.6 us
    ppermute x16, starting transfers between devices, from_behind(): return lax.ppermute(x, axis, pairs)  87.5 us
    gather x8, local copies, waits for them, and re-layouts, operate(): gathered = extended[:, cell_grid]  54 us
    ppermute x16, waiting for transfers between devices, from_behind(): return lax.ppermute(x, axis, pairs)  31.1 us
  transfers between devices with their start and end apart: 17, of which 12 were waited for; matrix products, arithmetic and copies ran while one was open for 2% of the time, Pallas kernels for 0%

commit v1 on v0

v1 whole, which is shorter than its diff:
```python
import jax
import jax.numpy as jnp
from jax import lax
from jax.experimental import pallas as pl
from jax.experimental.pallas import tpu as pltpu
from jax.sharding import PartitionSpec as P

BOTH = ("dom", "band")
BF16 = jnp.bfloat16
F32 = jnp.float32
CELL_PAD = 128
MIB = 1 << 20


def spec(space=pltpu.VMEM):
    return pl.BlockSpec(memory_space=space)


def nn(a, b):
    return lax.dot_general(a, b, (((1,), (0,)), ((), ())), preferred_element_type=F32)


def nt(a, b):
    return lax.dot_general(a, b, (((1,), (1,)), ((), ())), preferred_element_type=F32)


def one_hot(rows, row):
    hit = lax.broadcasted_iota(row.dtype, (rows, row.shape[1]), 0) == row
    return hit.astype(F32).astype(BF16)


def pair_mask(column, row):
    return (column == row).astype(F32).astype(BF16)


def send_body(block_ref, lists_ref, left_ref, right_ref):
    own = block_ref.shape[1]
    states = block_ref.shape[0]
    lists = lists_ref[...]
    slots = lists.shape[1]
    part = lax.broadcasted_iota(jnp.int32, (16, slots), 0)
    codes = jnp.zeros((16, slots), jnp.int32)
    for side in (0, 1):
        one = lists[side : side + 1]
        codes = jnp.where(part == 2 * side, one >> 5, codes)
        codes = jnp.where(part == 2 * side + 1, one & 31, codes)
    codes = codes.astype(F32).astype(BF16)
    for side, out in ((0, left_ref), (1, right_ref)):
        out[0:states, :] = nn(block_ref[...], one_hot(own, lists[side : side + 1])).astype(BF16)
        out[states : states + 16, :] = codes


def send_first(block, lists):
    states, slots = block.shape[0], lists.shape[1]
    shape = jax.ShapeDtypeStruct((states + 16, slots), BF16)
    return pl.pallas_call(
        send_body,
        out_shape=(shape, shape),
        in_specs=[spec()] * 2,
        out_specs=(spec(), spec()),
        name="send_first",
    )(block, lists)


def build_body(band_ref, nodes_ref, matrix_ref, scale_ref, out_ref, ids, mats, hot, left):
    cells, entries = nodes_ref.shape
    half, full = out_ref.shape
    ids[...] = jnp.full(ids.shape, -1, jnp.int32)
    ids[:, 0:entries] = nodes_ref[...]
    mats[...] = jnp.zeros(mats.shape, F32)
    matrix = matrix_ref[...].astype(F32)
    mats[0:entries, 0:entries] = matrix
    mats[CELL_PAD : CELL_PAD + entries, CELL_PAD : CELL_PAD + entries] = matrix
    pair_matrix = mats[...].astype(BF16)
    first = pl.multiple_of(band_ref[0] * half, 128)
    lane = lax.broadcasted_iota(jnp.int32, (1, 2 * CELL_PAD), 1)
    for pair in range(cells // 2):
        cols = slice(pair * 2 * CELL_PAD, (pair + 1) * 2 * CELL_PAD)
        for one in (0, 1):
            c = 2 * pair + one
            hot[:, c * CELL_PAD : (c + 1) * CELL_PAD] = one_hot(full, ids[c : c + 1, :])
        gain = jnp.where(lane < CELL_PAD, scale_ref[2 * pair], scale_ref[2 * pair + 1])
        left[:, cols] = (nt(hot[pl.ds(first, half), cols], pair_matrix) * gain).astype(BF16)

    @pl.loop(0, full // 256)
    def _(tile):
        rows = pl.ds(pl.multiple_of(tile * 256, 256), 256)
        out_ref[:, rows] = nt(left[...], hot[rows, :]).astype(BF16)


def build(band, cell_nodes, cell_matrix, cell_scale, full):
    cells = cell_nodes.shape[0]
    half = full // 2
    entries = cells * CELL_PAD
    return pl.pallas_call(
        build_body,
        out_shape=jax.ShapeDtypeStruct((half, full), BF16),
        in_specs=[spec(pltpu.SMEM), spec(), spec(), spec(pltpu.SMEM)],
        out_specs=spec(),
        scratch_shapes=[
            pltpu.VMEM((cells, CELL_PAD), jnp.int32),
            pltpu.VMEM((2 * CELL_PAD, 2 * CELL_PAD), F32),
            pltpu.VMEM((full, entries), BF16),
            pltpu.VMEM((half, entries), BF16),
        ],
        compiler_params=pltpu.CompilerParams(vmem_limit_bytes=44 * MIB),
        cost_estimate=pl.CostEstimate(
            flops=2 * half * entries * full, bytes_accessed=2 * half * full, transcendentals=0
        ),
        name="build",
    )(band, cell_nodes, cell_matrix, cell_scale)


def decode(codes_ref):
    slots = codes_ref.shape[1]
    codes = codes_ref[codes_ref.shape[0] - 16 :, :].astype(F32)
    rows = [codes[2 * s : 2 * s + 1] * 32.0 + codes[2 * s + 1 : 2 * s + 2] for s in (0, 1)]
    part = lax.broadcasted_iota(jnp.int32, (8, slots), 0)
    both = jnp.where(part == 0, rows[0], rows[1])
    columns = both.T
    return rows, [columns[:, 0:1], columns[:, 1:2]]


def assemble(partial_ref, ghost_ref, got_ref, lists, from_left_ref, from_right_ref, own):
    slots = lists.shape[1]
    (left_rows, left_cols), (right_rows, right_cols) = decode(from_left_ref), decode(from_right_ref)
    ghost = ghost_ref[...]
    ghost_left, ghost_right = ghost[:, 0:slots], ghost[:, slots : 2 * slots]
    states = ghost.shape[0]
    got_left, got_right = got_ref[0:states, :], got_ref[states : 2 * states, :]
    near_left, near_right = got_left[:, 0:slots], got_right[:, 0:slots]
    whole_own = (
        partial_ref[...]
        + nt(near_left, one_hot(own, lists[0:1]))
        + nt(near_right, one_hot(own, lists[1:2]))
    )
    whole_left = (
        got_left[:, slots : 2 * slots].astype(F32)
        + nn(got_left[:, 2 * slots : 3 * slots], pair_mask(left_cols[0], left_rows[1]))
        + nn(ghost_left, pair_mask(left_cols[1], left_rows[1]))
    )
    whole_right = (
        got_right[:, slots : 2 * slots].astype(F32)
        + nn(got_right[:, 2 * slots : 3 * slots], pair_mask(right_cols[1], right_rows[0]))
        + nn(ghost_right, pair_mask(right_cols[0], right_rows[0]))
    )
    return whole_own, whole_left, whole_right


def apply_body(band_ref, x, w_ref, potential_ref, lists, partial_out, ghost_out, near_out, far_out):
    own = partial_out.shape[1]
    slots = lists.shape[1]
    result = nn(x, w_ref[...])
    partial = result[:, 0:own] + potential_ref[...] * x[:, 0:own].astype(F32)
    partial_out[...] = partial
    ghost = result[:, own:].astype(BF16)
    ghost_out[...] = ghost
    right = band_ref[0] == 1
    mine = jnp.where(right, lists[1:2], lists[0:1])
    edge = jnp.where(right, ghost[:, slots : 2 * slots], ghost[:, 0:slots])
    near_out[:, 0:slots] = edge
    near_out[:, slots : 2 * slots] = nn(partial.astype(BF16), one_hot(own, mine)).astype(BF16)
    far_out[...] = edge


def first_body(band_ref, x_ref, w_ref, potential_ref, lists_ref, partial_out, ghost_out, near_out, far_out):
    apply_body(
        band_ref, x_ref[...], w_ref, potential_ref, lists_ref[...], partial_out, ghost_out, near_out, far_out
    )


def new_states(older_ref, x_out, pieces):
    own = pieces[0].shape[1]
    slots = pieces[1].shape[1]
    at = 0
    for piece in pieces:
        cols = slice(at, at + piece.shape[1])
        if older_ref is not None:
            piece = 2.0 * piece - older_ref[:, cols].astype(F32)
        x_out[:, cols] = piece.astype(BF16)
        at += piece.shape[1]


def next_body(chebyshev, *refs):
    if chebyshev:
        band_ref, w_ref, potential_ref, lists_ref, fl_ref, fr_ref, partial_ref, ghost_ref, got_ref, older_ref = refs[:10]
        refs = refs[10:]
    else:
        band_ref, w_ref, potential_ref, lists_ref, fl_ref, fr_ref, partial_ref, ghost_ref, got_ref = refs[:9]
        older_ref, refs = None, refs[9:]
    x_out, partial_out, ghost_out, near_out, far_out = refs
    lists = lists_ref[...]
    own = partial_ref.shape[1]
    new_states(older_ref, x_out, assemble(partial_ref, ghost_ref, got_ref, lists, fl_ref, fr_ref, own))
    apply_body(
        band_ref, x_out[...], w_ref, potential_ref, lists, partial_out, ghost_out, near_out, far_out
    )


def last_body(
    band_ref, w_ref, potential_ref, lists_ref, fl_ref, fr_ref, partial_ref, ghost_ref, got_ref, older_ref,
    own_out, sums_out, x_all, pot,
):
    lists = lists_ref[...]
    own = partial_ref.shape[1]
    states = partial_ref.shape[0]
    slots = lists.shape[1]
    new_states(older_ref, x_all, assemble(partial_ref, ghost_ref, got_ref, lists, fl_ref, fr_ref, own))
    pot[...] = potential_ref[...]
    half = own // 2
    mine = pl.ds(pl.multiple_of(band_ref[0] * half, 128), half)
    edge = pl.ds(pl.multiple_of(own + band_ref[0] * slots, 128), slots)
    x = x_all[...]
    x_mine = x_all[:, mine]
    own_out[...] = x_mine
    sums_out[:, 0:states] = nt(x_mine, x_mine)
    image = (nn(x, w_ref[:, mine]) + pot[:, mine] * x_mine.astype(F32)).astype(BF16)
    image_edge = nn(x, w_ref[:, edge]).astype(BF16)
    sums_out[:, states : 2 * states] = nt(x_mine, image) + nt(x_all[:, edge], image_edge)


def apply_shapes(states, own, slots):
    return (
        jax.ShapeDtypeStruct((states, own), F32),
        jax.ShapeDtypeStruct((states, 2 * slots), BF16),
        jax.ShapeDtypeStruct((states, 2 * slots), BF16),
        jax.ShapeDtypeStruct((states, slots), BF16),
    )


def stage_call(body, args, shapes, name, scratch=()):
    return pl.pallas_call(
        body,
        out_shape=tuple(shapes),
        in_specs=[spec(pltpu.SMEM)] + [spec()] * (len(args) - 1),
        out_specs=tuple(spec() for _ in shapes),
        scratch_shapes=list(scratch),
        compiler_params=pltpu.CompilerParams(vmem_limit_bytes=32 * MIB),
        name=name,
    )(*args)


def shift(x, axis, by):
    devices = lax.axis_size(axis)
    return lax.ppermute(x, axis, [(i, i + by) for i in range(devices) if 0 <= i + by < devices])


def across(x, by):
    parts = lax.axis_size("dom")
    pairs = [(2 * d + 1, 2 * (d + by)) for d in range(parts - by)]
    pairs += [(2 * (d + by), 2 * d + 1) for d in range(parts - by)]
    return lax.ppermute(x, BOTH, pairs)


def exchange(near, far):
    got = jnp.concatenate([across(near, 1), across(far, 2)], axis=1)
    return lax.all_gather(got, "band", axis=0, tiled=True)


def group_lists():
    eights, along_z, along_x = {}, {}, {}
    for x in range(4):
        for z in range(16):
            for y in range(4):
                for b in range(2):
                    i = ((x * 16 + z) * 4 + y) * 2 + b
                    eights.setdefault((x, z), []).append(i)
                    along_z.setdefault((x, z // 8, y, b), []).append(i)
                    along_x.setdefault((z % 8, y, b), []).append(i)
    return [list(g.values()) for g in (eights, along_z, along_x)]


def swap_pieces(x, groups):
    return lax.all_to_all(x, BOTH, 0, 0, axis_index_groups=groups, tiled=True)


def sum_everywhere(x):
    rows, cols = x.shape
    eights, along_z, along_x = group_lists()
    piece = swap_pieces(x, eights).reshape(8, rows // 8, cols).sum(0)
    for groups in (along_z, along_x):
        copies = jnp.broadcast_to(piece[None], (8,) + piece.shape).reshape(rows, cols)
        piece = swap_pieces(copies, groups).reshape(8, rows // 8, cols).sum(0)
    copies = jnp.broadcast_to(piece[None], (8,) + piece.shape).reshape(rows, cols)
    return swap_pieces(copies, eights)


def lower_solve(factor, right_hand):
    return lax.linalg.triangular_solve(factor, right_hand, left_side=True, lower=True)


def shards(block, cell_nodes, send_lists, cell_matrix, cell_scale, potential):
    lists = send_lists[0]
    own, slots = block.shape[1], lists.shape[1]
    full = own + 2 * slots
    states_here = block.shape[0]
    states = 2 * states_here
    band = lax.axis_index("band").astype(jnp.int32).reshape(1)
    potential = potential.reshape(1, own)

    to_left, to_right = send_first(block, lists)
    from_left = shift(to_right, "dom", 1)
    from_right = shift(to_left, "dom", -1)
    mine = build(band, cell_nodes, cell_matrix, cell_scale, full)
    other = lax.ppermute(mine, "band", [(0, 1), (1, 0)])
    first = band[0] == 0
    w = jnp.concatenate([jnp.where(first, mine, other), jnp.where(first, other, mine)], axis=0)
    x_here = jnp.concatenate([block, from_left[:states_here], from_right[:states_here]], axis=1)
    x0 = lax.all_gather(x_here, "band", axis=0, tiled=True)

    shapes = apply_shapes(states, own, slots)
    x_shape = jax.ShapeDtypeStruct((states, full), BF16)
    fixed = (band, w, potential, lists, from_left, from_right)
    partial, ghost, near, far = stage_call(first_body, (band, x0, w, potential, lists), shapes, "apply_one")
    got = exchange(near, far)
    x1, partial, ghost, near, far = stage_call(
        lambda *r: next_body(False, *r), fixed + (partial, ghost, got), (x_shape,) + shapes, "apply_two"
    )
    got = exchange(near, far)
    x2, partial, ghost, near, far = stage_call(
        lambda *r: next_body(True, *r), fixed + (partial, ghost, got, x0), (x_shape,) + shapes, "apply_three"
    )
    got = exchange(near, far)
    own_part, sums = stage_call(
        last_body,
        fixed + (partial, ghost, got, x1),
        (jax.ShapeDtypeStruct((states, own // 2), BF16), jax.ShapeDtypeStruct((states, 2 * states), F32)),
        "apply_four",
        (pltpu.VMEM((states, full), BF16), pltpu.VMEM((1, own), F32)),
    )
    total = sum_everywhere(sums) / (own * lax.axis_size("dom"))
    gram, hamiltonian = total[:, :states], total[:, states:]
    factor = jnp.linalg.cholesky(gram)
    ortho_block = lower_solve(factor, own_part.astype(F32))
    half_solved = lower_solve(factor, hamiltonian)
    projected = lower_solve(factor, half_solved.T).T
    return (ortho_block, projected)


def solution(mesh):
    return jax.shard_map(
        shards,
        mesh=mesh,
        in_specs=(P("band", "dom"), P("dom", None), P("dom", None, None), P(), P("dom"), P("dom")),
        out_specs=(P(None, ("dom", "band")), P()),
        check_vma=False,
    )
```

time: 739 us -> 196 us (0.27)
  the two profiles are of different devices: /device:TPU:6 before, /device:TPU:1 now
where the time goes in v1:
time: 196 us; the launch traced here: 194 us
  blocking collectives  87.8 us (45%)
  starting transfers between devices  33.2 us (17%)
  Pallas kernels  29.2 us (15%)
  other arithmetic  25.2 us (13%)
  waiting for transfers between devices  13.1 us (7%)
  local copies, waits for them, and re-layouts  3.36 us (2%)
    all_to_all x4, blocking collectives, swap_pieces(): return lax.all_to_all(x, BOTH, 0, 0, axis_index_groups=groups, tiled=True)  78.7 us
    ppermute x6, starting transfers between devices, across(): return lax.ppermute(x, BOTH, pairs)  21.8 us
    pallas_call x1, Pallas kernels, build(): pl.pallas_call(build_body, out_shape=jax.ShapeDtypeStruct((half, full), B...  21.7 us
    another operation x3, other arithmetic, shards(): factor = jnp.linalg.cholesky(gram)  12.4 us
    another operation x2, other arithmetic, lower_solve(): lax.linalg.triangular_solve(factor, right_hand, left_side=True, lower=True)  10.5 us
    ppermute x6, waiting for transfers between devices, across(): return lax.ppermute(x, BOTH, pairs)  9.49 us
    ppermute x1, starting transfers between devices, shards(): other = lax.ppermute(mine, 'band', [(0, 1), (1, 0)])  8.78 us
    all_gather x3, blocking collectives, exchange(): return lax.all_gather(got, 'band', axis=0, tiled=True)  6.26 us
  transfers between devices with their start and end apart: 9, of which 5 were waited for; matrix products, arithmetic and copies ran while one was open for 0% of the time, Pallas kernels for 1%

profile of v1, /device:TPU:1, one launch (start us, length us, event | category | flops | bytes accessed | tf_op | source)
XLA Modules:
  0.0 194.4 jit_solution(10554732938792831096)
XLA Ops:
  0.6 0.0 copy-start.2
  0.6 0.7 copy-done.2
  1.4 0.0 copy-start.3
  1.4 0.7 copy-done.3
  2.1 0.0 copy-start.4
  2.1 0.7 copy-done.4
  2.8 0.0 copy-start.5
  2.8 21.7 %build.1 = bf16[768,1536]{1,0:T(8,128)(2,1)S(1)} custom-call(s32[1]{0:T(128)} %bitcast.band_ref.r_0_, s32[32,125]{1,0:T(8,128)S(1)} %copy-done.3, bf16[125,125]{1,0:T(8,128)(2,1)S(1)} %copy-done.2, f32[32]{0:T(128)S(1)} %copy-done.4), custom_call_target="tpu_custom_call" | custom-call | flops 9663676416 | bytes 2359296 | tf_op jit(solution)/shard_map/build/pallas_call | solution.py:95
  24.5 8.8 %collective-permute-start = (bf16[768,1536]{1,0:T(8,128)(2,1)S(1)}, bf16[768,1536]{1,0:T(8,128)(2,1)}, u32[]{:S(2)}, u32[]{:S(2)}) collective-permute-start(bf16[768,1536]{1,0:T(8,128)(2,1)S(1)} %build.1), channel_id=1, source_target_pairs={{0,1},{1,0},{2,3},{3,2},{4,5},{5,4},{6,7},{7,6},{8,9},{9,8},{10,11... | collective-permute-start | bytes 7077896 | tf_op jit(solution)/shard_map/ppermute | solution.py:305
  33.3 1.8 send_first.1
  35.1 1.3 collective-permute-start.1
  36.4 1.3 collective-permute-start.2
  37.7 0.2 collective-permute-done.1.r_4_.fl_ref
  37.9 3.5 %collective-permute-done.2.r_5_.fr_ref = bf16[80,256]{1,0:T(8,128)(2,1)S(1)} collective-permute-done((bf16[80,256]{1,0:T(8,128)(2,1)}, bf16[80,256]{1,0:T(8,128)(2,1)S(1)}, u32[]{:S(2)}, u32[]{:S(2)}) %collective-permute-start.2) | collective-permute-done | bytes 40992 | tf_op jit(solution)/shard_map/ppermute | solution.py:245
  41.4 0.0 copy-done.5
  41.4 2.9 %all_gather.12.x_ref.r_9_ = bf16[128,1536]{1,0:T(8,128)(2,1)S(1)} all-gather(bf16[64,1536]{1,0:T(8,128)(2,1)S(1)} %pad_maximum_fusion.1), channel_id=1, replica_groups=mesh['dom'=256,'band'=2] {'band'}, dimensions={0}, use_global_device_ids=true | all-gather | bytes 589824 | tf_op jit(solution)/shard_map/all_gather | solution.py:309
  44.3 0.0 collective-permute-done
  44.3 2.0 %broadcast_select_fusion.1 = (bf16[768,1536]{1,0:T(8,128)(2,1)S(1)}, bf16[768,1536]{1,0:T(8,128)(2,1)S(1)}) fusion(bf16[768,1536]{1,0:T(8,128)(2,1)S(1)} %build.1, bf16[768,1536]{1,0:T(8,128)(2,1)} %collective-permute-done, pred[]{:T(512)S(6)} %eq.3), kind=kLoop, calls=%fused_computation.2 | loop fusion | flops 2359296 | bytes 9437185 | tf_op jit(solution)/shard_map/jit(_where)/select_n | solution.py:307
  46.3 0.0 copy-start
  46.3 0.0 copy-start.1
  46.3 0.3 pad_maximum_fusion.w_ref.r_1_
  46.6 0.4 copy-done
  47.0 0.0 copy-done.1
  47.0 0.9 apply_one.1
  47.9 2.1 %collective-permute-start.3 = (bf16[128,512]{1,0:T(8,128)(2,1)S(1)}, bf16[128,512]{1,0:T(8,128)(2,1)S(1)}, u32[]{:S(2)}, u32[]{:S(2)}) collective-permute-start(bf16[128,512]{1,0:T(8,128)(2,1)S(1)} %get-tuple-element.24), channel_id=1, source_target_pairs={{1,2},{3,4},{5,6},{7,8},{9,10},{11,12},{13,14},{15,16},{17,18},{19... | collective-permute-start | bytes 393224 | tf_op jit(solution)/shard_map/ppermute | solution.py:252
  50.0 3.3 %collective-permute-start.4 = (bf16[128,256]{1,0:T(8,128)(2,1)S(1)}, bf16[128,256]{1,0:T(8,128)(2,1)S(1)}, u32[]{:S(2)}, u32[]{:S(2)}) collective-permute-start(bf16[128,256]{1,0:T(8,128)(2,1)S(1)} %get-tuple-element.25), channel_id=1, source_target_pairs={{1,4},{3,6},{5,8},{7,10},{9,12},{11,14},{13,16},{15,18},{17,20},{1... | collective-permute-start | bytes 196616 | tf_op jit(solution)/shard_map/ppermute | solution.py:252
  53.3 3.8 %collective-permute-done.4 = bf16[128,256]{1,0:T(8,128)(2,1)S(1)} collective-permute-done((bf16[128,256]{1,0:T(8,128)(2,1)S(1)}, bf16[128,256]{1,0:T(8,128)(2,1)S(1)}, u32[]{:S(2)}, u32[]{:S(2)}) %collective-permute-start.4) | collective-permute-done | bytes 65568 | tf_op jit(solution)/shard_map/ppermute | solution.py:252
  57.1 0.0 collective-permute-done.3
  57.1 2.1 %all_gather.13.r_8_ = bf16[256,768]{1,0:T(8,128)(2,1)S(1)} all-gather(bf16[128,768]{1,0:T(8,128)(2,1)S(1)} %pad_maximum_fusion.2), channel_id=1, replica_groups=mesh['dom'=256,'band'=2] {'band'}, dimensions={0}, use_global_device_ids=true | all-gather | bytes 589824 | tf_op jit(solution)/shard_map/all_gather | solution.py:257
  59.2 1.4 apply_two.1
  60.6 1.9 collective-permute-start.5
  62.5 5.7 %collective-permute-start.6 = (bf16[128,256]{1,0:T(8,128)(2,1)S(1)}, bf16[128,256]{1,0:T(8,128)(2,1)S(1)}, u32[]{:S(2)}, u32[]{:S(2)}) collective-permute-start(bf16[128,256]{1,0:T(8,128)(2,1)S(1)} %get-tuple-element.29), channel_id=1, source_target_pairs={{1,4},{3,6},{5,8},{7,10},{9,12},{11,14},{13,16},{15,18},{17,20},{1... | collective-permute-start | bytes 196616 | tf_op jit(solution)/shard_map/ppermute | solution.py:252
  68.3 1.9 collective-permute-done.6
  70.2 0.0 collective-permute-done.5
  70.2 2.1 %all_gather.14.r_8_ = bf16[256,768]{1,0:T(8,128)(2,1)S(1)} all-gather(bf16[128,768]{1,0:T(8,128)(2,1)S(1)} %pad_maximum_fusion.3), channel_id=1, replica_groups=mesh['dom'=256,'band'=2] {'band'}, dimensions={0}, use_global_device_ids=true | all-gather | bytes 589824 | tf_op jit(solution)/shard_map/all_gather | solution.py:257
  72.3 2.0 %apply_three.1 = (bf16[128,1536]{1,0:T(8,128)(2,1)}, f32[128,1024]{1,0:T(8,128)S(1)}, bf16[128,512]{1,0:T(8,128)(2,1)S(1)}, bf16[128,512]{1,0:T(8,128)(2,1)S(1)}, bf16[128,256]{1,0:T(8,128)(2,1)S(1)}) custom-call(s32[1]{0:T(128)} %bitcast.band_ref.r_0_, bf16[1536,1536]{1,0:T(8,128)(2,1)S(1)} %pad_maximum_fusion.w_ref.r_1_, f32[1,1024]{1,0:T(1,128)S(1)} %bitcast.31, ...), custom_call_target="tpu_custom_call" | custom-call | tf_op jit(solution)/shard_map/apply_three/pallas_call | solution.py:232
  74.3 4.8 %collective-permute-start.7 = (bf16[128,512]{1,0:T(8,128)(2,1)S(1)}, bf16[128,512]{1,0:T(8,128)(2,1)S(1)}, u32[]{:S(2)}, u32[]{:S(2)}) collective-permute-start(bf16[128,512]{1,0:T(8,128)(2,1)S(1)} %get-tuple-element.32), channel_id=1, source_target_pairs={{1,2},{3,4},{5,6},{7,8},{9,10},{11,12},{13,14},{15,16},{17,18},{19... | collective-permute-start | bytes 393224 | tf_op jit(solution)/shard_map/ppermute | solution.py:252
  79.1 4.0 %collective-permute-start.8 = (bf16[128,256]{1,0:T(8,128)(2,1)S(1)}, bf16[128,256]{1,0:T(8,128)(2,1)S(1)}, u32[]{:S(2)}, u32[]{:S(2)}) collective-permute-start(bf16[128,256]{1,0:T(8,128)(2,1)S(1)} %get-tuple-element.33), channel_id=1, source_target_pairs={{1,4},{3,6},{5,8},{7,10},{9,12},{11,14},{13,16},{15,18},{17,20},{1... | collective-permute-start | bytes 196616 | tf_op jit(solution)/shard_map/ppermute | solution.py:252
  83.1 3.8 %collective-permute-done.8 = bf16[128,256]{1,0:T(8,128)(2,1)S(1)} collective-permute-done((bf16[128,256]{1,0:T(8,128)(2,1)S(1)}, bf16[128,256]{1,0:T(8,128)(2,1)S(1)}, u32[]{:S(2)}, u32[]{:S(2)}) %collective-permute-start.8) | collective-permute-done | bytes 65568 | tf_op jit(solution)/shard_map/ppermute | solution.py:252
  86.9 0.0 collective-permute-done.7
  86.9 2.1 %all_gather.15.got_ref = bf16[256,768]{1,0:T(8,128)(2,1)S(1)} all-gather(bf16[128,768]{1,0:T(8,128)(2,1)S(1)} %pad_maximum_fusion.4), channel_id=1, replica_groups=mesh['dom'=256,'band'=2] {'band'}, dimensions={0}, use_global_device_ids=true | all-gather | bytes 589824 | tf_op jit(solution)/shard_map/all_gather | solution.py:257
  89.0 1.3 apply_four.1
  90.3 11.8 %all_to_all.27 = f32[8,16,256]{2,1,0:T(8,128)S(1)} all-to-all(f32[8,16,256]{2,1,0:T(8,128)S(1)} %bitcast.28), channel_id=1, replica_groups={{0,1,2,3,4,5,6,7},{8,9,10,11,12,13,14,15},{16,17,18,19,20,21,22,23},{24..., dimensions={0} | all-to-all | bytes 262144 | tf_op jit(solution)/shard_map/all_to_all | solution.py:274
  102.2 29.6 %all_to_all.28 = f32[8,16,256]{2,1,0:T(8,128)S(1)} all-to-all(f32[8,16,256]{2,1,0:T(8,128)S(1)} %broadcast_in_dim.7), channel_id=1, replica_groups={{0,8,16,24,32,40,48,56},{1,9,17,25,33,41,49,57},{2,10,18,26,34,42,50,58..., dimensions={0} | all-to-all | bytes 262144 | tf_op jit(solution)/shard_map/all_to_all | solution.py:274
  131.8 25.6 %all_to_all.29 = f32[8,16,256]{2,1,0:T(8,128)S(1)} all-to-all(f32[8,16,256]{2,1,0:T(8,128)S(1)} %broadcast_in_dim.8), channel_id=1, replica_groups={{0,64,128,192,256,320,384,448},{1,65,129,193,257,321,385,449},{2,66,130..., dimensions={0} | all-to-all | bytes 262144 | tf_op jit(solution)/shard_map/all_to_all | solution.py:274
  157.4 11.7 %all_to_all.30 = f32[8,16,256]{2,1,0:T(8,128)S(1)} all-to-all(f32[8,16,256]{2,1,0:T(8,128)S(1)} %broadcast_in_dim.9), channel_id=1, replica_groups={{0,1,2,3,4,5,6,7},{8,9,10,11,12,13,14,15},{16,17,18,19,20,21,22,23},{24..., dimensions={0} | all-to-all | bytes 262144 | tf_op jit(solution)/shard_map/all_to_all | solution.py:274
  169.1 0.1 copy.16
  169.2 11.7 %cholesky.16 = f32[128,128]{1,0:T(8,128)S(1)} custom-call(f32[128,128]{1,0:T(8,128)S(1)} %fusion.6), custom_call_target="Cholesky" | custom-call | tf_op jit(solution)/shard_map/jit(cholesky)/cholesky | solution.py:333
  181.0 0.6 compare_reduce_fusion
  181.6 0.7 fusion
  182.3 9.8 %custom-call.9 = f32[1,128,128]{1,2,0:T(8,128)S(1)} custom-call(f32[1,128,128]{2,1,0:T(8,128)S(1)} %fusion), custom_call_target="InvertDiagBlocksLowerTriangular" | custom-call | tf_op jit(solution)/shard_map/triangular_solve | solution.py:289
  192.1 0.3 convolution_bitcast_fusion.1
  192.4 0.3 convolution_bitcast_fusion
  192.7 0.7 copy.15
  193.4 1.0 fusion.4
  (16 shorter events, 0.2 us)
Async XLA Ops:
  0.6 0.8 copy-start.2
  1.4 0.7 copy-start.3
  2.1 0.7 copy-start.4
  2.8 38.6 %copy-start.5 = (bf16[64,1024]{1,0:T(8,128)(2,1)S(1)}, bf16[64,1024]{1,0:T(8,128)(2,1)}, u32[]{:S(2)}) copy-start(bf16[64,1024]{1,0:T(8,128)(2,1)} %block_ref.1) | copy-start | bytes 393220
  24.5 19.8 %collective-permute-start = (bf16[768,1536]{1,0:T(8,128)(2,1)S(1)}, bf16[768,1536]{1,0:T(8,128)(2,1)}, u32[]{:S(2)}, u32[]{:S(2)}) collective-permute-start(bf16[768,1536]{1,0:T(8,128)(2,1)S(1)} %build.1), channel_id=1, source_target_pairs={{0,1},{1,0},{2,3},{3,2},{4,5},{5,4},{6,7},{7,6},{8,9},{9,8},{10,11... | collective-permute-start | bytes 7077896 | tf_op jit(solution)/shard_map/ppermute | solution.py:305
  35.1 2.8 %collective-permute-start.1 = (bf16[80,256]{1,0:T(8,128)(2,1)}, bf16[80,256]{1,0:T(8,128)(2,1)S(1)}, u32[]{:S(2)}, u32[]{:S(2)}) collective-permute-start(bf16[80,256]{1,0:T(8,128)(2,1)} %get-tuple-element.20), channel_id=1, source_target_pairs={{0,2},{2,4},{4,6},{6,8},{8,10},{10,12},{12,14},{14,16},{16,18},{18... | collective-permute-start | bytes 122888 | tf_op jit(solution)/shard_map/ppermute | solution.py:245
  36.4 5.0 %collective-permute-start.2 = (bf16[80,256]{1,0:T(8,128)(2,1)}, bf16[80,256]{1,0:T(8,128)(2,1)S(1)}, u32[]{:S(2)}, u32[]{:S(2)}) collective-permute-start(bf16[80,256]{1,0:T(8,128)(2,1)} %get-tuple-element.21), channel_id=1, source_target_pairs={{2,0},{4,2},{6,4},{8,6},{10,8},{12,10},{14,12},{16,14},{18,16},{20... | collective-permute-start | bytes 122888 | tf_op jit(solution)/shard_map/ppermute | solution.py:245
  46.3 0.7 copy-start
  46.3 0.7 copy-start.1
  47.9 9.2 %collective-permute-start.3 = (bf16[128,512]{1,0:T(8,128)(2,1)S(1)}, bf16[128,512]{1,0:T(8,128)(2,1)S(1)}, u32[]{:S(2)}, u32[]{:S(2)}) collective-permute-start(bf16[128,512]{1,0:T(8,128)(2,1)S(1)} %get-tuple-element.24), channel_id=1, source_target_pairs={{1,2},{3,4},{5,6},{7,8},{9,10},{11,12},{13,14},{15,16},{17,18},{19... | collective-permute-start | bytes 393224 | tf_op jit(solution)/shard_map/ppermute | solution.py:252
  50.0 7.1 %collective-permute-start.4 = (bf16[128,256]{1,0:T(8,128)(2,1)S(1)}, bf16[128,256]{1,0:T(8,128)(2,1)S(1)}, u32[]{:S(2)}, u32[]{:S(2)}) collective-permute-start(bf16[128,256]{1,0:T(8,128)(2,1)S(1)} %get-tuple-element.25), channel_id=1, source_target_pairs={{1,4},{3,6},{5,8},{7,10},{9,12},{11,14},{13,16},{15,18},{17,20},{1... | collective-permute-start | bytes 196616 | tf_op jit(solution)/shard_map/ppermute | solution.py:252
  60.6 9.6 %collective-permute-start.5 = (bf16[128,512]{1,0:T(8,128)(2,1)S(1)}, bf16[128,512]{1,0:T(8,128)(2,1)S(1)}, u32[]{:S(2)}, u32[]{:S(2)}) collective-permute-start(bf16[128,512]{1,0:T(8,128)(2,1)S(1)} %get-tuple-element.28), channel_id=1, source_target_pairs={{1,2},{3,4},{5,6},{7,8},{9,10},{11,12},{13,14},{15,16},{17,18},{19... | collective-permute-start | bytes 393224 | tf_op jit(solution)/shard_map/ppermute | solution.py:252
  62.5 7.7 %collective-permute-start.6 = (bf16[128,256]{1,0:T(8,128)(2,1)S(1)}, bf16[128,256]{1,0:T(8,128)(2,1)S(1)}, u32[]{:S(2)}, u32[]{:S(2)}) collective-permute-start(bf16[128,256]{1,0:T(8,128)(2,1)S(1)} %get-tuple-element.29), channel_id=1, source_target_pairs={{1,4},{3,6},{5,8},{7,10},{9,12},{11,14},{13,16},{15,18},{17,20},{1... | collective-permute-start | bytes 196616 | tf_op jit(solution)/shard_map/ppermute | solution.py:252
  74.3 12.6 %collective-permute-start.7 = (bf16[128,512]{1,0:T(8,128)(2,1)S(1)}, bf16[128,512]{1,0:T(8,128)(2,1)S(1)}, u32[]{:S(2)}, u32[]{:S(2)}) collective-permute-start(bf16[128,512]{1,0:T(8,128)(2,1)S(1)} %get-tuple-element.32), channel_id=1, source_target_pairs={{1,2},{3,4},{5,6},{7,8},{9,10},{11,12},{13,14},{15,16},{17,18},{19... | collective-permute-start | bytes 393224 | tf_op jit(solution)/shard_map/ppermute | solution.py:252
  79.1 7.7 %collective-permute-start.8 = (bf16[128,256]{1,0:T(8,128)(2,1)S(1)}, bf16[128,256]{1,0:T(8,128)(2,1)S(1)}, u32[]{:S(2)}, u32[]{:S(2)}) collective-permute-start(bf16[128,256]{1,0:T(8,128)(2,1)S(1)} %get-tuple-element.33), channel_id=1, source_target_pairs={{1,4},{3,6},{5,8},{7,10},{9,12},{11,14},{13,16},{15,18},{17,20},{1... | collective-permute-start | bytes 196616 | tf_op jit(solution)/shard_map/ppermute | solution.py:252

commit v2 on v1

--- a/solution.py
+++ b/solution.py
@@ -147,11 +147,20 @@
     return whole_own, whole_left, whole_right
 
 
-def apply_body(band_ref, x, w_ref, potential_ref, lists, partial_out, ghost_out, near_out, far_out):
+def times_operator(band, x_ref, mine_ref, other_ref, cols):
+    half = mine_ref.shape[0]
+    here = pl.ds(pl.multiple_of(band * half, 128), half)
+    there = pl.ds(pl.multiple_of((1 - band) * half, 128), half)
+    return nn(x_ref[:, here], mine_ref[:, cols]) + nn(x_ref[:, there], other_ref[:, cols])
+
+
+def apply_body(
+    band_ref, x_ref, mine_ref, other_ref, potential_ref, lists, partial_out, ghost_out, near_out, far_out
+):
     own = partial_out.shape[1]
     slots = lists.shape[1]
-    result = nn(x, w_ref[...])
-    partial = result[:, 0:own] + potential_ref[...] * x[:, 0:own].astype(F32)
+    result = times_operator(band_ref[0], x_ref, mine_ref, other_ref, slice(None))
+    partial = result[:, 0:own] + potential_ref[...] * x_ref[:, 0:own].astype(F32)
     partial_out[...] = partial
     ghost = result[:, own:].astype(BF16)
     ghost_out[...] = ghost
@@ -163,10 +172,8 @@
     far_out[...] = edge
 
 
-def first_body(band_ref, x_ref, w_ref, potential_ref, lists_ref, partial_out, ghost_out, near_out, far_out):
-    apply_body(
-        band_ref, x_ref[...], w_ref, potential_ref, lists_ref[...], partial_out, ghost_out, near_out, far_out
-    )
+def first_body(band_ref, mine_ref, other_ref, potential_ref, lists_ref, x_ref, *outs):
+    apply_body(band_ref, x_ref, mine_ref, other_ref, potential_ref, lists_ref[...], *outs)
 
 
 def new_states(older_ref, x_out, pieces):
@@ -182,24 +189,18 @@
 
 
 def next_body(chebyshev, *refs):
-    if chebyshev:
-        band_ref, w_ref, potential_ref, lists_ref, fl_ref, fr_ref, partial_ref, ghost_ref, got_ref, older_ref = refs[:10]
-        refs = refs[10:]
-    else:
-        band_ref, w_ref, potential_ref, lists_ref, fl_ref, fr_ref, partial_ref, ghost_ref, got_ref = refs[:9]
-        older_ref, refs = None, refs[9:]
-    x_out, partial_out, ghost_out, near_out, far_out = refs
+    band_ref, mine_ref, other_ref, potential_ref, lists_ref, fl_ref, fr_ref, partial_ref, ghost_ref, got_ref = refs[:10]
+    older_ref = refs[10] if chebyshev else None
+    x_out, *outs = refs[11:] if chebyshev else refs[10:]
     lists = lists_ref[...]
     own = partial_ref.shape[1]
     new_states(older_ref, x_out, assemble(partial_ref, ghost_ref, got_ref, lists, fl_ref, fr_ref, own))
-    apply_body(
-        band_ref, x_out[...], w_ref, potential_ref, lists, partial_out, ghost_out, near_out, far_out
-    )
+    apply_body(band_ref, x_out, mine_ref, other_ref, potential_ref, lists, *outs)
 
 
 def last_body(
-    band_ref, w_ref, potential_ref, lists_ref, fl_ref, fr_ref, partial_ref, ghost_ref, got_ref, older_ref,
-    own_out, sums_out, x_all, pot,
+    band_ref, mine_ref, other_ref, potential_ref, lists_ref, fl_ref, fr_ref, partial_ref, ghost_ref, got_ref,
+    older_ref, own_out, sums_out, x_all, pot,
 ):
     lists = lists_ref[...]
     own = partial_ref.shape[1]
@@ -210,13 +211,12 @@
     half = own // 2
     mine = pl.ds(pl.multiple_of(band_ref[0] * half, 128), half)
     edge = pl.ds(pl.multiple_of(own + band_ref[0] * slots, 128), slots)
-    x = x_all[...]
     x_mine = x_all[:, mine]
     own_out[...] = x_mine
-    sums_out[:, 0:states] = nt(x_mine, x_mine)
-    image = (nn(x, w_ref[:, mine]) + pot[:, mine] * x_mine.astype(F32)).astype(BF16)
-    image_edge = nn(x, w_ref[:, edge]).astype(BF16)
-    sums_out[:, states : 2 * states] = nt(x_mine, image) + nt(x_all[:, edge], image_edge)
+    sums_out[0:states, :] = nt(x_mine, x_mine)
+    image = times_operator(band_ref[0], x_all, mine_ref, other_ref, mine) + pot[:, mine] * x_mine.astype(F32)
+    image_edge = times_operator(band_ref[0], x_all, mine_ref, other_ref, edge)
+    sums_out[states : 2 * states, :] = nt(x_mine, image.astype(BF16)) + nt(x_all[:, edge], image_edge.astype(BF16))
 
 
 def apply_shapes(states, own, slots):
@@ -258,35 +258,122 @@
 
 
 def group_lists():
-    eights, along_z, along_x = {}, {}, {}
+    planes, along_z = {}, {}
     for x in range(4):
         for z in range(16):
             for y in range(4):
                 for b in range(2):
                     i = ((x * 16 + z) * 4 + y) * 2 + b
-                    eights.setdefault((x, z), []).append(i)
-                    along_z.setdefault((x, z // 8, y, b), []).append(i)
-                    along_x.setdefault((z % 8, y, b), []).append(i)
-    return [list(g.values()) for g in (eights, along_z, along_x)]
+                    planes.setdefault(z, []).append(i)
+                    along_z.setdefault((x, y, b), []).append(i)
+    return list(planes.values()), list(along_z.values())
 
 
 def swap_pieces(x, groups):
     return lax.all_to_all(x, BOTH, 0, 0, axis_index_groups=groups, tiled=True)
 
 
+def copies(piece, count):
+    return jnp.broadcast_to(piece[None], (count,) + piece.shape).reshape(count * piece.shape[0], piece.shape[1])
+
+
+def sum_pieces(x, count):
+    return x.reshape(count, x.shape[0] // count, x.shape[1]).sum(0)
+
+
 def sum_everywhere(x):
-    rows, cols = x.shape
-    eights, along_z, along_x = group_lists()
-    piece = swap_pieces(x, eights).reshape(8, rows // 8, cols).sum(0)
-    for groups in (along_z, along_x):
-        copies = jnp.broadcast_to(piece[None], (8,) + piece.shape).reshape(rows, cols)
-        piece = swap_pieces(copies, groups).reshape(8, rows // 8, cols).sum(0)
-    copies = jnp.broadcast_to(piece[None], (8,) + piece.shape).reshape(rows, cols)
-    return swap_pieces(copies, eights)
-
-
-def lower_solve(factor, right_hand):
-    return lax.linalg.triangular_solve(factor, right_hand, left_side=True, lower=True)
+    planes, along_z = group_lists()
+    in_plane, depth = len(planes[0]), len(along_z[0])
+    piece = sum_pieces(swap_pieces(x, planes), in_plane)
+    piece = sum_pieces(swap_pieces(copies(piece, depth), along_z), depth)
+    return swap_pieces(copies(piece, in_plane), planes)
+
+
+def exact(a, b):
+    return jnp.dot(a, b, precision=lax.Precision.HIGHEST, preferred_element_type=F32)
+
+
+def weighted(weights, rows):
+    total = None
+    for w, r in zip(weights, rows):
+        total = w * r if total is None else total + w * r
+    return total
+
+
+def stack(rows):
+    part = lax.broadcasted_iota(jnp.int32, rows[0].shape, 0)
+    out = rows[0]
+    for i in range(1, len(rows)):
+        out = jnp.where(part == i, rows[i], out)
+    return out
+
+
+def inverse_of_eight(panel, first):
+    wide = panel.shape
+    columns = [jnp.broadcast_to(panel[:, first + j : first + j + 1], wide) for j in range(8)]
+    low = {(i, j): jnp.broadcast_to(columns[j][i : i + 1, :], wide) for j in range(8) for i in range(j, 8)}
+    inv = {}
+    for j in range(8):
+        inv[j, j] = lax.rsqrt(low[j, j])
+        for i in range(j + 1, 8):
+            low[i, j] = low[i, j] * inv[j, j]
+        for k in range(j + 1, 8):
+            for i in range(k, 8):
+                low[i, k] = low[i, k] - low[i, j] * low[k, j]
+        for k in range(j):
+            inv[j, k] = -inv[j, j] * weighted([low[j, m] for m in range(k, j)], [inv[m, k] for m in range(k, j)])
+    return inv
+
+
+def finish_body(scale, total_ref, own_ref, ortho_out, projected_out, inverse_ref):
+    size = total_ref.shape[1]
+    schur = total_ref[0:size, :] * scale
+    at = lax.broadcasted_iota(jnp.int32, (size, size), 0)
+    beside = (at == lax.broadcasted_iota(jnp.int32, (size, size), 1)).astype(F32)
+    for first in range(0, size, 8):
+        top, top_beside = schur[0:8], beside[0:8]
+        inv = inverse_of_eight(top, first)
+        rows = [jnp.broadcast_to(top[i : i + 1], top.shape) for i in range(8)]
+        rows_beside = [jnp.broadcast_to(top_beside[i : i + 1], top.shape) for i in range(8)]
+        solved = [weighted([inv[i, k] for k in range(i + 1)], rows) for i in range(8)]
+        solved_beside = [weighted([inv[i, k] for k in range(i + 1)], rows_beside) for i in range(8)]
+        inverse_ref[first : first + 8, :] = stack(solved_beside)
+        if first + 8 == size:
+            break
+        twice = stack([weighted([inv[k, i] for k in range(i, 8)], solved[i:]) for i in range(8)])
+        twice_beside = stack([weighted([inv[k, i] for k in range(i, 8)], solved_beside[i:]) for i in range(8)])
+        both = jnp.concatenate([twice, twice_beside], axis=1)
+        pieces = [both]
+        if first:
+            pieces = [jnp.zeros((first, 2 * size), F32)] + pieces
+        pieces.append(jnp.zeros((size - first - 8, 2 * size), F32))
+        taken = exact(schur[8:], jnp.concatenate(pieces, axis=0))
+        schur = schur[8:] - taken[:, 0:size]
+        beside = beside[8:] - taken[:, size:]
+    inverse = inverse_ref[...]
+    coarse = inverse.astype(BF16)
+    rest = inverse - coarse.astype(F32)
+    fine = rest.astype(BF16)
+    finest = (rest - fine.astype(F32)).astype(BF16)
+    own = own_ref[...]
+    ortho_out[...] = nn(coarse, own) + (nn(fine, own) + nn(finest, own))
+    half_solved = exact(inverse, total_ref[size : 2 * size, :] * scale)
+    projected_out[...] = lax.dot_general(
+        half_solved, inverse, (((1,), (1,)), ((), ())), precision=lax.Precision.HIGHEST, preferred_element_type=F32
+    )
+
+
+def finish(scale, total, own_part):
+    states, nodes = own_part.shape
+    return pl.pallas_call(
+        lambda *refs: finish_body(scale, *refs),
+        out_shape=(jax.ShapeDtypeStruct((states, nodes), F32), jax.ShapeDtypeStruct((states, states), F32)),
+        in_specs=[spec()] * 2,
+        out_specs=(spec(), spec()),
+        scratch_shapes=[pltpu.VMEM((states, states), F32)],
+        compiler_params=pltpu.CompilerParams(vmem_limit_bytes=32 * MIB),
+        name="finish",
+    )(total, own_part)
 
 
 def shards(block, cell_nodes, send_lists, cell_matrix, cell_scale, potential):
@@ -299,42 +386,36 @@
     potential = potential.reshape(1, own)
 
     to_left, to_right = send_first(block, lists)
+    to_left, to_right, cell_nodes = lax.optimization_barrier((to_left, to_right, cell_nodes))
     from_left = shift(to_right, "dom", 1)
     from_right = shift(to_left, "dom", -1)
     mine = build(band, cell_nodes, cell_matrix, cell_scale, full)
     other = lax.ppermute(mine, "band", [(0, 1), (1, 0)])
-    first = band[0] == 0
-    w = jnp.concatenate([jnp.where(first, mine, other), jnp.where(first, other, mine)], axis=0)
     x_here = jnp.concatenate([block, from_left[:states_here], from_right[:states_here]], axis=1)
     x0 = lax.all_gather(x_here, "band", axis=0, tiled=True)
 
     shapes = apply_shapes(states, own, slots)
     x_shape = jax.ShapeDtypeStruct((states, full), BF16)
-    fixed = (band, w, potential, lists, from_left, from_right)
-    partial, ghost, near, far = stage_call(first_body, (band, x0, w, potential, lists), shapes, "apply_one")
+    fixed = (band, mine, other, potential, lists)
+    ends = fixed + (from_left, from_right)
+    partial, ghost, near, far = stage_call(first_body, fixed + (x0,), shapes, "apply_one")
     got = exchange(near, far)
     x1, partial, ghost, near, far = stage_call(
-        lambda *r: next_body(False, *r), fixed + (partial, ghost, got), (x_shape,) + shapes, "apply_two"
+        lambda *r: next_body(False, *r), ends + (partial, ghost, got), (x_shape,) + shapes, "apply_two"
     )
     got = exchange(near, far)
     x2, partial, ghost, near, far = stage_call(
-        lambda *r: next_body(True, *r), fixed + (partial, ghost, got, x0), (x_shape,) + shapes, "apply_three"
+        lambda *r: next_body(True, *r), ends + (partial, ghost, got, x0), (x_shape,) + shapes, "apply_three"
     )
     got = exchange(near, far)
     own_part, sums = stage_call(
         last_body,
-        fixed + (partial, ghost, got, x1),
-        (jax.ShapeDtypeStruct((states, own // 2), BF16), jax.ShapeDtypeStruct((states, 2 * states), F32)),
+        ends + (partial, ghost, got, x1),
+        (jax.ShapeDtypeStruct((states, own // 2), BF16), jax.ShapeDtypeStruct((2 * states, states), F32)),
         "apply_four",
         (pltpu.VMEM((states, full), BF16), pltpu.VMEM((1, own), F32)),
     )
-    total = sum_everywhere(sums) / (own * lax.axis_size("dom"))
-    gram, hamiltonian = total[:, :states], total[:, states:]
-    factor = jnp.linalg.cholesky(gram)
-    ortho_block = lower_solve(factor, own_part.astype(F32))
-    half_solved = lower_solve(factor, hamiltonian)
-    projected = lower_solve(factor, half_solved.T).T
-    return (ortho_block, projected)
+    return finish(1.0 / (own * lax.axis_size("dom")), sum_everywhere(sums), own_part)
 
 
 def solution(mesh):

time: 196 us -> 159 us (0.81)
  other arithmetic: 25.2 us -> 0.11 us
  blocking collectives: 87.8 us -> 71.5 us
  Pallas kernels: 29.2 us -> 37.3 us
    another operation x5 -> x0, other arithmetic: 22.9 us -> none  [the longest x3 12.4 us: shards(): factor = jnp.linalg.cholesky(gram)]
    all_to_all x4 -> x3, blocking collectives: 78.7 us -> 62.2 us  [swap_pieces(): return lax.all_to_all(x, BOTH, 0, 0, axis_index_groups=groups, tiled=True)]
    pallas_call x0 -> x1, Pallas kernels: none -> 7.6 us  [finish(): pl.pallas_call(lambda *refs: finish_body(scale, *refs), out_shape=(jax.Sh...]
    select_n x1 -> x0, other arithmetic: 1.97 us -> none  [shards(): jnp.where(first, mine, other)]
  transfers between devices with their start and end apart: 9 -> 9, of which waited for: 5 -> 4; matrix products, arithmetic and copies ran while one was open for 0% -> 0% of each run, Pallas kernels for 1% -> 0%
where the time goes in v2:
time: 159 us; the launch traced here: 158 us
  blocking collectives  71.5 us (45%)
  Pallas kernels  37.3 us (23%)
  starting transfers between devices  33.3 us (21%)
  waiting for transfers between devices  12.8 us (8%)
  local copies, waits for them, and re-layouts  2.18 us (1%)
    all_to_all x3, blocking collectives, swap_pieces(): return lax.all_to_all(x, BOTH, 0, 0, axis_index_groups=groups, tiled=True)  62.2 us
    ppermute x6, starting transfers between devices, across(): return lax.ppermute(x, BOTH, pairs)  21.9 us
    pallas_call x1, Pallas kernels, build(): pl.pallas_call(build_body, out_shape=jax.ShapeDtypeStruct((half, full), B...  21.7 us
    ppermute x6, waiting for transfers between devices, across(): return lax.ppermute(x, BOTH, pairs)  9.41 us
    ppermute x1, starting transfers between devices, shards(): other = lax.ppermute(mine, 'band', [(0, 1), (1, 0)])  8.78 us
    pallas_call x1, Pallas kernels, finish(): pl.pallas_call(lambda *refs: finish_body(scale, *refs), out_shape=(jax.Sh...  7.6 us
    all_gather x3, blocking collectives, exchange(): return lax.all_gather(got, 'band', axis=0, tiled=True)  6.44 us
    pallas_call x4, Pallas kernels, stage_call(): pl.pallas_call(body, out_shape=tuple(shapes), in_specs=[spec(pltpu.SMEM)]...  6.15 us
  transfers between devices with their start and end apart: 9, of which 4 were waited for; matrix products, arithmetic and copies ran while one was open for 0% of the time, Pallas kernels for 0%

profile of v2, /device:TPU:1, one launch (start us, length us, event | category | flops | bytes accessed | tf_op | source)
XLA Modules:
  0.0 158.1 jit_solution(14453659496713767629)
XLA Ops:
  0.6 1.8 %send_first.1 = (bf16[80,256]{1,0:T(8,128)(2,1)}, bf16[80,256]{1,0:T(8,128)(2,1)}) custom-call(bf16[64,1024]{1,0:T(8,128)(2,1)} %block_ref.1, s32[2,256]{1,0:T(2,128)} %bitcast.11), custom_call_target="tpu_custom_call" | custom-call | tf_op jit(solution)/shard_map/send_first/pallas_call | solution.py:56
  2.5 0.0 copy-start.2
  2.5 0.8 copy-done.2
  3.2 0.0 copy-start.3
  3.2 0.7 copy-done.3
  4.0 0.0 copy-start.4
  4.0 0.7 copy-done.4
  4.6 0.0 copy-start.7
  4.6 0.0 copy-start.6
  4.6 0.0 copy-start.5
  4.6 0.0 copy-start
  4.6 0.0 copy-start.1
  4.6 21.7 %build.1.mine_ref.r_1_ = bf16[768,1536]{1,0:T(8,128)(2,1)S(1)} custom-call(s32[1]{0:T(128)} %bitcast.band_ref.r_0_, s32[32,125]{1,0:T(8,128)S(1)} %copy-done.3, bf16[125,125]{1,0:T(8,128)(2,1)S(1)} %copy-done.2, f32[32]{0:T(128)S(1)} %copy-done.4), custom_call_target="tpu_custom_call" | custom-call | flops 9663676416 | bytes 2359296 | tf_op jit(solution)/shard_map/build/pallas_call | solution.py:95
  26.4 8.8 %collective-permute-start = (bf16[768,1536]{1,0:T(8,128)(2,1)S(1)}, bf16[768,1536]{1,0:T(8,128)(2,1)S(1)}, u32[]{:S(2)}, u32[]{:S(2)}) collective-permute-start(bf16[768,1536]{1,0:T(8,128)(2,1)S(1)} %build.1.mine_ref.r_1_), channel_id=1, source_target_pairs={{0,1},{1,0},{2,3},{3,2},{4,5},{5,4},{6,7},{7,6},{8,9},{9,8},{10,11... | collective-permute-start | bytes 7077896 | tf_op jit(solution)/shard_map/ppermute | solution.py:393
  35.2 0.0 copy-done.7
  35.2 1.3 collective-permute-start.1
  36.5 0.0 copy-done.6
  36.5 1.3 collective-permute-start.2
  37.8 0.0 collective-permute-done.1.r_5_.fl_ref
  37.8 3.4 %collective-permute-done.2.r_6_.fr_ref = bf16[80,256]{1,0:T(8,128)(2,1)S(1)} collective-permute-done((bf16[80,256]{1,0:T(8,128)(2,1)S(1)}, bf16[80,256]{1,0:T(8,128)(2,1)S(1)}, u32[]{:S(2)}, u32[]{:S(2)}) %collective-permute-start.2) | collective-permute-done | bytes 40992 | tf_op jit(solution)/shard_map/ppermute | solution.py:245
  41.2 0.0 copy-done.5
  41.3 2.9 %all_gather.12.x_ref.r_10_ = bf16[128,1536]{1,0:T(8,128)(2,1)S(1)} all-gather(bf16[64,1536]{1,0:T(8,128)(2,1)S(1)} %pad_maximum_fusion), channel_id=1, replica_groups=mesh['dom'=256,'band'=2] {'band'}, dimensions={0}, use_global_device_ids=true | all-gather | bytes 589824 | tf_op jit(solution)/shard_map/all_gather | solution.py:395
  44.1 0.0 collective-permute-done.other_ref.r_2_
  44.1 0.0 copy-done
  44.1 0.0 copy-done.1
  44.1 0.9 apply_one.1
  45.1 1.9 %collective-permute-start.3 = (bf16[128,512]{1,0:T(8,128)(2,1)S(1)}, bf16[128,512]{1,0:T(8,128)(2,1)S(1)}, u32[]{:S(2)}, u32[]{:S(2)}) collective-permute-start(bf16[128,512]{1,0:T(8,128)(2,1)S(1)} %get-tuple-element.29), channel_id=1, source_target_pairs={{1,2},{3,4},{5,6},{7,8},{9,10},{11,12},{13,14},{15,16},{17,18},{19... | collective-permute-start | bytes 393224 | tf_op jit(solution)/shard_map/ppermute | solution.py:252
  47.0 3.4 %collective-permute-start.4 = (bf16[128,256]{1,0:T(8,128)(2,1)S(1)}, bf16[128,256]{1,0:T(8,128)(2,1)S(1)}, u32[]{:S(2)}, u32[]{:S(2)}) collective-permute-start(bf16[128,256]{1,0:T(8,128)(2,1)S(1)} %get-tuple-element.30), channel_id=1, source_target_pairs={{1,4},{3,6},{5,8},{7,10},{9,12},{11,14},{13,16},{15,18},{17,20},{1... | collective-permute-start | bytes 196616 | tf_op jit(solution)/shard_map/ppermute | solution.py:252
  50.4 3.7 %collective-permute-done.4 = bf16[128,256]{1,0:T(8,128)(2,1)S(1)} collective-permute-done((bf16[128,256]{1,0:T(8,128)(2,1)S(1)}, bf16[128,256]{1,0:T(8,128)(2,1)S(1)}, u32[]{:S(2)}, u32[]{:S(2)}) %collective-permute-start.4) | collective-permute-done | bytes 65568 | tf_op jit(solution)/shard_map/ppermute | solution.py:252
  54.1 0.0 collective-permute-done.3
  54.1 2.3 %all_gather.13.r_9_ = bf16[256,768]{1,0:T(8,128)(2,1)S(1)} all-gather(bf16[128,768]{1,0:T(8,128)(2,1)S(1)} %pad_maximum_fusion.1), channel_id=1, replica_groups=mesh['dom'=256,'band'=2] {'band'}, dimensions={0}, use_global_device_ids=true | all-gather | bytes 589824 | tf_op jit(solution)/shard_map/all_gather | solution.py:257
  56.4 1.6 %apply_two.1 = (bf16[128,1536]{1,0:T(8,128)(2,1)S(1)}, f32[128,1024]{1,0:T(8,128)S(1)}, bf16[128,512]{1,0:T(8,128)(2,1)S(1)}, bf16[128,512]{1,0:T(8,128)(2,1)S(1)}, bf16[128,256]{1,0:T(8,128)(2,1)S(1)}) custom-call(s32[1]{0:T(128)} %bitcast.band_ref.r_0_, bf16[768,1536]{1,0:T(8,128)(2,1)S(1)} %build.1.mine_ref.r_1_, ...), custom_call_target="tpu_custom_call" | custom-call | tf_op jit(solution)/shard_map/apply_two/pallas_call | solution.py:232
  58.0 1.9 %collective-permute-start.5 = (bf16[128,512]{1,0:T(8,128)(2,1)S(1)}, bf16[128,512]{1,0:T(8,128)(2,1)S(1)}, u32[]{:S(2)}, u32[]{:S(2)}) collective-permute-start(bf16[128,512]{1,0:T(8,128)(2,1)S(1)} %get-tuple-element.33), channel_id=1, source_target_pairs={{1,2},{3,4},{5,6},{7,8},{9,10},{11,12},{13,14},{15,16},{17,18},{19... | collective-permute-start | bytes 393224 | tf_op jit(solution)/shard_map/ppermute | solution.py:252
  59.9 5.9 %collective-permute-start.6 = (bf16[128,256]{1,0:T(8,128)(2,1)S(1)}, bf16[128,256]{1,0:T(8,128)(2,1)S(1)}, u32[]{:S(2)}, u32[]{:S(2)}) collective-permute-start(bf16[128,256]{1,0:T(8,128)(2,1)S(1)} %get-tuple-element.34), channel_id=1, source_target_pairs={{1,4},{3,6},{5,8},{7,10},{9,12},{11,14},{13,16},{15,18},{17,20},{1... | collective-permute-start | bytes 196616 | tf_op jit(solution)/shard_map/ppermute | solution.py:252
  65.8 1.9 %collective-permute-done.6 = bf16[128,256]{1,0:T(8,128)(2,1)S(1)} collective-permute-done((bf16[128,256]{1,0:T(8,128)(2,1)S(1)}, bf16[128,256]{1,0:T(8,128)(2,1)S(1)}, u32[]{:S(2)}, u32[]{:S(2)}) %collective-permute-start.6) | collective-permute-done | bytes 65568 | tf_op jit(solution)/shard_map/ppermute | solution.py:252
  67.8 0.0 collective-permute-done.5
  67.8 2.1 %all_gather.14.r_9_ = bf16[256,768]{1,0:T(8,128)(2,1)S(1)} all-gather(bf16[128,768]{1,0:T(8,128)(2,1)S(1)} %pad_maximum_fusion.2), channel_id=1, replica_groups=mesh['dom'=256,'band'=2] {'band'}, dimensions={0}, use_global_device_ids=true | all-gather | bytes 589824 | tf_op jit(solution)/shard_map/all_gather | solution.py:257
  69.9 2.2 %apply_three.1 = (bf16[128,1536]{1,0:T(8,128)(2,1)}, f32[128,1024]{1,0:T(8,128)S(1)}, bf16[128,512]{1,0:T(8,128)(2,1)S(1)}, bf16[128,512]{1,0:T(8,128)(2,1)S(1)}, bf16[128,256]{1,0:T(8,128)(2,1)S(1)}) custom-call(s32[1]{0:T(128)} %bitcast.band_ref.r_0_, bf16[768,1536]{1,0:T(8,128)(2,1)S(1)} %build.1.mine_ref.r_1_, ...), custom_call_target="tpu_custom_call" | custom-call | tf_op jit(solution)/shard_map/apply_three/pallas_call | solution.py:232
  72.1 4.8 %collective-permute-start.7 = (bf16[128,512]{1,0:T(8,128)(2,1)S(1)}, bf16[128,512]{1,0:T(8,128)(2,1)S(1)}, u32[]{:S(2)}, u32[]{:S(2)}) collective-permute-start(bf16[128,512]{1,0:T(8,128)(2,1)S(1)} %get-tuple-element.37), channel_id=1, source_target_pairs={{1,2},{3,4},{5,6},{7,8},{9,10},{11,12},{13,14},{15,16},{17,18},{19... | collective-permute-start | bytes 393224 | tf_op jit(solution)/shard_map/ppermute | solution.py:252
  76.9 4.0 %collective-permute-start.8 = (bf16[128,256]{1,0:T(8,128)(2,1)S(1)}, bf16[128,256]{1,0:T(8,128)(2,1)S(1)}, u32[]{:S(2)}, u32[]{:S(2)}) collective-permute-start(bf16[128,256]{1,0:T(8,128)(2,1)S(1)} %get-tuple-element.38), channel_id=1, source_target_pairs={{1,4},{3,6},{5,8},{7,10},{9,12},{11,14},{13,16},{15,18},{17,20},{1... | collective-permute-start | bytes 196616 | tf_op jit(solution)/shard_map/ppermute | solution.py:252
  80.9 3.8 %collective-permute-done.8 = bf16[128,256]{1,0:T(8,128)(2,1)S(1)} collective-permute-done((bf16[128,256]{1,0:T(8,128)(2,1)S(1)}, bf16[128,256]{1,0:T(8,128)(2,1)S(1)}, u32[]{:S(2)}, u32[]{:S(2)}) %collective-permute-start.8) | collective-permute-done | bytes 65568 | tf_op jit(solution)/shard_map/ppermute | solution.py:252
  84.7 0.0 collective-permute-done.7
  84.7 2.1 %all_gather.15.got_ref = bf16[256,768]{1,0:T(8,128)(2,1)S(1)} all-gather(bf16[128,768]{1,0:T(8,128)(2,1)S(1)} %pad_maximum_fusion.3), channel_id=1, replica_groups=mesh['dom'=256,'band'=2] {'band'}, dimensions={0}, use_global_device_ids=true | all-gather | bytes 589824 | tf_op jit(solution)/shard_map/all_gather | solution.py:257
  86.8 1.4 apply_four.1
  88.2 34.1 %all_to_all.23 = f32[32,8,128]{2,1,0:T(8,128)S(1)} all-to-all(f32[32,8,128]{2,1,0:T(8,128)S(1)} %bitcast.6), channel_id=1, replica_groups={{0,1,2,3,4,5,6,7,128,129,130,131,132,133,134,135,256,257,258,259,260,26..., dimensions={0} | all-to-all | bytes 262144 | tf_op jit(solution)/shard_map/all_to_all | solution.py:273
  122.4 15.2 %all_to_all.24 = f32[16,8,128]{2,1,0:T(8,128)S(1)} all-to-all(f32[16,8,128]{2,1,0:T(8,128)S(1)} %broadcast_in_dim.4), channel_id=1, replica_groups={{0,8,16,24,32,40,48,56,64,72,80,88,96,104,112,120},{1,9,17,25,33,41,49,..., dimensions={0} | all-to-all | bytes 131072 | tf_op jit(solution)/shard_map/all_to_all | solution.py:273
  137.6 12.8 %all_to_all.25 = f32[32,8,128]{2,1,0:T(8,128)S(1)} all-to-all(f32[32,8,128]{2,1,0:T(8,128)S(1)} %broadcast_in_dim.5), channel_id=1, replica_groups={{0,1,2,3,4,5,6,7,128,129,130,131,132,133,134,135,256,257,258,259,260,26..., dimensions={0} | all-to-all | bytes 262144 | tf_op jit(solution)/shard_map/all_to_all | solution.py:273
  150.5 7.6 %finish.1 = (f32[128,512]{1,0:T(8,128)}, f32[128,128]{1,0:T(8,128)}) custom-call(f32[256,128]{1,0:T(8,128)S(1)} %bitcast.5, bf16[128,512]{1,0:T(8,128)(2,1)S(1)} %get-tuple-element.41.refs_1_), custom_call_target="tpu_custom_call" | custom-call | tf_op jit(solution)/shard_map/finish/pallas_call | solution.py:368
  (10 shorter events, 0.1 us)
Async XLA Ops:
  2.5 0.8 copy-start.2
  3.2 0.7 copy-start.3
  4.0 0.7 copy-start.4
  4.6 30.6 %copy-start.7 = (bf16[80,256]{1,0:T(8,128)(2,1)S(1)}, bf16[80,256]{1,0:T(8,128)(2,1)}, u32[]{:S(2)}) copy-start(bf16[80,256]{1,0:T(8,128)(2,1)} %get-tuple-element.25) | copy-start | bytes 122884
  4.6 31.9 %copy-start.6 = (bf16[80,256]{1,0:T(8,128)(2,1)S(1)}, bf16[80,256]{1,0:T(8,128)(2,1)}, u32[]{:S(2)}) copy-start(bf16[80,256]{1,0:T(8,128)(2,1)} %get-tuple-element.26) | copy-start | bytes 122884
  4.6 36.6 %copy-start.5 = (bf16[64,1024]{1,0:T(8,128)(2,1)S(1)}, bf16[64,1024]{1,0:T(8,128)(2,1)}, u32[]{:S(2)}) copy-start(bf16[64,1024]{1,0:T(8,128)(2,1)} %block_ref.1) | copy-start | bytes 393220
  4.6 39.5 %copy-start = (f32[1024]{0:T(1024)S(1)}, f32[1024]{0:T(1024)}, u32[]{:S(2)}) copy-start(f32[1024]{0:T(1024)} %param.11) | copy-start | bytes 12292
  4.6 39.5 %copy-start.1 = (s32[1,2,256]{2,1,0:T(2,128)S(1)}, s32[1,2,256]{2,1,0:T(2,128)}, u32[]{:S(2)}) copy-start(s32[1,2,256]{2,1,0:T(2,128)} %param.8) | copy-start | bytes 6148
  26.4 17.8 %collective-permute-start = (bf16[768,1536]{1,0:T(8,128)(2,1)S(1)}, bf16[768,1536]{1,0:T(8,128)(2,1)S(1)}, u32[]{:S(2)}, u32[]{:S(2)}) collective-permute-start(bf16[768,1536]{1,0:T(8,128)(2,1)S(1)} %build.1.mine_ref.r_1_), channel_id=1, source_target_pairs={{0,1},{1,0},{2,3},{3,2},{4,5},{5,4},{6,7},{7,6},{8,9},{9,8},{10,11... | collective-permute-start | bytes 7077896 | tf_op jit(solution)/shard_map/ppermute | solution.py:393
  35.2 2.6 %collective-permute-start.1 = (bf16[80,256]{1,0:T(8,128)(2,1)S(1)}, bf16[80,256]{1,0:T(8,128)(2,1)S(1)}, u32[]{:S(2)}, u32[]{:S(2)}) collective-permute-start(bf16[80,256]{1,0:T(8,128)(2,1)S(1)} %copy-done.7), channel_id=1, source_target_pairs={{0,2},{2,4},{4,6},{6,8},{8,10},{10,12},{12,14},{14,16},{16,18},{18... | collective-permute-start | bytes 122888 | tf_op jit(solution)/shard_map/ppermute | solution.py:245
  36.5 4.7 %collective-permute-start.2 = (bf16[80,256]{1,0:T(8,128)(2,1)S(1)}, bf16[80,256]{1,0:T(8,128)(2,1)S(1)}, u32[]{:S(2)}, u32[]{:S(2)}) collective-permute-start(bf16[80,256]{1,0:T(8,128)(2,1)S(1)} %copy-done.6), channel_id=1, source_target_pairs={{2,0},{4,2},{6,4},{8,6},{10,8},{12,10},{14,12},{16,14},{18,16},{20... | collective-permute-start | bytes 122888 | tf_op jit(solution)/shard_map/ppermute | solution.py:245
  45.1 9.0 %collective-permute-start.3 = (bf16[128,512]{1,0:T(8,128)(2,1)S(1)}, bf16[128,512]{1,0:T(8,128)(2,1)S(1)}, u32[]{:S(2)}, u32[]{:S(2)}) collective-permute-start(bf16[128,512]{1,0:T(8,128)(2,1)S(1)} %get-tuple-element.29), channel_id=1, source_target_pairs={{1,2},{3,4},{5,6},{7,8},{9,10},{11,12},{13,14},{15,16},{17,18},{19... | collective-permute-start | bytes 393224 | tf_op jit(solution)/shard_map/ppermute | solution.py:252
  47.0 7.1 %collective-permute-start.4 = (bf16[128,256]{1,0:T(8,128)(2,1)S(1)}, bf16[128,256]{1,0:T(8,128)(2,1)S(1)}, u32[]{:S(2)}, u32[]{:S(2)}) collective-permute-start(bf16[128,256]{1,0:T(8,128)(2,1)S(1)} %get-tuple-element.30), channel_id=1, source_target_pairs={{1,4},{3,6},{5,8},{7,10},{9,12},{11,14},{13,16},{15,18},{17,20},{1... | collective-permute-start | bytes 196616 | tf_op jit(solution)/shard_map/ppermute | solution.py:252
  58.0 9.8 %collective-permute-start.5 = (bf16[128,512]{1,0:T(8,128)(2,1)S(1)}, bf16[128,512]{1,0:T(8,128)(2,1)S(1)}, u32[]{:S(2)}, u32[]{:S(2)}) collective-permute-start(bf16[128,512]{1,0:T(8,128)(2,1)S(1)} %get-tuple-element.33), channel_id=1, source_target_pairs={{1,2},{3,4},{5,6},{7,8},{9,10},{11,12},{13,14},{15,16},{17,18},{19... | collective-permute-start | bytes 393224 | tf_op jit(solution)/shard_map/ppermute | solution.py:252
  59.9 7.9 %collective-permute-start.6 = (bf16[128,256]{1,0:T(8,128)(2,1)S(1)}, bf16[128,256]{1,0:T(8,128)(2,1)S(1)}, u32[]{:S(2)}, u32[]{:S(2)}) collective-permute-start(bf16[128,256]{1,0:T(8,128)(2,1)S(1)} %get-tuple-element.34), channel_id=1, source_target_pairs={{1,4},{3,6},{5,8},{7,10},{9,12},{11,14},{13,16},{15,18},{17,20},{1... | collective-permute-start | bytes 196616 | tf_op jit(solution)/shard_map/ppermute | solution.py:252
  72.1 12.6 %collective-permute-start.7 = (bf16[128,512]{1,0:T(8,128)(2,1)S(1)}, bf16[128,512]{1,0:T(8,128)(2,1)S(1)}, u32[]{:S(2)}, u32[]{:S(2)}) collective-permute-start(bf16[128,512]{1,0:T(8,128)(2,1)S(1)} %get-tuple-element.37), channel_id=1, source_target_pairs={{1,2},{3,4},{5,6},{7,8},{9,10},{11,12},{13,14},{15,16},{17,18},{19... | collective-permute-start | bytes 393224 | tf_op jit(solution)/shard_map/ppermute | solution.py:252
  76.9 7.7 %collective-permute-start.8 = (bf16[128,256]{1,0:T(8,128)(2,1)S(1)}, bf16[128,256]{1,0:T(8,128)(2,1)S(1)}, u32[]{:S(2)}, u32[]{:S(2)}) collective-permute-start(bf16[128,256]{1,0:T(8,128)(2,1)S(1)} %get-tuple-element.38), channel_id=1, source_target_pairs={{1,4},{3,6},{5,8},{7,10},{9,12},{11,14},{13,16},{15,18},{17,20},{1... | collective-permute-start | bytes 196616 | tf_op jit(solution)/shard_map/ppermute | solution.py:252

commit v3 on v2

--- a/solution.py
+++ b/solution.py
@@ -71,21 +71,18 @@
     matrix = matrix_ref[...].astype(F32)
     mats[0:entries, 0:entries] = matrix
     mats[CELL_PAD : CELL_PAD + entries, CELL_PAD : CELL_PAD + entries] = matrix
-    pair_matrix = mats[...].astype(BF16)
-    first = pl.multiple_of(band_ref[0] * half, 128)
+    pair_matrix = mats[...].T.astype(BF16)
+    first = band_ref[0] * half
     lane = lax.broadcasted_iota(jnp.int32, (1, 2 * CELL_PAD), 1)
     for pair in range(cells // 2):
+        rows = [ids[c : c + 1, :] for c in (2 * pair, 2 * pair + 1)]
+        row = jnp.concatenate(rows, axis=1)
         cols = slice(pair * 2 * CELL_PAD, (pair + 1) * 2 * CELL_PAD)
-        for one in (0, 1):
-            c = 2 * pair + one
-            hot[:, c * CELL_PAD : (c + 1) * CELL_PAD] = one_hot(full, ids[c : c + 1, :])
         gain = jnp.where(lane < CELL_PAD, scale_ref[2 * pair], scale_ref[2 * pair + 1])
-        left[:, cols] = (nt(hot[pl.ds(first, half), cols], pair_matrix) * gain).astype(BF16)
-
-    @pl.loop(0, full // 256)
-    def _(tile):
-        rows = pl.ds(pl.multiple_of(tile * 256, 256), 256)
-        out_ref[:, rows] = nt(left[...], hot[rows, :]).astype(BF16)
+        left[:, cols] = (nn(one_hot(half, row - first), pair_matrix) * gain).astype(BF16)
+        hot[:, cols] = one_hot(full, row)
+    for at in range(0, half, 256):
+        out_ref[at : at + 256, :] = nt(left[at : at + 256, :], hot[...]).astype(BF16)
 
 
 def build(band, cell_nodes, cell_matrix, cell_scale, full):
@@ -327,29 +324,38 @@
 
 def finish_body(scale, total_ref, own_ref, ortho_out, projected_out, inverse_ref):
     size = total_ref.shape[1]
+    block = 32
     schur = total_ref[0:size, :] * scale
     at = lax.broadcasted_iota(jnp.int32, (size, size), 0)
     beside = (at == lax.broadcasted_iota(jnp.int32, (size, size), 1)).astype(F32)
-    for first in range(0, size, 8):
-        top, top_beside = schur[0:8], beside[0:8]
-        inv = inverse_of_eight(top, first)
-        rows = [jnp.broadcast_to(top[i : i + 1], top.shape) for i in range(8)]
-        rows_beside = [jnp.broadcast_to(top_beside[i : i + 1], top.shape) for i in range(8)]
-        solved = [weighted([inv[i, k] for k in range(i + 1)], rows) for i in range(8)]
-        solved_beside = [weighted([inv[i, k] for k in range(i + 1)], rows_beside) for i in range(8)]
-        inverse_ref[first : first + 8, :] = stack(solved_beside)
-        if first + 8 == size:
-            break
-        twice = stack([weighted([inv[k, i] for k in range(i, 8)], solved[i:]) for i in range(8)])
-        twice_beside = stack([weighted([inv[k, i] for k in range(i, 8)], solved_beside[i:]) for i in range(8)])
-        both = jnp.concatenate([twice, twice_beside], axis=1)
-        pieces = [both]
-        if first:
-            pieces = [jnp.zeros((first, 2 * size), F32)] + pieces
-        pieces.append(jnp.zeros((size - first - 8, 2 * size), F32))
-        taken = exact(schur[8:], jnp.concatenate(pieces, axis=0))
-        schur = schur[8:] - taken[:, 0:size]
-        beside = beside[8:] - taken[:, size:]
+    for start in range(0, size, block):
+        here = [schur[i : i + 8] for i in range(0, block, 8)]
+        here_beside = [beside[i : i + 8] for i in range(0, block, 8)]
+        done, done_beside = [], []
+        for p in range(block // 8):
+            first = start + 8 * p
+            top, top_beside = here[p], here_beside[p]
+            inv = inverse_of_eight(top, first)
+            rows = [jnp.broadcast_to(top[i : i + 1], top.shape) for i in range(8)]
+            rows_beside = [jnp.broadcast_to(top_beside[i : i + 1], top.shape) for i in range(8)]
+            solved = [weighted([inv[i, k] for k in range(i + 1)], rows) for i in range(8)]
+            solved_beside = [weighted([inv[i, k] for k in range(i + 1)], rows_beside) for i in range(8)]
+            done.append(stack(solved))
+            done_beside.append(stack(solved_beside))
+            inverse_ref[first : first + 8, :] = done_beside[-1]
+            if p + 1 < block // 8:
+                twice = [weighted([inv[k, i] for k in range(i, 8)], solved[i:]) for i in range(8)]
+                twice_beside = [weighted([inv[k, i] for k in range(i, 8)], solved_beside[i:]) for i in range(8)]
+            for q in range(p + 1, block // 8):
+                columns = [jnp.broadcast_to(here[q][:, first + j : first + j + 1], top.shape) for j in range(8)]
+                here[q] = here[q] - weighted(columns, twice)
+                here_beside[q] = here_beside[q] - weighted(columns, twice_beside)
+        if start + block < size:
+            solved = jnp.concatenate(done, axis=0)
+            both = jnp.concatenate([solved, jnp.concatenate(done_beside, axis=0)], axis=1)
+            taken = exact(solved.T[start + block :], both)
+            schur = schur[block:] - taken[:, 0:size]
+            beside = beside[block:] - taken[:, size:]
     inverse = inverse_ref[...]
     coarse = inverse.astype(BF16)
     rest = inverse - coarse.astype(F32)
@@ -390,6 +396,7 @@
     from_left = shift(to_right, "dom", 1)
     from_right = shift(to_left, "dom", -1)
     mine = build(band, cell_nodes, cell_matrix, cell_scale, full)
+    mine, from_left, from_right = lax.optimization_barrier((mine, from_left, from_right))
     other = lax.ppermute(mine, "band", [(0, 1), (1, 0)])
     x_here = jnp.concatenate([block, from_left[:states_here], from_right[:states_here]], axis=1)
     x0 = lax.all_gather(x_here, "band", axis=0, tiled=True)

time: 159 us -> 146 us (0.918)
  Pallas kernels: 37.3 us -> 26.2 us
  waiting for transfers between devices: 12.8 us -> 8.73 us
  blocking collectives: 71.5 us -> 73.2 us
    pallas_call x1, Pallas kernels: 21.7 us -> 12.3 us  [build(): pl.pallas_call(build_body, out_shape=jax.ShapeDtypeStruct((half, full), B...]
    ppermute x2, waiting for transfers between devices: 3.43 us -> 0.01 us  [shift(): lax.ppermute(x, axis, [(i, i + by) for i in range(devices) if 0 <= i + by...]
    ppermute x1, starting transfers between devices: 8.78 us -> 6.05 us  [shards(): other = lax.ppermute(mine, 'band', [(0, 1), (1, 0)])]
    ppermute x2, starting transfers between devices: 2.58 us -> 5.31 us  [shift(): lax.ppermute(x, axis, [(i, i + by) for i in range(devices) if 0 <= i + by...]
    pallas_call x1, Pallas kernels: 7.6 us -> 5.86 us  [finish(): pl.pallas_call(lambda *refs: finish_body(scale, *refs), out_shape=(jax.Sh...]
  transfers between devices with their start and end apart: 9 -> 9, of which waited for: 4 -> 3; matrix products, arithmetic and copies ran while one was open for 0% -> 0% of each run, Pallas kernels for 0% -> 9%
where the time goes in v3:
time: 146 us; the launch traced here: 145 us
  blocking collectives  73.2 us (50%)
  starting transfers between devices  33.7 us (23%)
  Pallas kernels  26.2 us (18%)
  waiting for transfers between devices  8.73 us (6%)
  local copies, waits for them, and re-layouts  2.17 us (1%)
    all_to_all x3, blocking collectives, swap_pieces(): return lax.all_to_all(x, BOTH, 0, 0, axis_index_groups=groups, tiled=True)  62.4 us
    ppermute x6, starting transfers between devices, across(): return lax.ppermute(x, BOTH, pairs)  22.3 us
    pallas_call x1, Pallas kernels, build(): pl.pallas_call(build_body, out_shape=jax.ShapeDtypeStruct((half, full), B...  12.3 us
    ppermute x6, waiting for transfers between devices, across(): return lax.ppermute(x, BOTH, pairs)  8.72 us
    all_gather x3, blocking collectives, exchange(): return lax.all_gather(got, 'band', axis=0, tiled=True)  6.44 us
    pallas_call x4, Pallas kernels, stage_call(): pl.pallas_call(body, out_shape=tuple(shapes), in_specs=[spec(pltpu.SMEM)]...  6.14 us
    ppermute x1, starting transfers between devices, shards(): other = lax.ppermute(mine, 'band', [(0, 1), (1, 0)])  6.05 us
    pallas_call x1, Pallas kernels, finish(): pl.pallas_call(lambda *refs: finish_body(scale, *refs), out_shape=(jax.Sh...  5.86 us
  transfers between devices with their start and end apart: 9, of which 3 were waited for; matrix products, arithmetic and copies ran while one was open for 0% of the time, Pallas kernels for 9%

profile of v3, /device:TPU:1, one launch (start us, length us, event | category | flops | bytes accessed | tf_op | source)
XLA Modules:
  0.0 144.9 jit_solution(15306731529548712432)
XLA Ops:
  0.6 1.8 %send_first.1 = (bf16[80,256]{1,0:T(8,128)(2,1)}, bf16[80,256]{1,0:T(8,128)(2,1)}) custom-call(bf16[64,1024]{1,0:T(8,128)(2,1)} %block_ref.1, s32[2,256]{1,0:T(2,128)} %bitcast.11), custom_call_target="tpu_custom_call" | custom-call | tf_op jit(solution)/shard_map/send_first/pallas_call | solution.py:56
  2.5 4.0 %collective-permute-start = (bf16[80,256]{1,0:T(8,128)(2,1)}, bf16[80,256]{1,0:T(8,128)(2,1)S(1)}, u32[]{:S(2)}, u32[]{:S(2)}) collective-permute-start(bf16[80,256]{1,0:T(8,128)(2,1)} %get-tuple-element.28), channel_id=1, source_target_pairs={{0,2},{2,4},{4,6},{6,8},{8,10},{10,12},{12,14},{14,16},{16,18},{18... | collective-permute-start | bytes 122888 | tf_op jit(solution)/shard_map/ppermute | solution.py:242
  6.5 1.3 collective-permute-start.1
  7.8 0.0 copy-start.2
  7.8 0.7 copy-done.2
  8.6 0.0 copy-start.3
  8.6 0.7 copy-done.3
  9.3 0.0 copy-start.4
  9.3 0.7 copy-done.4
  9.9 0.0 copy-start.5
  9.9 0.0 copy-start
  9.9 0.0 copy-start.1
  9.9 12.3 %build.1.mine_ref.r_1_ = bf16[768,1536]{1,0:T(8,128)(2,1)S(1)} custom-call(s32[1]{0:T(128)} %bitcast.band_ref.r_0_, s32[32,125]{1,0:T(8,128)S(1)} %copy-done.3, bf16[125,125]{1,0:T(8,128)(2,1)S(1)} %copy-done.2, f32[32]{0:T(128)S(1)} %copy-done.4), custom_call_target="tpu_custom_call" | custom-call | flops 9663676416 | bytes 2359296 | tf_op jit(solution)/shard_map/build/pallas_call | solution.py:92
  22.3 0.0 collective-permute-done.r_5_.fl_ref
  22.3 0.0 collective-permute-done.1.r_6_.fr_ref
  22.3 6.0 %collective-permute-start.2 = (bf16[768,1536]{1,0:T(8,128)(2,1)S(1)}, bf16[768,1536]{1,0:T(8,128)(2,1)S(1)}, u32[]{:S(2)}, u32[]{:S(2)}) collective-permute-start(bf16[768,1536]{1,0:T(8,128)(2,1)S(1)} %build.1.mine_ref.r_1_), channel_id=1, source_target_pairs={{0,1},{1,0},{2,3},{3,2},{4,5},{5,4},{6,7},{7,6},{8,9},{9,8},{10,11... | collective-permute-start | bytes 7077896 | tf_op jit(solution)/shard_map/ppermute | solution.py:400
  28.4 0.0 copy-done.5
  28.4 4.4 %all_gather.12.x_ref.r_10_ = bf16[128,1536]{1,0:T(8,128)(2,1)S(1)} all-gather(bf16[64,1536]{1,0:T(8,128)(2,1)S(1)} %pad_maximum_fusion), channel_id=1, replica_groups=mesh['dom'=256,'band'=2] {'band'}, dimensions={0}, use_global_device_ids=true | all-gather | bytes 589824 | tf_op jit(solution)/shard_map/all_gather | solution.py:402
  32.8 0.0 collective-permute-done.2.other_ref.r_2_
  32.8 0.0 copy-done
  32.8 0.0 copy-done.1
  32.8 0.9 apply_one.1
  33.7 4.5 %collective-permute-start.3 = (bf16[128,512]{1,0:T(8,128)(2,1)S(1)}, bf16[128,512]{1,0:T(8,128)(2,1)S(1)}, u32[]{:S(2)}, u32[]{:S(2)}) collective-permute-start(bf16[128,512]{1,0:T(8,128)(2,1)S(1)} %get-tuple-element.35), channel_id=1, source_target_pairs={{1,2},{3,4},{5,6},{7,8},{9,10},{11,12},{13,14},{15,16},{17,18},{19... | collective-permute-start | bytes 393224 | tf_op jit(solution)/shard_map/ppermute | solution.py:249
  38.2 3.7 %collective-permute-start.4 = (bf16[128,256]{1,0:T(8,128)(2,1)S(1)}, bf16[128,256]{1,0:T(8,128)(2,1)S(1)}, u32[]{:S(2)}, u32[]{:S(2)}) collective-permute-start(bf16[128,256]{1,0:T(8,128)(2,1)S(1)} %get-tuple-element.36), channel_id=1, source_target_pairs={{1,4},{3,6},{5,8},{7,10},{9,12},{11,14},{13,16},{15,18},{17,20},{1... | collective-permute-start | bytes 196616 | tf_op jit(solution)/shard_map/ppermute | solution.py:249
  42.0 3.4 %collective-permute-done.4 = bf16[128,256]{1,0:T(8,128)(2,1)S(1)} collective-permute-done((bf16[128,256]{1,0:T(8,128)(2,1)S(1)}, bf16[128,256]{1,0:T(8,128)(2,1)S(1)}, u32[]{:S(2)}, u32[]{:S(2)}) %collective-permute-start.4) | collective-permute-done | bytes 65568 | tf_op jit(solution)/shard_map/ppermute | solution.py:249
  45.3 0.0 collective-permute-done.3
  45.3 2.3 %all_gather.13.r_9_ = bf16[256,768]{1,0:T(8,128)(2,1)S(1)} all-gather(bf16[128,768]{1,0:T(8,128)(2,1)S(1)} %pad_maximum_fusion.1), channel_id=1, replica_groups=mesh['dom'=256,'band'=2] {'band'}, dimensions={0}, use_global_device_ids=true | all-gather | bytes 589824 | tf_op jit(solution)/shard_map/all_gather | solution.py:254
  47.6 1.6 %apply_two.1 = (bf16[128,1536]{1,0:T(8,128)(2,1)S(1)}, f32[128,1024]{1,0:T(8,128)S(1)}, bf16[128,512]{1,0:T(8,128)(2,1)S(1)}, bf16[128,512]{1,0:T(8,128)(2,1)S(1)}, bf16[128,256]{1,0:T(8,128)(2,1)S(1)}) custom-call(s32[1]{0:T(128)} %bitcast.band_ref.r_0_, bf16[768,1536]{1,0:T(8,128)(2,1)S(1)} %build.1.mine_ref.r_1_, ...), custom_call_target="tpu_custom_call" | custom-call | tf_op jit(solution)/shard_map/apply_two/pallas_call | solution.py:229
  49.2 1.9 %collective-permute-start.5 = (bf16[128,512]{1,0:T(8,128)(2,1)S(1)}, bf16[128,512]{1,0:T(8,128)(2,1)S(1)}, u32[]{:S(2)}, u32[]{:S(2)}) collective-permute-start(bf16[128,512]{1,0:T(8,128)(2,1)S(1)} %get-tuple-element.39), channel_id=1, source_target_pairs={{1,2},{3,4},{5,6},{7,8},{9,10},{11,12},{13,14},{15,16},{17,18},{19... | collective-permute-start | bytes 393224 | tf_op jit(solution)/shard_map/ppermute | solution.py:249
  51.1 3.7 %collective-permute-start.6 = (bf16[128,256]{1,0:T(8,128)(2,1)S(1)}, bf16[128,256]{1,0:T(8,128)(2,1)S(1)}, u32[]{:S(2)}, u32[]{:S(2)}) collective-permute-start(bf16[128,256]{1,0:T(8,128)(2,1)S(1)} %get-tuple-element.40), channel_id=1, source_target_pairs={{1,4},{3,6},{5,8},{7,10},{9,12},{11,14},{13,16},{15,18},{17,20},{1... | collective-permute-start | bytes 196616 | tf_op jit(solution)/shard_map/ppermute | solution.py:249
  54.9 3.4 %collective-permute-done.6 = bf16[128,256]{1,0:T(8,128)(2,1)S(1)} collective-permute-done((bf16[128,256]{1,0:T(8,128)(2,1)S(1)}, bf16[128,256]{1,0:T(8,128)(2,1)S(1)}, u32[]{:S(2)}, u32[]{:S(2)}) %collective-permute-start.6) | collective-permute-done | bytes 65568 | tf_op jit(solution)/shard_map/ppermute | solution.py:249
  58.2 0.0 collective-permute-done.5
  58.3 2.1 %all_gather.14.r_9_ = bf16[256,768]{1,0:T(8,128)(2,1)S(1)} all-gather(bf16[128,768]{1,0:T(8,128)(2,1)S(1)} %pad_maximum_fusion.2), channel_id=1, replica_groups=mesh['dom'=256,'band'=2] {'band'}, dimensions={0}, use_global_device_ids=true | all-gather | bytes 589824 | tf_op jit(solution)/shard_map/all_gather | solution.py:254
  60.3 2.2 %apply_three.1 = (bf16[128,1536]{1,0:T(8,128)(2,1)}, f32[128,1024]{1,0:T(8,128)S(1)}, bf16[128,512]{1,0:T(8,128)(2,1)S(1)}, bf16[128,512]{1,0:T(8,128)(2,1)S(1)}, bf16[128,256]{1,0:T(8,128)(2,1)S(1)}) custom-call(s32[1]{0:T(128)} %bitcast.band_ref.r_0_, bf16[768,1536]{1,0:T(8,128)(2,1)S(1)} %build.1.mine_ref.r_1_, ...), custom_call_target="tpu_custom_call" | custom-call | tf_op jit(solution)/shard_map/apply_three/pallas_call | solution.py:229
  62.6 3.4 %collective-permute-start.7 = (bf16[128,512]{1,0:T(8,128)(2,1)S(1)}, bf16[128,512]{1,0:T(8,128)(2,1)S(1)}, u32[]{:S(2)}, u32[]{:S(2)}) collective-permute-start(bf16[128,512]{1,0:T(8,128)(2,1)S(1)} %get-tuple-element.43), channel_id=1, source_target_pairs={{1,2},{3,4},{5,6},{7,8},{9,10},{11,12},{13,14},{15,16},{17,18},{19... | collective-permute-start | bytes 393224 | tf_op jit(solution)/shard_map/ppermute | solution.py:249
  65.9 5.1 %collective-permute-start.8 = (bf16[128,256]{1,0:T(8,128)(2,1)S(1)}, bf16[128,256]{1,0:T(8,128)(2,1)S(1)}, u32[]{:S(2)}, u32[]{:S(2)}) collective-permute-start(bf16[128,256]{1,0:T(8,128)(2,1)S(1)} %get-tuple-element.44), channel_id=1, source_target_pairs={{1,4},{3,6},{5,8},{7,10},{9,12},{11,14},{13,16},{15,18},{17,20},{1... | collective-permute-start | bytes 196616 | tf_op jit(solution)/shard_map/ppermute | solution.py:249
  71.0 2.0 %collective-permute-done.8 = bf16[128,256]{1,0:T(8,128)(2,1)S(1)} collective-permute-done((bf16[128,256]{1,0:T(8,128)(2,1)S(1)}, bf16[128,256]{1,0:T(8,128)(2,1)S(1)}, u32[]{:S(2)}, u32[]{:S(2)}) %collective-permute-start.8) | collective-permute-done | bytes 65568 | tf_op jit(solution)/shard_map/ppermute | solution.py:249
  73.0 0.0 collective-permute-done.7
  73.0 2.1 %all_gather.15.got_ref = bf16[256,768]{1,0:T(8,128)(2,1)S(1)} all-gather(bf16[128,768]{1,0:T(8,128)(2,1)S(1)} %pad_maximum_fusion.3), channel_id=1, replica_groups=mesh['dom'=256,'band'=2] {'band'}, dimensions={0}, use_global_device_ids=true | all-gather | bytes 589824 | tf_op jit(solution)/shard_map/all_gather | solution.py:254
  75.1 1.4 apply_four.1
  76.6 32.8 %all_to_all.23 = f32[32,8,128]{2,1,0:T(8,128)S(1)} all-to-all(f32[32,8,128]{2,1,0:T(8,128)S(1)} %bitcast.6), channel_id=1, replica_groups={{0,1,2,3,4,5,6,7,128,129,130,131,132,133,134,135,256,257,258,259,260,26..., dimensions={0} | all-to-all | bytes 262144 | tf_op jit(solution)/shard_map/all_to_all | solution.py:270
  109.4 16.8 %all_to_all.24 = f32[16,8,128]{2,1,0:T(8,128)S(1)} all-to-all(f32[16,8,128]{2,1,0:T(8,128)S(1)} %broadcast_in_dim.4), channel_id=1, replica_groups={{0,8,16,24,32,40,48,56,64,72,80,88,96,104,112,120},{1,9,17,25,33,41,49,..., dimensions={0} | all-to-all | bytes 131072 | tf_op jit(solution)/shard_map/all_to_all | solution.py:270
  126.2 12.8 %all_to_all.25 = f32[32,8,128]{2,1,0:T(8,128)S(1)} all-to-all(f32[32,8,128]{2,1,0:T(8,128)S(1)} %broadcast_in_dim.5), channel_id=1, replica_groups={{0,1,2,3,4,5,6,7,128,129,130,131,132,133,134,135,256,257,258,259,260,26..., dimensions={0} | all-to-all | bytes 262144 | tf_op jit(solution)/shard_map/all_to_all | solution.py:270
  139.0 5.9 %finish.1 = (f32[128,512]{1,0:T(8,128)}, f32[128,128]{1,0:T(8,128)}) custom-call(f32[256,128]{1,0:T(8,128)S(1)} %bitcast.5, bf16[128,512]{1,0:T(8,128)(2,1)S(1)} %get-tuple-element.47.refs_1_), custom_call_target="tpu_custom_call" | custom-call | tf_op jit(solution)/shard_map/finish/pallas_call | solution.py:374
  (10 shorter events, 0.1 us)
Async XLA Ops:
  2.5 19.8 %collective-permute-start = (bf16[80,256]{1,0:T(8,128)(2,1)}, bf16[80,256]{1,0:T(8,128)(2,1)S(1)}, u32[]{:S(2)}, u32[]{:S(2)}) collective-permute-start(bf16[80,256]{1,0:T(8,128)(2,1)} %get-tuple-element.28), channel_id=1, source_target_pairs={{0,2},{2,4},{4,6},{6,8},{8,10},{10,12},{12,14},{14,16},{16,18},{18... | collective-permute-start | bytes 122888 | tf_op jit(solution)/shard_map/ppermute | solution.py:242
  6.5 15.8 %collective-permute-start.1 = (bf16[80,256]{1,0:T(8,128)(2,1)}, bf16[80,256]{1,0:T(8,128)(2,1)S(1)}, u32[]{:S(2)}, u32[]{:S(2)}) collective-permute-start(bf16[80,256]{1,0:T(8,128)(2,1)} %get-tuple-element.29), channel_id=1, source_target_pairs={{2,0},{4,2},{6,4},{8,6},{10,8},{12,10},{14,12},{16,14},{18,16},{20... | collective-permute-start | bytes 122888 | tf_op jit(solution)/shard_map/ppermute | solution.py:242
  7.8 0.8 copy-start.2
  8.6 0.7 copy-start.3
  9.3 0.7 copy-start.4
  9.9 18.4 %copy-start.5 = (bf16[64,1024]{1,0:T(8,128)(2,1)S(1)}, bf16[64,1024]{1,0:T(8,128)(2,1)}, u32[]{:S(2)}) copy-start(bf16[64,1024]{1,0:T(8,128)(2,1)} %block_ref.1) | copy-start | bytes 393220
  9.9 22.8 %copy-start = (f32[1024]{0:T(1024)S(1)}, f32[1024]{0:T(1024)}, u32[]{:S(2)}) copy-start(f32[1024]{0:T(1024)} %param.11) | copy-start | bytes 12292
  9.9 22.8 %copy-start.1 = (s32[1,2,256]{2,1,0:T(2,128)S(1)}, s32[1,2,256]{2,1,0:T(2,128)}, u32[]{:S(2)}) copy-start(s32[1,2,256]{2,1,0:T(2,128)} %param.8) | copy-start | bytes 6148
  22.3 10.5 %collective-permute-start.2 = (bf16[768,1536]{1,0:T(8,128)(2,1)S(1)}, bf16[768,1536]{1,0:T(8,128)(2,1)S(1)}, u32[]{:S(2)}, u32[]{:S(2)}) collective-permute-start(bf16[768,1536]{1,0:T(8,128)(2,1)S(1)} %build.1.mine_ref.r_1_), channel_id=1, source_target_pairs={{0,1},{1,0},{2,3},{3,2},{4,5},{5,4},{6,7},{7,6},{8,9},{9,8},{10,11... | collective-permute-start | bytes 7077896 | tf_op jit(solution)/shard_map/ppermute | solution.py:400
  33.7 11.6 %collective-permute-start.3 = (bf16[128,512]{1,0:T(8,128)(2,1)S(1)}, bf16[128,512]{1,0:T(8,128)(2,1)S(1)}, u32[]{:S(2)}, u32[]{:S(2)}) collective-permute-start(bf16[128,512]{1,0:T(8,128)(2,1)S(1)} %get-tuple-element.35), channel_id=1, source_target_pairs={{1,2},{3,4},{5,6},{7,8},{9,10},{11,12},{13,14},{15,16},{17,18},{19... | collective-permute-start | bytes 393224 | tf_op jit(solution)/shard_map/ppermute | solution.py:249
  38.2 7.1 %collective-permute-start.4 = (bf16[128,256]{1,0:T(8,128)(2,1)S(1)}, bf16[128,256]{1,0:T(8,128)(2,1)S(1)}, u32[]{:S(2)}, u32[]{:S(2)}) collective-permute-start(bf16[128,256]{1,0:T(8,128)(2,1)S(1)} %get-tuple-element.36), channel_id=1, source_target_pairs={{1,4},{3,6},{5,8},{7,10},{9,12},{11,14},{13,16},{15,18},{17,20},{1... | collective-permute-start | bytes 196616 | tf_op jit(solution)/shard_map/ppermute | solution.py:249
  49.2 9.0 %collective-permute-start.5 = (bf16[128,512]{1,0:T(8,128)(2,1)S(1)}, bf16[128,512]{1,0:T(8,128)(2,1)S(1)}, u32[]{:S(2)}, u32[]{:S(2)}) collective-permute-start(bf16[128,512]{1,0:T(8,128)(2,1)S(1)} %get-tuple-element.39), channel_id=1, source_target_pairs={{1,2},{3,4},{5,6},{7,8},{9,10},{11,12},{13,14},{15,16},{17,18},{19... | collective-permute-start | bytes 393224 | tf_op jit(solution)/shard_map/ppermute | solution.py:249
  51.1 7.1 %collective-permute-start.6 = (bf16[128,256]{1,0:T(8,128)(2,1)S(1)}, bf16[128,256]{1,0:T(8,128)(2,1)S(1)}, u32[]{:S(2)}, u32[]{:S(2)}) collective-permute-start(bf16[128,256]{1,0:T(8,128)(2,1)S(1)} %get-tuple-element.40), channel_id=1, source_target_pairs={{1,4},{3,6},{5,8},{7,10},{9,12},{11,14},{13,16},{15,18},{17,20},{1... | collective-permute-start | bytes 196616 | tf_op jit(solution)/shard_map/ppermute | solution.py:249
  62.6 10.5 %collective-permute-start.7 = (bf16[128,512]{1,0:T(8,128)(2,1)S(1)}, bf16[128,512]{1,0:T(8,128)(2,1)S(1)}, u32[]{:S(2)}, u32[]{:S(2)}) collective-permute-start(bf16[128,512]{1,0:T(8,128)(2,1)S(1)} %get-tuple-element.43), channel_id=1, source_target_pairs={{1,2},{3,4},{5,6},{7,8},{9,10},{11,12},{13,14},{15,16},{17,18},{19... | collective-permute-start | bytes 393224 | tf_op jit(solution)/shard_map/ppermute | solution.py:249
  65.9 7.1 %collective-permute-start.8 = (bf16[128,256]{1,0:T(8,128)(2,1)S(1)}, bf16[128,256]{1,0:T(8,128)(2,1)S(1)}, u32[]{:S(2)}, u32[]{:S(2)}) collective-permute-start(bf16[128,256]{1,0:T(8,128)(2,1)S(1)} %get-tuple-element.44), channel_id=1, source_target_pairs={{1,4},{3,6},{5,8},{7,10},{9,12},{11,14},{13,16},{15,18},{17,20},{1... | collective-permute-start | bytes 196616 | tf_op jit(solution)/shard_map/ppermute | solution.py:249

commit v4 on v3

--- a/solution.py
+++ b/solution.py
@@ -62,50 +62,53 @@
     )(block, lists)
 
 
-def build_body(band_ref, nodes_ref, matrix_ref, scale_ref, out_ref, ids, mats, hot, left):
-    cells, entries = nodes_ref.shape
+def build_body(band_ref, packed_ref, out_ref, hot, left):
     half, full = out_ref.shape
-    ids[...] = jnp.full(ids.shape, -1, jnp.int32)
-    ids[:, 0:entries] = nodes_ref[...]
-    mats[...] = jnp.zeros(mats.shape, F32)
-    matrix = matrix_ref[...].astype(F32)
-    mats[0:entries, 0:entries] = matrix
-    mats[CELL_PAD : CELL_PAD + entries, CELL_PAD : CELL_PAD + entries] = matrix
-    pair_matrix = mats[...].T.astype(BF16)
+    cells = left.shape[1] // CELL_PAD
     first = band_ref[0] * half
-    lane = lax.broadcasted_iota(jnp.int32, (1, 2 * CELL_PAD), 1)
+    matrix = packed_ref[cells : cells + CELL_PAD, :].T
+    nothing = jnp.zeros((CELL_PAD, CELL_PAD), F32)
+    pair_matrix = jnp.concatenate(
+        [jnp.concatenate([matrix, nothing], axis=1), jnp.concatenate([nothing, matrix], axis=1)], axis=0
+    ).astype(BF16)
     for pair in range(cells // 2):
-        rows = [ids[c : c + 1, :] for c in (2 * pair, 2 * pair + 1)]
-        row = jnp.concatenate(rows, axis=1)
+        both = (2 * pair, 2 * pair + 1)
+        row = jnp.concatenate([packed_ref[c : c + 1, :] for c in both], axis=1).astype(jnp.int32)
+        at = cells + CELL_PAD
+        gain = [jnp.broadcast_to(packed_ref[at : at + 1, c : c + 1], (1, CELL_PAD)) for c in both]
         cols = slice(pair * 2 * CELL_PAD, (pair + 1) * 2 * CELL_PAD)
-        gain = jnp.where(lane < CELL_PAD, scale_ref[2 * pair], scale_ref[2 * pair + 1])
-        left[:, cols] = (nn(one_hot(half, row - first), pair_matrix) * gain).astype(BF16)
+        product = nn(one_hot(half, row - first), pair_matrix)
+        left[:, cols] = (product * jnp.concatenate(gain, axis=1)).astype(BF16)
         hot[:, cols] = one_hot(full, row)
     for at in range(0, half, 256):
         out_ref[at : at + 256, :] = nt(left[at : at + 256, :], hot[...]).astype(BF16)
 
 
 def build(band, cell_nodes, cell_matrix, cell_scale, full):
-    cells = cell_nodes.shape[0]
+    cells, nodes = cell_nodes.shape
     half = full // 2
     entries = cells * CELL_PAD
+    spare = CELL_PAD - nodes
+    packed = jnp.concatenate(
+        [
+            jnp.pad(cell_nodes.astype(F32), ((0, 0), (0, spare)), constant_values=-8192.0),
+            jnp.pad(cell_matrix.astype(F32), ((0, spare), (0, spare))),
+            jnp.pad(cell_scale[None], ((0, 7), (0, CELL_PAD - cells))),
+        ],
+        axis=0,
+    )
     return pl.pallas_call(
         build_body,
         out_shape=jax.ShapeDtypeStruct((half, full), BF16),
-        in_specs=[spec(pltpu.SMEM), spec(), spec(), spec(pltpu.SMEM)],
+        in_specs=[spec(pltpu.SMEM), spec()],
         out_specs=spec(),
-        scratch_shapes=[
-            pltpu.VMEM((cells, CELL_PAD), jnp.int32),
-            pltpu.VMEM((2 * CELL_PAD, 2 * CELL_PAD), F32),
-            pltpu.VMEM((full, entries), BF16),
-            pltpu.VMEM((half, entries), BF16),
-        ],
+        scratch_shapes=[pltpu.VMEM((full, entries), BF16), pltpu.VMEM((half, entries), BF16)],
         compiler_params=pltpu.CompilerParams(vmem_limit_bytes=44 * MIB),
         cost_estimate=pl.CostEstimate(
             flops=2 * half * entries * full, bytes_accessed=2 * half * full, transcendentals=0
         ),
         name="build",
-    )(band, cell_nodes, cell_matrix, cell_scale)
+    )(band, packed)
 
 
 def decode(codes_ref):
@@ -118,7 +121,7 @@
     return rows, [columns[:, 0:1], columns[:, 1:2]]
 
 
-def assemble(partial_ref, ghost_ref, got_ref, lists, from_left_ref, from_right_ref, own):
+def assemble(band_ref, partial_ref, ghost_ref, got_ref, lists, from_left_ref, from_right_ref, own):
     slots = lists.shape[1]
     (left_rows, left_cols), (right_rows, right_cols) = decode(from_left_ref), decode(from_right_ref)
     ghost = ghost_ref[...]
@@ -126,6 +129,10 @@
     states = ghost.shape[0]
     got_left, got_right = got_ref[0:states, :], got_ref[states : 2 * states, :]
     near_left, near_right = got_left[:, 0:slots], got_right[:, 0:slots]
+    far_left, far_right = (
+        jnp.where(band_ref[1 + side] == 1, got[:, 2 * slots : 3 * slots], jnp.zeros((states, slots), BF16))
+        for side, got in ((0, got_left), (1, got_right))
+    )
     whole_own = (
         partial_ref[...]
         + nt(near_left, one_hot(own, lists[0:1]))
@@ -133,12 +140,12 @@
     )
     whole_left = (
         got_left[:, slots : 2 * slots].astype(F32)
-        + nn(got_left[:, 2 * slots : 3 * slots], pair_mask(left_cols[0], left_rows[1]))
+        + nn(far_left, pair_mask(left_cols[0], left_rows[1]))
         + nn(ghost_left, pair_mask(left_cols[1], left_rows[1]))
     )
     whole_right = (
         got_right[:, slots : 2 * slots].astype(F32)
-        + nn(got_right[:, 2 * slots : 3 * slots], pair_mask(right_cols[1], right_rows[0]))
+        + nn(far_right, pair_mask(right_cols[1], right_rows[0]))
         + nn(ghost_right, pair_mask(right_cols[0], right_rows[0]))
     )
     return whole_own, whole_left, whole_right
@@ -191,7 +198,7 @@
     x_out, *outs = refs[11:] if chebyshev else refs[10:]
     lists = lists_ref[...]
     own = partial_ref.shape[1]
-    new_states(older_ref, x_out, assemble(partial_ref, ghost_ref, got_ref, lists, fl_ref, fr_ref, own))
+    new_states(older_ref, x_out, assemble(band_ref, partial_ref, ghost_ref, got_ref, lists, fl_ref, fr_ref, own))
     apply_body(band_ref, x_out, mine_ref, other_ref, potential_ref, lists, *outs)
 
 
@@ -203,7 +210,7 @@
     own = partial_ref.shape[1]
     states = partial_ref.shape[0]
     slots = lists.shape[1]
-    new_states(older_ref, x_all, assemble(partial_ref, ghost_ref, got_ref, lists, fl_ref, fr_ref, own))
+    new_states(older_ref, x_all, assemble(band_ref, partial_ref, ghost_ref, got_ref, lists, fl_ref, fr_ref, own))
     pot[...] = potential_ref[...]
     half = own // 2
     mine = pl.ds(pl.multiple_of(band_ref[0] * half, 128), half)
@@ -249,9 +256,17 @@
     return lax.ppermute(x, BOTH, pairs)
 
 
-def exchange(near, far):
-    got = jnp.concatenate([across(near, 1), across(far, 2)], axis=1)
-    return lax.all_gather(got, "band", axis=0, tiled=True)
+def far_groups(parts):
+    pairs = [[2 * d + 1, 2 * d + 4] for d in range(parts - 2)]
+    return pairs + [[0, 2], [2 * parts - 3, 2 * parts - 1]]
+
+
+def exchange(band, near, far):
+    rows = far.shape[0]
+    near = across(near, 1)
+    both = lax.all_gather(far, BOTH, axis_index_groups=far_groups(lax.axis_size("dom")), axis=0, tiled=True)
+    far = lax.dynamic_slice_in_dim(both, band * rows, rows, 0)
+    return lax.all_gather(jnp.concatenate([near, far], axis=1), "band", axis=0, tiled=True)
 
 
 def group_lists():
@@ -388,7 +403,8 @@
     full = own + 2 * slots
     states_here = block.shape[0]
     states = 2 * states_here
-    band = lax.axis_index("band").astype(jnp.int32).reshape(1)
+    core, part = lax.axis_index("band"), lax.axis_index("dom")
+    band = jnp.stack([core, part >= 2, part < lax.axis_size("dom") - 2]).astype(jnp.int32)
     potential = potential.reshape(1, own)
 
     to_left, to_right = send_first(block, lists)
@@ -406,15 +422,15 @@
     fixed = (band, mine, other, potential, lists)
     ends = fixed + (from_left, from_right)
     partial, ghost, near, far = stage_call(first_body, fixed + (x0,), shapes, "apply_one")
-    got = exchange(near, far)
+    got = exchange(core, near, far)
     x1, partial, ghost, near, far = stage_call(
         lambda *r: next_body(False, *r), ends + (partial, ghost, got), (x_shape,) + shapes, "apply_two"
     )
-    got = exchange(near, far)
+    got = exchange(core, near, far)
     x2, partial, ghost, near, far = stage_call(
         lambda *r: next_body(True, *r), ends + (partial, ghost, got, x0), (x_shape,) + shapes, "apply_three"
     )
-    got = exchange(near, far)
+    got = exchange(core, near, far)
     own_part, sums = stage_call(
         last_body,
         ends + (partial, ghost, got, x1),

time: 146 us -> 149 us (1.021)
  blocking collectives: 73.2 us -> 91.1 us
  starting transfers between devices: 33.7 us -> 20.8 us
  waiting for transfers between devices: 8.73 us -> 0.02 us
  Pallas kernels: 26.2 us -> 32.8 us
  other arithmetic: 0.11 us -> 2.34 us
  local copies, waits for them, and re-layouts: 2.17 us -> 0.06 us
    all_gather x3 -> x6, blocking collectives: 6.44 us -> 25.4 us  [the longest x3 19 us: exchange(): lax.all_gather(far, BOTH, axis_index_groups=far_groups(lax.axis_size('dom...]
    ppermute x6 -> x3, starting transfers between devices: 22.3 us -> 9.49 us  [across(): return lax.ppermute(x, BOTH, pairs)]
    ppermute x6 -> x3, waiting for transfers between devices: 8.72 us -> 0.01 us  [across(): return lax.ppermute(x, BOTH, pairs)]
    pallas_call x4, Pallas kernels: 6.14 us -> 12.8 us  [stage_call(): pl.pallas_call(body, out_shape=tuple(shapes), in_specs=[spec(pltpu.SMEM)]...]
    unnamed x12 -> x6, local copies, waits for them, and re-layouts: 2.14 us -> 0.02 us
  transfers between devices with their start and end apart: 9 -> 6, of which waited for: 3 -> 0; matrix products, arithmetic and copies ran while one was open for 0% -> 2% of each run, Pallas kernels for 9% -> 8%
where the time goes in v4:
time: 149 us; the launch traced here: 148 us
  blocking collectives  91.1 us (61%)
  Pallas kernels  32.8 us (22%)
  starting transfers between devices  20.8 us (14%)
  other arithmetic  2.34 us (2%)
    all_to_all x3, blocking collectives, swap_pieces(): return lax.all_to_all(x, BOTH, 0, 0, axis_index_groups=groups, tiled=True)  61.4 us
    all_gather x3, blocking collectives, exchange(): lax.all_gather(far, BOTH, axis_index_groups=far_groups(lax.axis_size('dom...  19 us
    pallas_call x4, Pallas kernels, stage_call(): pl.pallas_call(body, out_shape=tuple(shapes), in_specs=[spec(pltpu.SMEM)]...  12.8 us
    pallas_call x1, Pallas kernels, build(): pl.pallas_call(build_body, out_shape=jax.ShapeDtypeStruct((half, full), B...  12.3 us
    ppermute x3, starting transfers between devices, across(): return lax.ppermute(x, BOTH, pairs)  9.49 us
    all_gather x3, blocking collectives, exchange(): lax.all_gather(jnp.concatenate([near, far], axis=1), 'band', axis=0, tile...  6.44 us
    ppermute x1, starting transfers between devices, shards(): other = lax.ppermute(mine, 'band', [(0, 1), (1, 0)])  6.05 us
    pallas_call x1, Pallas kernels, finish(): pl.pallas_call(lambda *refs: finish_body(scale, *refs), out_shape=(jax.Sh...  5.86 us
  transfers between devices with their start and end apart: 6, of which 0 were waited for; matrix products, arithmetic and copies ran while one was open for 2% of the time, Pallas kernels for 8%

profile of v4, /device:TPU:1, one launch (start us, length us, event | category | flops | bytes accessed | tf_op | source)
XLA Modules:
  0.0 148.1 jit_solution(15573889085856184604)
XLA Ops:
  0.6 1.8 %send_first.1 = (bf16[80,256]{1,0:T(8,128)(2,1)}, bf16[80,256]{1,0:T(8,128)(2,1)}) custom-call(bf16[64,1024]{1,0:T(8,128)(2,1)} %block_ref.1, s32[2,256]{1,0:T(2,128)} %bitcast.14), custom_call_target="tpu_custom_call" | custom-call | tf_op jit(solution)/shard_map/send_first/pallas_call | solution.py:56
  2.5 4.0 %collective-permute-start = (bf16[80,256]{1,0:T(8,128)(2,1)}, bf16[80,256]{1,0:T(8,128)(2,1)S(1)}, u32[]{:S(2)}, u32[]{:S(2)}) collective-permute-start(bf16[80,256]{1,0:T(8,128)(2,1)} %get-tuple-element.28), channel_id=1, source_target_pairs={{0,2},{2,4},{4,6},{6,8},{8,10},{10,12},{12,14},{14,16},{16,18},{18... | collective-permute-start | bytes 122888 | tf_op jit(solution)/shard_map/ppermute | solution.py:249
  6.5 1.3 collective-permute-start.1
  7.8 0.8 pad_convert_fusion
  8.6 0.7 convert_element_type.4
  9.3 0.1 pad_add_fusion.band_ref.r_0_
  9.4 0.7 select_maximum_fusion.packed_ref
  10.0 0.0 copy-start.2
  10.0 0.0 copy-start
  10.1 0.0 copy-start.1
  10.1 12.3 %build.1.mine_ref.r_1_ = bf16[768,1536]{1,0:T(8,128)(2,1)S(1)} custom-call(s32[3]{0:T(128)S(1)} %pad_add_fusion.band_ref.r_0_, f32[168,128]{1,0:T(8,128)S(1)} %select_maximum_fusion.packed_ref), custom_call_target="tpu_custom_call" | custom-call | flops 9663676416 | bytes 2359296 | tf_op jit(solution)/shard_map/build/pallas_call | solution.py:100
  22.4 0.0 collective-permute-done.r_5_.fl_ref
  22.4 0.0 collective-permute-done.1.r_6_.fr_ref
  22.4 6.0 %collective-permute-start.2 = (bf16[768,1536]{1,0:T(8,128)(2,1)S(1)}, bf16[768,1536]{1,0:T(8,128)(2,1)}, u32[]{:S(2)}, u32[]{:S(2)}) collective-permute-start(bf16[768,1536]{1,0:T(8,128)(2,1)S(1)} %build.1.mine_ref.r_1_), channel_id=1, source_target_pairs={{0,1},{1,0},{2,3},{3,2},{4,5},{5,4},{6,7},{7,6},{8,9},{9,8},{10,11... | collective-permute-start | bytes 7077896 | tf_op jit(solution)/shard_map/ppermute | solution.py:416
  28.5 0.0 copy-done.2
  28.5 4.4 %all_gather.21.x_ref.r_10_ = bf16[128,1536]{1,0:T(8,128)(2,1)S(1)} all-gather(bf16[64,1536]{1,0:T(8,128)(2,1)S(1)} %pad_maximum_fusion), channel_id=1, replica_groups=mesh['dom'=256,'band'=2] {'band'}, dimensions={0}, use_global_device_ids=true | all-gather | bytes 589824 | tf_op jit(solution)/shard_map/all_gather | solution.py:418
  32.9 0.0 collective-permute-done.2.other_ref.r_2_
  32.9 0.0 copy-done
  32.9 0.0 copy-done.1
  32.9 2.6 %apply_one.1 = (f32[128,1024]{1,0:T(8,128)S(1)}, bf16[128,512]{1,0:T(8,128)(2,1)S(1)}, bf16[128,512]{1,0:T(8,128)(2,1)S(1)}, bf16[128,256]{1,0:T(8,128)(2,1)S(1)}) custom-call(s32[3]{0:T(128)S(1)} %pad_add_fusion.band_ref.r_0_, bf16[768,1536]{1,0:T(8,128)(2,1)S(1)} %build.1.mine_ref.r_1_, bf16[768,1536]{1,0:T(8,128)(2,1)} %collective-permute-done.2.other_ref.r_2_, ...), custom_call_target="tpu_custom_call" | custom-call | tf_op jit(solution)/shard_map/apply_one/pallas_call | solution.py:236
  35.4 4.5 %collective-permute-start.3 = (bf16[128,512]{1,0:T(8,128)(2,1)S(1)}, bf16[128,512]{1,0:T(8,128)(2,1)S(1)}, u32[]{:S(2)}, u32[]{:S(2)}) collective-permute-start(bf16[128,512]{1,0:T(8,128)(2,1)S(1)} %get-tuple-element.35), channel_id=1, source_target_pairs={{1,2},{3,4},{5,6},{7,8},{9,10},{11,12},{13,14},{15,16},{17,18},{19... | collective-permute-start | bytes 393224 | tf_op jit(solution)/shard_map/ppermute | solution.py:256
  40.0 5.9 %all_gather.22 = bf16[256,256]{1,0:T(8,128)(2,1)S(1)} all-gather(bf16[128,256]{1,0:T(8,128)(2,1)S(1)} %get-tuple-element.36), channel_id=1, replica_groups={{1,4},{3,6},{5,8},{7,10},{9,12},{11,14},{13,16},{15,18},{17,20},{19,22}..., dimensions={0}, use_global_device_ids=true | all-gather | bytes 196608 | tf_op jit(solution)/shard_map/all_gather | solution.py:267
  45.8 0.0 collective-permute-done.3
  45.9 2.3 %all_gather.23.r_9_ = bf16[256,768]{1,0:T(8,128)(2,1)S(1)} all-gather(bf16[128,768]{1,0:T(8,128)(2,1)S(1)} %pad_maximum_fusion.1), channel_id=1, replica_groups=mesh['dom'=256,'band'=2] {'band'}, dimensions={0}, use_global_device_ids=true | all-gather | bytes 589824 | tf_op jit(solution)/shard_map/all_gather | solution.py:269
  48.1 3.3 %apply_two.1 = (bf16[128,1536]{1,0:T(8,128)(2,1)S(1)}, f32[128,1024]{1,0:T(8,128)S(1)}, bf16[128,512]{1,0:T(8,128)(2,1)S(1)}, bf16[128,512]{1,0:T(8,128)(2,1)S(1)}, bf16[128,256]{1,0:T(8,128)(2,1)S(1)}) custom-call(s32[3]{0:T(128)S(1)} %pad_add_fusion.band_ref.r_0_, bf16[768,1536]{1,0:T(8,128)(2,1)S(1)} %build.1.mine_ref.r_1_, ...), custom_call_target="tpu_custom_call" | custom-call | tf_op jit(solution)/shard_map/apply_two/pallas_call | solution.py:236
  51.4 2.1 %collective-permute-start.4 = (bf16[128,512]{1,0:T(8,128)(2,1)S(1)}, bf16[128,512]{1,0:T(8,128)(2,1)S(1)}, u32[]{:S(2)}, u32[]{:S(2)}) collective-permute-start(bf16[128,512]{1,0:T(8,128)(2,1)S(1)} %get-tuple-element.39), channel_id=1, source_target_pairs={{1,2},{3,4},{5,6},{7,8},{9,10},{11,12},{13,14},{15,16},{17,18},{19... | collective-permute-start | bytes 393224 | tf_op jit(solution)/shard_map/ppermute | solution.py:256
  53.5 6.5 %all_gather.24 = bf16[256,256]{1,0:T(8,128)(2,1)S(1)} all-gather(bf16[128,256]{1,0:T(8,128)(2,1)S(1)} %get-tuple-element.40), channel_id=1, replica_groups={{1,4},{3,6},{5,8},{7,10},{9,12},{11,14},{13,16},{15,18},{17,20},{19,22}..., dimensions={0}, use_global_device_ids=true | all-gather | bytes 196608 | tf_op jit(solution)/shard_map/all_gather | solution.py:267
  60.0 0.0 collective-permute-done.4
  60.1 2.1 %all_gather.25.r_9_ = bf16[256,768]{1,0:T(8,128)(2,1)S(1)} all-gather(bf16[128,768]{1,0:T(8,128)(2,1)S(1)} %pad_maximum_fusion.2), channel_id=1, replica_groups=mesh['dom'=256,'band'=2] {'band'}, dimensions={0}, use_global_device_ids=true | all-gather | bytes 589824 | tf_op jit(solution)/shard_map/all_gather | solution.py:269
  62.2 3.9 %apply_three.1 = (bf16[128,1536]{1,0:T(8,128)(2,1)}, f32[128,1024]{1,0:T(8,128)S(1)}, bf16[128,512]{1,0:T(8,128)(2,1)S(1)}, bf16[128,512]{1,0:T(8,128)(2,1)S(1)}, bf16[128,256]{1,0:T(8,128)(2,1)S(1)}) custom-call(s32[3]{0:T(128)S(1)} %pad_add_fusion.band_ref.r_0_, bf16[768,1536]{1,0:T(8,128)(2,1)S(1)} %build.1.mine_ref.r_1_, ...), custom_call_target="tpu_custom_call" | custom-call | tf_op jit(solution)/shard_map/apply_three/pallas_call | solution.py:236
  66.1 2.9 %collective-permute-start.5 = (bf16[128,512]{1,0:T(8,128)(2,1)S(1)}, bf16[128,512]{1,0:T(8,128)(2,1)S(1)}, u32[]{:S(2)}, u32[]{:S(2)}) collective-permute-start(bf16[128,512]{1,0:T(8,128)(2,1)S(1)} %get-tuple-element.43), channel_id=1, source_target_pairs={{1,2},{3,4},{5,6},{7,8},{9,10},{11,12},{13,14},{15,16},{17,18},{19... | collective-permute-start | bytes 393224 | tf_op jit(solution)/shard_map/ppermute | solution.py:256
  68.9 6.6 %all_gather.26 = bf16[256,256]{1,0:T(8,128)(2,1)S(1)} all-gather(bf16[128,256]{1,0:T(8,128)(2,1)S(1)} %get-tuple-element.44), channel_id=1, replica_groups={{1,4},{3,6},{5,8},{7,10},{9,12},{11,14},{13,16},{15,18},{17,20},{19,22}..., dimensions={0}, use_global_device_ids=true | all-gather | bytes 196608 | tf_op jit(solution)/shard_map/all_gather | solution.py:267
  75.5 0.0 collective-permute-done.5
  75.6 2.1 %all_gather.27.got_ref = bf16[256,768]{1,0:T(8,128)(2,1)S(1)} all-gather(bf16[128,768]{1,0:T(8,128)(2,1)S(1)} %pad_maximum_fusion.3), channel_id=1, replica_groups=mesh['dom'=256,'band'=2] {'band'}, dimensions={0}, use_global_device_ids=true | all-gather | bytes 589824 | tf_op jit(solution)/shard_map/all_gather | solution.py:269
  77.6 3.1 %apply_four.1 = (bf16[128,512]{1,0:T(8,128)(2,1)S(1)}, f32[256,128]{1,0:T(8,128)S(1)}) custom-call(s32[3]{0:T(128)S(1)} %pad_add_fusion.band_ref.r_0_, bf16[768,1536]{1,0:T(8,128)(2,1)S(1)} %build.1.mine_ref.r_1_, bf16[768,1536]{1,0:T(8,128)(2,1)} %collective-permute-done.2.other_ref.r_2_, f32[1,1024]{1,0:T(1,128)S(1)} %bitcast.13, s32[2,256]{1,0:T(2,128)S(1)} %bitcast.18, ...), custom_call_target="tpu_custom_call" | custom-call | tf_op jit(solution)/shard_map/apply_four/pallas_call | solution.py:236
  80.7 31.8 %all_to_all.23 = f32[32,8,128]{2,1,0:T(8,128)S(1)} all-to-all(f32[32,8,128]{2,1,0:T(8,128)S(1)} %bitcast.9), channel_id=1, replica_groups={{0,1,2,3,4,5,6,7,128,129,130,131,132,133,134,135,256,257,258,259,260,26..., dimensions={0} | all-to-all | bytes 262144 | tf_op jit(solution)/shard_map/all_to_all | solution.py:285
  112.5 16.8 %all_to_all.24 = f32[16,8,128]{2,1,0:T(8,128)S(1)} all-to-all(f32[16,8,128]{2,1,0:T(8,128)S(1)} %broadcast_in_dim.7), channel_id=1, replica_groups={{0,8,16,24,32,40,48,56,64,72,80,88,96,104,112,120},{1,9,17,25,33,41,49,..., dimensions={0} | all-to-all | bytes 131072 | tf_op jit(solution)/shard_map/all_to_all | solution.py:285
  129.3 12.8 %all_to_all.25 = f32[32,8,128]{2,1,0:T(8,128)S(1)} all-to-all(f32[32,8,128]{2,1,0:T(8,128)S(1)} %broadcast_in_dim.8), channel_id=1, replica_groups={{0,1,2,3,4,5,6,7,128,129,130,131,132,133,134,135,256,257,258,259,260,26..., dimensions={0} | all-to-all | bytes 262144 | tf_op jit(solution)/shard_map/all_to_all | solution.py:285
  142.2 5.9 %finish.1 = (f32[128,512]{1,0:T(8,128)}, f32[128,128]{1,0:T(8,128)}) custom-call(f32[256,128]{1,0:T(8,128)S(1)} %bitcast.8, bf16[128,512]{1,0:T(8,128)(2,1)S(1)} %get-tuple-element.47.refs_1_), custom_call_target="tpu_custom_call" | custom-call | tf_op jit(solution)/shard_map/finish/pallas_call | solution.py:389
  (13 shorter events, 0.2 us)
Async XLA Ops:
  2.5 19.9 %collective-permute-start = (bf16[80,256]{1,0:T(8,128)(2,1)}, bf16[80,256]{1,0:T(8,128)(2,1)S(1)}, u32[]{:S(2)}, u32[]{:S(2)}) collective-permute-start(bf16[80,256]{1,0:T(8,128)(2,1)} %get-tuple-element.28), channel_id=1, source_target_pairs={{0,2},{2,4},{4,6},{6,8},{8,10},{10,12},{12,14},{14,16},{16,18},{18... | collective-permute-start | bytes 122888 | tf_op jit(solution)/shard_map/ppermute | solution.py:249
  6.5 15.9 %collective-permute-start.1 = (bf16[80,256]{1,0:T(8,128)(2,1)}, bf16[80,256]{1,0:T(8,128)(2,1)S(1)}, u32[]{:S(2)}, u32[]{:S(2)}) collective-permute-start(bf16[80,256]{1,0:T(8,128)(2,1)} %get-tuple-element.29), channel_id=1, source_target_pairs={{2,0},{4,2},{6,4},{8,6},{10,8},{12,10},{14,12},{16,14},{18,16},{20... | collective-permute-start | bytes 122888 | tf_op jit(solution)/shard_map/ppermute | solution.py:249
  10.0 18.4 %copy-start.2 = (bf16[64,1024]{1,0:T(8,128)(2,1)S(1)}, bf16[64,1024]{1,0:T(8,128)(2,1)}, u32[]{:S(2)}) copy-start(bf16[64,1024]{1,0:T(8,128)(2,1)} %block_ref.1) | copy-start | bytes 393220
  10.0 22.8 %copy-start = (f32[1024]{0:T(1024)S(1)}, f32[1024]{0:T(1024)}, u32[]{:S(2)}) copy-start(f32[1024]{0:T(1024)} %param.11) | copy-start | bytes 12292
  10.1 22.8 %copy-start.1 = (s32[1,2,256]{2,1,0:T(2,128)S(1)}, s32[1,2,256]{2,1,0:T(2,128)}, u32[]{:S(2)}) copy-start(s32[1,2,256]{2,1,0:T(2,128)} %param.8) | copy-start | bytes 6148
  22.4 10.5 %collective-permute-start.2 = (bf16[768,1536]{1,0:T(8,128)(2,1)S(1)}, bf16[768,1536]{1,0:T(8,128)(2,1)}, u32[]{:S(2)}, u32[]{:S(2)}) collective-permute-start(bf16[768,1536]{1,0:T(8,128)(2,1)S(1)} %build.1.mine_ref.r_1_), channel_id=1, source_target_pairs={{0,1},{1,0},{2,3},{3,2},{4,5},{5,4},{6,7},{7,6},{8,9},{9,8},{10,11... | collective-permute-start | bytes 7077896 | tf_op jit(solution)/shard_map/ppermute | solution.py:416
  35.4 10.4 %collective-permute-start.3 = (bf16[128,512]{1,0:T(8,128)(2,1)S(1)}, bf16[128,512]{1,0:T(8,128)(2,1)S(1)}, u32[]{:S(2)}, u32[]{:S(2)}) collective-permute-start(bf16[128,512]{1,0:T(8,128)(2,1)S(1)} %get-tuple-element.35), channel_id=1, source_target_pairs={{1,2},{3,4},{5,6},{7,8},{9,10},{11,12},{13,14},{15,16},{17,18},{19... | collective-permute-start | bytes 393224 | tf_op jit(solution)/shard_map/ppermute | solution.py:256
  51.4 8.6 %collective-permute-start.4 = (bf16[128,512]{1,0:T(8,128)(2,1)S(1)}, bf16[128,512]{1,0:T(8,128)(2,1)S(1)}, u32[]{:S(2)}, u32[]{:S(2)}) collective-permute-start(bf16[128,512]{1,0:T(8,128)(2,1)S(1)} %get-tuple-element.39), channel_id=1, source_target_pairs={{1,2},{3,4},{5,6},{7,8},{9,10},{11,12},{13,14},{15,16},{17,18},{19... | collective-permute-start | bytes 393224 | tf_op jit(solution)/shard_map/ppermute | solution.py:256
  66.1 9.5 %collective-permute-start.5 = (bf16[128,512]{1,0:T(8,128)(2,1)S(1)}, bf16[128,512]{1,0:T(8,128)(2,1)S(1)}, u32[]{:S(2)}, u32[]{:S(2)}) collective-permute-start(bf16[128,512]{1,0:T(8,128)(2,1)S(1)} %get-tuple-element.43), channel_id=1, source_target_pairs={{1,2},{3,4},{5,6},{7,8},{9,10},{11,12},{13,14},{15,16},{17,18},{19... | collective-permute-start | bytes 393224 | tf_op jit(solution)/shard_map/ppermute | solution.py:256

commit v5 on v4

--- a/solution.py
+++ b/solution.py
@@ -103,7 +103,7 @@
         in_specs=[spec(pltpu.SMEM), spec()],
         out_specs=spec(),
         scratch_shapes=[pltpu.VMEM((full, entries), BF16), pltpu.VMEM((half, entries), BF16)],
-        compiler_params=pltpu.CompilerParams(vmem_limit_bytes=44 * MIB),
+        compiler_params=pltpu.CompilerParams(vmem_limit_bytes=26 * MIB),
         cost_estimate=pl.CostEstimate(
             flops=2 * half * entries * full, bytes_accessed=2 * half * full, transcendentals=0
         ),
@@ -151,19 +151,22 @@
     return whole_own, whole_left, whole_right
 
 
+def times_half(which, x_ref, w_ref, cols):
+    half = w_ref.shape[0]
+    return nn(x_ref[:, pl.ds(pl.multiple_of(which * half, 128), half)], w_ref[:, cols])
+
+
 def times_operator(band, x_ref, mine_ref, other_ref, cols):
-    half = mine_ref.shape[0]
-    here = pl.ds(pl.multiple_of(band * half, 128), half)
-    there = pl.ds(pl.multiple_of((1 - band) * half, 128), half)
-    return nn(x_ref[:, here], mine_ref[:, cols]) + nn(x_ref[:, there], other_ref[:, cols])
-
-
-def apply_body(
-    band_ref, x_ref, mine_ref, other_ref, potential_ref, lists, partial_out, ghost_out, near_out, far_out
-):
+    return times_half(band, x_ref, mine_ref, cols) + times_half(1 - band, x_ref, other_ref, cols)
+
+
+def apply_body(band_ref, x_ref, mine_ref, other_ref, *refs):
+    give(band_ref, times_operator(band_ref[0], x_ref, mine_ref, other_ref, slice(None)), x_ref, *refs)
+
+
+def give(band_ref, result, x_ref, potential_ref, lists, partial_out, ghost_out, near_out, far_out):
     own = partial_out.shape[1]
     slots = lists.shape[1]
-    result = times_operator(band_ref[0], x_ref, mine_ref, other_ref, slice(None))
     partial = result[:, 0:own] + potential_ref[...] * x_ref[:, 0:own].astype(F32)
     partial_out[...] = partial
     ghost = result[:, own:].astype(BF16)
@@ -176,8 +179,16 @@
     far_out[...] = edge
 
 
-def first_body(band_ref, mine_ref, other_ref, potential_ref, lists_ref, x_ref, *outs):
-    apply_body(band_ref, x_ref, mine_ref, other_ref, potential_ref, lists_ref[...], *outs)
+def first_body(
+    band_ref, mine_ref, other_hbm, potential_ref, lists_ref, x_ref, other_out, partial_out, ghost_out, near_out,
+    far_out, sem,
+):
+    arrival = pltpu.make_async_copy(other_hbm, other_out, sem)
+    arrival.start()
+    result = times_half(band_ref[0], x_ref, mine_ref, slice(None))
+    arrival.wait()
+    result = result + times_half(1 - band_ref[0], x_ref, other_out, slice(None))
+    give(band_ref, result, x_ref, potential_ref, lists_ref[...], partial_out, ghost_out, near_out, far_out)
 
 
 def new_states(older_ref, x_out, pieces):
@@ -232,14 +243,14 @@
     )
 
 
-def stage_call(body, args, shapes, name, scratch=()):
+def stage_call(body, args, shapes, name, scratch=(), anywhere=()):
     return pl.pallas_call(
         body,
         out_shape=tuple(shapes),
-        in_specs=[spec(pltpu.SMEM)] + [spec()] * (len(args) - 1),
+        in_specs=[spec(pltpu.SMEM)] + [spec(pl.ANY if i in anywhere else pltpu.VMEM) for i in range(1, len(args))],
         out_specs=tuple(spec() for _ in shapes),
         scratch_shapes=list(scratch),
-        compiler_params=pltpu.CompilerParams(vmem_limit_bytes=32 * MIB),
+        compiler_params=pltpu.CompilerParams(vmem_limit_bytes=16 * MIB),
         name=name,
     )(*args)
 
@@ -392,7 +403,7 @@
         in_specs=[spec()] * 2,
         out_specs=(spec(), spec()),
         scratch_shapes=[pltpu.VMEM((states, states), F32)],
-        compiler_params=pltpu.CompilerParams(vmem_limit_bytes=32 * MIB),
+        compiler_params=pltpu.CompilerParams(vmem_limit_bytes=16 * MIB),
         name="finish",
     )(total, own_part)
 
@@ -421,7 +432,12 @@
     x_shape = jax.ShapeDtypeStruct((states, full), BF16)
     fixed = (band, mine, other, potential, lists)
     ends = fixed + (from_left, from_right)
-    partial, ghost, near, far = stage_call(first_body, fixed + (x0,), shapes, "apply_one")
+    other_shape = jax.ShapeDtypeStruct(other.shape, other.dtype)
+    other, partial, ghost, near, far = stage_call(
+        first_body, fixed + (x0,), (other_shape,) + shapes, "apply_one", (pltpu.SemaphoreType.DMA,), (2,)
+    )
+    fixed = (band, mine, other, potential, lists)
+    ends = fixed + (from_left, from_right)
     got = exchange(core, near, far)
     x1, partial, ghost, near, far = stage_call(
         lambda *r: next_body(False, *r), ends + (partial, ghost, got), (x_shape,) + shapes, "apply_two"

time: 149 us -> 146 us (0.980)
  Pallas kernels: 32.8 us -> 29.9 us
    pallas_call x4, Pallas kernels: 12.8 us -> 9.95 us  [stage_call(): pl.pallas_call(body, out_shape=tuple(shapes), in_specs=[spec(pltpu.SMEM)]...]
where the time goes in v5:
time: 146 us; the launch traced here: 145 us
  blocking collectives  91.1 us (62%)
  Pallas kernels  29.9 us (20%)
  starting transfers between devices  20.9 us (14%)
  other arithmetic  2.34 us (2%)
    all_to_all x3, blocking collectives, swap_pieces(): return lax.all_to_all(x, BOTH, 0, 0, axis_index_groups=groups, tiled=True)  61.4 us
    all_gather x3, blocking collectives, exchange(): lax.all_gather(far, BOTH, axis_index_groups=far_groups(lax.axis_size('dom...  19 us
    pallas_call x1, Pallas kernels, build(): pl.pallas_call(build_body, out_shape=jax.ShapeDtypeStruct((half, full), B...  12.3 us
    pallas_call x4, Pallas kernels, stage_call(): pl.pallas_call(body, out_shape=tuple(shapes), in_specs=[spec(pltpu.SMEM)]...  9.95 us
    ppermute x3, starting transfers between devices, across(): return lax.ppermute(x, BOTH, pairs)  9.51 us
    all_gather x3, blocking collectives, exchange(): lax.all_gather(jnp.concatenate([near, far], axis=1), 'band', axis=0, tile...  6.44 us
    ppermute x1, starting transfers between devices, shards(): other = lax.ppermute(mine, 'band', [(0, 1), (1, 0)])  6.05 us
    pallas_call x1, Pallas kernels, finish(): pl.pallas_call(lambda *refs: finish_body(scale, *refs), out_shape=(jax.Sh...  5.86 us
  transfers between devices with their start and end apart: 6, of which 0 were waited for; matrix products, arithmetic and copies ran while one was open for 2% of the time, Pallas kernels for 8%

profile of v5, /device:TPU:1, one launch (start us, length us, event | category | flops | bytes accessed | tf_op | source)
XLA Modules:
  0.0 145.2 jit_solution(14596597285182786993)
XLA Ops:
  0.6 1.8 %send_first.1 = (bf16[80,256]{1,0:T(8,128)(2,1)}, bf16[80,256]{1,0:T(8,128)(2,1)}) custom-call(bf16[64,1024]{1,0:T(8,128)(2,1)} %block_ref.1, s32[2,256]{1,0:T(2,128)} %bitcast.14), custom_call_target="tpu_custom_call" | custom-call | tf_op jit(solution)/shard_map/send_first/pallas_call | solution.py:56
  2.5 4.0 %collective-permute-start = (bf16[80,256]{1,0:T(8,128)(2,1)}, bf16[80,256]{1,0:T(8,128)(2,1)S(1)}, u32[]{:S(2)}, u32[]{:S(2)}) collective-permute-start(bf16[80,256]{1,0:T(8,128)(2,1)} %get-tuple-element.29), channel_id=1, source_target_pairs={{0,2},{2,4},{4,6},{6,8},{8,10},{10,12},{12,14},{14,16},{16,18},{18... | collective-permute-start | bytes 122888 | tf_op jit(solution)/shard_map/ppermute | solution.py:260
  6.5 1.3 collective-permute-start.1
  7.8 0.8 pad_convert_fusion
  8.6 0.7 convert_element_type.4
  9.3 0.1 pad_add_fusion.band_ref.r_0_
  9.4 0.7 select_maximum_fusion.packed_ref
  10.0 0.0 copy-start.2
  10.0 0.0 copy-start
  10.1 0.0 copy-start.1
  10.1 12.3 %build.1.mine_ref.r_1_ = bf16[768,1536]{1,0:T(8,128)(2,1)S(1)} custom-call(s32[3]{0:T(128)S(1)} %pad_add_fusion.band_ref.r_0_, f32[168,128]{1,0:T(8,128)S(1)} %select_maximum_fusion.packed_ref), custom_call_target="tpu_custom_call" | custom-call | flops 9663676416 | bytes 2359296 | tf_op jit(solution)/shard_map/build/pallas_call | solution.py:100
  22.4 0.0 collective-permute-done.r_5_.fl_ref
  22.4 0.0 collective-permute-done.1.r_6_.fr_ref
  22.4 6.0 %collective-permute-start.2 = (bf16[768,1536]{1,0:T(8,128)(2,1)S(1)}, bf16[768,1536]{1,0:T(8,128)(2,1)}, u32[]{:S(2)}, u32[]{:S(2)}) collective-permute-start(bf16[768,1536]{1,0:T(8,128)(2,1)S(1)} %build.1.mine_ref.r_1_), channel_id=1, source_target_pairs={{0,1},{1,0},{2,3},{3,2},{4,5},{5,4},{6,7},{7,6},{8,9},{9,8},{10,11... | collective-permute-start | bytes 7077896 | tf_op jit(solution)/shard_map/ppermute | solution.py:427
  28.5 0.0 copy-done.2
  28.5 4.4 %all_gather.21.x_ref.r_10_ = bf16[128,1536]{1,0:T(8,128)(2,1)S(1)} all-gather(bf16[64,1536]{1,0:T(8,128)(2,1)S(1)} %pad_maximum_fusion), channel_id=1, replica_groups=mesh['dom'=256,'band'=2] {'band'}, dimensions={0}, use_global_device_ids=true | all-gather | bytes 589824 | tf_op jit(solution)/shard_map/all_gather | solution.py:429
  32.9 0.0 collective-permute-done.2.other_hbm
  32.9 0.0 copy-done
  32.9 0.0 copy-done.1
  32.9 3.1 %apply_one.1 = (bf16[768,1536]{1,0:T(8,128)(2,1)S(1)}, f32[128,1024]{1,0:T(8,128)S(1)}, bf16[128,512]{1,0:T(8,128)(2,1)S(1)}, bf16[128,512]{1,0:T(8,128)(2,1)S(1)}, bf16[128,256]{1,0:T(8,128)(2,1)S(1)}) custom-call(s32[3]{0:T(128)S(1)} %pad_add_fusion.band_ref.r_0_, bf16[768,1536]{1,0:T(8,128)(2,1)S(1)} %build.1.mine_ref.r_1_, ...), custom_call_target="tpu_custom_call" | custom-call | tf_op jit(solution)/shard_map/apply_one/pallas_call | solution.py:247
  36.0 4.5 %collective-permute-start.3 = (bf16[128,512]{1,0:T(8,128)(2,1)S(1)}, bf16[128,512]{1,0:T(8,128)(2,1)S(1)}, u32[]{:S(2)}, u32[]{:S(2)}) collective-permute-start(bf16[128,512]{1,0:T(8,128)(2,1)S(1)} %get-tuple-element.37), channel_id=1, source_target_pairs={{1,2},{3,4},{5,6},{7,8},{9,10},{11,12},{13,14},{15,16},{17,18},{19... | collective-permute-start | bytes 393224 | tf_op jit(solution)/shard_map/ppermute | solution.py:267
  40.5 5.9 %all_gather.22 = bf16[256,256]{1,0:T(8,128)(2,1)S(1)} all-gather(bf16[128,256]{1,0:T(8,128)(2,1)S(1)} %get-tuple-element.38), channel_id=1, replica_groups={{1,4},{3,6},{5,8},{7,10},{9,12},{11,14},{13,16},{15,18},{17,20},{19,22}..., dimensions={0}, use_global_device_ids=true | all-gather | bytes 196608 | tf_op jit(solution)/shard_map/all_gather | solution.py:278
  46.4 0.0 collective-permute-done.3
  46.4 2.3 %all_gather.23.r_9_ = bf16[256,768]{1,0:T(8,128)(2,1)S(1)} all-gather(bf16[128,768]{1,0:T(8,128)(2,1)S(1)} %pad_maximum_fusion.1), channel_id=1, replica_groups=mesh['dom'=256,'band'=2] {'band'}, dimensions={0}, use_global_device_ids=true | all-gather | bytes 589824 | tf_op jit(solution)/shard_map/all_gather | solution.py:280
  48.7 2.1 %apply_two.1 = (bf16[128,1536]{1,0:T(8,128)(2,1)S(1)}, f32[128,1024]{1,0:T(8,128)S(1)}, bf16[128,512]{1,0:T(8,128)(2,1)S(1)}, bf16[128,512]{1,0:T(8,128)(2,1)S(1)}, bf16[128,256]{1,0:T(8,128)(2,1)S(1)}) custom-call(s32[3]{0:T(128)S(1)} %pad_add_fusion.band_ref.r_0_, bf16[768,1536]{1,0:T(8,128)(2,1)S(1)} %build.1.mine_ref.r_1_, ...), custom_call_target="tpu_custom_call" | custom-call | tf_op jit(solution)/shard_map/apply_two/pallas_call | solution.py:247
  50.8 2.1 %collective-permute-start.4 = (bf16[128,512]{1,0:T(8,128)(2,1)S(1)}, bf16[128,512]{1,0:T(8,128)(2,1)S(1)}, u32[]{:S(2)}, u32[]{:S(2)}) collective-permute-start(bf16[128,512]{1,0:T(8,128)(2,1)S(1)} %get-tuple-element.41), channel_id=1, source_target_pairs={{1,2},{3,4},{5,6},{7,8},{9,10},{11,12},{13,14},{15,16},{17,18},{19... | collective-permute-start | bytes 393224 | tf_op jit(solution)/shard_map/ppermute | solution.py:267
  53.0 6.5 %all_gather.24 = bf16[256,256]{1,0:T(8,128)(2,1)S(1)} all-gather(bf16[128,256]{1,0:T(8,128)(2,1)S(1)} %get-tuple-element.42), channel_id=1, replica_groups={{1,4},{3,6},{5,8},{7,10},{9,12},{11,14},{13,16},{15,18},{17,20},{19,22}..., dimensions={0}, use_global_device_ids=true | all-gather | bytes 196608 | tf_op jit(solution)/shard_map/all_gather | solution.py:278
  59.5 0.0 collective-permute-done.4
  59.5 2.1 %all_gather.25.r_9_ = bf16[256,768]{1,0:T(8,128)(2,1)S(1)} all-gather(bf16[128,768]{1,0:T(8,128)(2,1)S(1)} %pad_maximum_fusion.2), channel_id=1, replica_groups=mesh['dom'=256,'band'=2] {'band'}, dimensions={0}, use_global_device_ids=true | all-gather | bytes 589824 | tf_op jit(solution)/shard_map/all_gather | solution.py:280
  61.6 2.8 %apply_three.1 = (bf16[128,1536]{1,0:T(8,128)(2,1)}, f32[128,1024]{1,0:T(8,128)S(1)}, bf16[128,512]{1,0:T(8,128)(2,1)S(1)}, bf16[128,512]{1,0:T(8,128)(2,1)S(1)}, bf16[128,256]{1,0:T(8,128)(2,1)S(1)}) custom-call(s32[3]{0:T(128)S(1)} %pad_add_fusion.band_ref.r_0_, bf16[768,1536]{1,0:T(8,128)(2,1)S(1)} %build.1.mine_ref.r_1_, ...), custom_call_target="tpu_custom_call" | custom-call | tf_op jit(solution)/shard_map/apply_three/pallas_call | solution.py:247
  64.4 2.9 %collective-permute-start.5 = (bf16[128,512]{1,0:T(8,128)(2,1)S(1)}, bf16[128,512]{1,0:T(8,128)(2,1)S(1)}, u32[]{:S(2)}, u32[]{:S(2)}) collective-permute-start(bf16[128,512]{1,0:T(8,128)(2,1)S(1)} %get-tuple-element.45), channel_id=1, source_target_pairs={{1,2},{3,4},{5,6},{7,8},{9,10},{11,12},{13,14},{15,16},{17,18},{19... | collective-permute-start | bytes 393224 | tf_op jit(solution)/shard_map/ppermute | solution.py:267
  67.2 6.6 %all_gather.26 = bf16[256,256]{1,0:T(8,128)(2,1)S(1)} all-gather(bf16[128,256]{1,0:T(8,128)(2,1)S(1)} %get-tuple-element.46), channel_id=1, replica_groups={{1,4},{3,6},{5,8},{7,10},{9,12},{11,14},{13,16},{15,18},{17,20},{19,22}..., dimensions={0}, use_global_device_ids=true | all-gather | bytes 196608 | tf_op jit(solution)/shard_map/all_gather | solution.py:278
  73.8 0.0 collective-permute-done.5
  73.8 2.1 %all_gather.27.got_ref = bf16[256,768]{1,0:T(8,128)(2,1)S(1)} all-gather(bf16[128,768]{1,0:T(8,128)(2,1)S(1)} %pad_maximum_fusion.3), channel_id=1, replica_groups=mesh['dom'=256,'band'=2] {'band'}, dimensions={0}, use_global_device_ids=true | all-gather | bytes 589824 | tf_op jit(solution)/shard_map/all_gather | solution.py:280
  75.9 2.0 %apply_four.1 = (bf16[128,512]{1,0:T(8,128)(2,1)S(1)}, f32[256,128]{1,0:T(8,128)S(1)}) custom-call(s32[3]{0:T(128)S(1)} %pad_add_fusion.band_ref.r_0_, bf16[768,1536]{1,0:T(8,128)(2,1)S(1)} %build.1.mine_ref.r_1_, bf16[768,1536]{1,0:T(8,128)(2,1)S(1)} %get-tuple-element.34.r_2_.other_ref, f32[1,1024]{1,0:T(1,128)S(1)} %bitcast.13, s32[2,256]{1,0:T(2,128)S(1)} %bitcast.18, ...), custom_call_target="tpu_custom_call" | custom-call | tf_op jit(solution)/shard_map/apply_four/pallas_call | solution.py:247
  77.9 31.8 %all_to_all.23 = f32[32,8,128]{2,1,0:T(8,128)S(1)} all-to-all(f32[32,8,128]{2,1,0:T(8,128)S(1)} %bitcast.9), channel_id=1, replica_groups={{0,1,2,3,4,5,6,7,128,129,130,131,132,133,134,135,256,257,258,259,260,26..., dimensions={0} | all-to-all | bytes 262144 | tf_op jit(solution)/shard_map/all_to_all | solution.py:296
  109.7 16.8 %all_to_all.24 = f32[16,8,128]{2,1,0:T(8,128)S(1)} all-to-all(f32[16,8,128]{2,1,0:T(8,128)S(1)} %broadcast_in_dim.7), channel_id=1, replica_groups={{0,8,16,24,32,40,48,56,64,72,80,88,96,104,112,120},{1,9,17,25,33,41,49,..., dimensions={0} | all-to-all | bytes 131072 | tf_op jit(solution)/shard_map/all_to_all | solution.py:296
  126.5 12.8 %all_to_all.25 = f32[32,8,128]{2,1,0:T(8,128)S(1)} all-to-all(f32[32,8,128]{2,1,0:T(8,128)S(1)} %broadcast_in_dim.8), channel_id=1, replica_groups={{0,1,2,3,4,5,6,7,128,129,130,131,132,133,134,135,256,257,258,259,260,26..., dimensions={0} | all-to-all | bytes 262144 | tf_op jit(solution)/shard_map/all_to_all | solution.py:296
  139.3 5.9 %finish.1 = (f32[128,512]{1,0:T(8,128)}, f32[128,128]{1,0:T(8,128)}) custom-call(f32[256,128]{1,0:T(8,128)S(1)} %bitcast.8, bf16[128,512]{1,0:T(8,128)(2,1)S(1)} %get-tuple-element.49.refs_1_), custom_call_target="tpu_custom_call" | custom-call | tf_op jit(solution)/shard_map/finish/pallas_call | solution.py:400
  (13 shorter events, 0.2 us)
Async XLA Ops:
  2.5 19.9 %collective-permute-start = (bf16[80,256]{1,0:T(8,128)(2,1)}, bf16[80,256]{1,0:T(8,128)(2,1)S(1)}, u32[]{:S(2)}, u32[]{:S(2)}) collective-permute-start(bf16[80,256]{1,0:T(8,128)(2,1)} %get-tuple-element.29), channel_id=1, source_target_pairs={{0,2},{2,4},{4,6},{6,8},{8,10},{10,12},{12,14},{14,16},{16,18},{18... | collective-permute-start | bytes 122888 | tf_op jit(solution)/shard_map/ppermute | solution.py:260
  6.5 15.9 %collective-permute-start.1 = (bf16[80,256]{1,0:T(8,128)(2,1)}, bf16[80,256]{1,0:T(8,128)(2,1)S(1)}, u32[]{:S(2)}, u32[]{:S(2)}) collective-permute-start(bf16[80,256]{1,0:T(8,128)(2,1)} %get-tuple-element.30), channel_id=1, source_target_pairs={{2,0},{4,2},{6,4},{8,6},{10,8},{12,10},{14,12},{16,14},{18,16},{20... | collective-permute-start | bytes 122888 | tf_op jit(solution)/shard_map/ppermute | solution.py:260
  10.0 18.4 %copy-start.2 = (bf16[64,1024]{1,0:T(8,128)(2,1)S(1)}, bf16[64,1024]{1,0:T(8,128)(2,1)}, u32[]{:S(2)}) copy-start(bf16[64,1024]{1,0:T(8,128)(2,1)} %block_ref.1) | copy-start | bytes 393220
  10.0 22.8 %copy-start = (f32[1024]{0:T(1024)S(1)}, f32[1024]{0:T(1024)}, u32[]{:S(2)}) copy-start(f32[1024]{0:T(1024)} %param.11) | copy-start | bytes 12292
  10.1 22.8 %copy-start.1 = (s32[1,2,256]{2,1,0:T(2,128)S(1)}, s32[1,2,256]{2,1,0:T(2,128)}, u32[]{:S(2)}) copy-start(s32[1,2,256]{2,1,0:T(2,128)} %param.8) | copy-start | bytes 6148
  22.4 10.5 %collective-permute-start.2 = (bf16[768,1536]{1,0:T(8,128)(2,1)S(1)}, bf16[768,1536]{1,0:T(8,128)(2,1)}, u32[]{:S(2)}, u32[]{:S(2)}) collective-permute-start(bf16[768,1536]{1,0:T(8,128)(2,1)S(1)} %build.1.mine_ref.r_1_), channel_id=1, source_target_pairs={{0,1},{1,0},{2,3},{3,2},{4,5},{5,4},{6,7},{7,6},{8,9},{9,8},{10,11... | collective-permute-start | bytes 7077896 | tf_op jit(solution)/shard_map/ppermute | solution.py:427
  36.0 10.4 %collective-permute-start.3 = (bf16[128,512]{1,0:T(8,128)(2,1)S(1)}, bf16[128,512]{1,0:T(8,128)(2,1)S(1)}, u32[]{:S(2)}, u32[]{:S(2)}) collective-permute-start(bf16[128,512]{1,0:T(8,128)(2,1)S(1)} %get-tuple-element.37), channel_id=1, source_target_pairs={{1,2},{3,4},{5,6},{7,8},{9,10},{11,12},{13,14},{15,16},{17,18},{19... | collective-permute-start | bytes 393224 | tf_op jit(solution)/shard_map/ppermute | solution.py:267
  50.8 8.6 %collective-permute-start.4 = (bf16[128,512]{1,0:T(8,128)(2,1)S(1)}, bf16[128,512]{1,0:T(8,128)(2,1)S(1)}, u32[]{:S(2)}, u32[]{:S(2)}) collective-permute-start(bf16[128,512]{1,0:T(8,128)(2,1)S(1)} %get-tuple-element.41), channel_id=1, source_target_pairs={{1,2},{3,4},{5,6},{7,8},{9,10},{11,12},{13,14},{15,16},{17,18},{19... | collective-permute-start | bytes 393224 | tf_op jit(solution)/shard_map/ppermute | solution.py:267
  64.4 9.4 %collective-permute-start.5 = (bf16[128,512]{1,0:T(8,128)(2,1)S(1)}, bf16[128,512]{1,0:T(8,128)(2,1)S(1)}, u32[]{:S(2)}, u32[]{:S(2)}) collective-permute-start(bf16[128,512]{1,0:T(8,128)(2,1)S(1)} %get-tuple-element.45), channel_id=1, source_target_pairs={{1,2},{3,4},{5,6},{7,8},{9,10},{11,12},{13,14},{15,16},{17,18},{19... | collective-permute-start | bytes 393224 | tf_op jit(solution)/shard_map/ppermute | solution.py:267

commit v6 on v5

--- a/solution.py
+++ b/solution.py
@@ -129,10 +129,7 @@
     states = ghost.shape[0]
     got_left, got_right = got_ref[0:states, :], got_ref[states : 2 * states, :]
     near_left, near_right = got_left[:, 0:slots], got_right[:, 0:slots]
-    far_left, far_right = (
-        jnp.where(band_ref[1 + side] == 1, got[:, 2 * slots : 3 * slots], jnp.zeros((states, slots), BF16))
-        for side, got in ((0, got_left), (1, got_right))
-    )
+    gone_left, gone_right = ((1 - band_ref[1 + side]).astype(F32) * 4096.0 for side in (0, 1))
     whole_own = (
         partial_ref[...]
         + nt(near_left, one_hot(own, lists[0:1]))
@@ -140,12 +137,12 @@
     )
     whole_left = (
         got_left[:, slots : 2 * slots].astype(F32)
-        + nn(far_left, pair_mask(left_cols[0], left_rows[1]))
+        + nn(got_left[:, 2 * slots : 3 * slots], pair_mask(left_cols[0] + gone_left, left_rows[1]))
         + nn(ghost_left, pair_mask(left_cols[1], left_rows[1]))
     )
     whole_right = (
         got_right[:, slots : 2 * slots].astype(F32)
-        + nn(far_right, pair_mask(right_cols[1], right_rows[0]))
+        + nn(got_right[:, 2 * slots : 3 * slots], pair_mask(right_cols[1] + gone_right, right_rows[0]))
         + nn(ghost_right, pair_mask(right_cols[0], right_rows[0]))
     )
     return whole_own, whole_left, whole_right
@@ -183,10 +180,16 @@
     band_ref, mine_ref, other_hbm, potential_ref, lists_ref, x_ref, other_out, partial_out, ghost_out, near_out,
     far_out, sem,
 ):
-    arrival = pltpu.make_async_copy(other_hbm, other_out, sem)
-    arrival.start()
+    piece = other_out.shape[0] // 4
+    arrivals = [
+        pltpu.make_async_copy(other_hbm.at[i * piece : (i + 1) * piece], other_out.at[i * piece : (i + 1) * piece], sem.at[i])
+        for i in range(4)
+    ]
+    for arrival in arrivals:
+        arrival.start()
     result = times_half(band_ref[0], x_ref, mine_ref, slice(None))
-    arrival.wait()
+    for arrival in arrivals:
+        arrival.wait()
     result = result + times_half(1 - band_ref[0], x_ref, other_out, slice(None))
     give(band_ref, result, x_ref, potential_ref, lists_ref[...], partial_out, ghost_out, near_out, far_out)
 
@@ -434,7 +437,7 @@
     ends = fixed + (from_left, from_right)
     other_shape = jax.ShapeDtypeStruct(other.shape, other.dtype)
     other, partial, ghost, near, far = stage_call(
-        first_body, fixed + (x0,), (other_shape,) + shapes, "apply_one", (pltpu.SemaphoreType.DMA,), (2,)
+        first_body, fixed + (x0,), (other_shape,) + shapes, "apply_one", (pltpu.SemaphoreType.DMA((4,)),), (2,)
     )
     fixed = (band, mine, other, potential, lists)
     ends = fixed + (from_left, from_right)

time: 146 us -> 146 us (level)
  no operation moved by 1% of the time
where the time goes in v6:
time: 146 us; the launch traced here: 145 us
  blocking collectives  91.1 us (62%)
  Pallas kernels  29.9 us (20%)
  starting transfers between devices  20.9 us (14%)
  other arithmetic  2.34 us (2%)
    all_to_all x3, blocking collectives, swap_pieces(): return lax.all_to_all(x, BOTH, 0, 0, axis_index_groups=groups, tiled=True)  61.4 us
    all_gather x3, blocking collectives, exchange(): lax.all_gather(far, BOTH, axis_index_groups=far_groups(lax.axis_size('dom...  19 us
    pallas_call x1, Pallas kernels, build(): pl.pallas_call(build_body, out_shape=jax.ShapeDtypeStruct((half, full), B...  12.3 us
    pallas_call x4, Pallas kernels, stage_call(): pl.pallas_call(body, out_shape=tuple(shapes), in_specs=[spec(pltpu.SMEM)]...  9.89 us
    ppermute x3, starting transfers between devices, across(): return lax.ppermute(x, BOTH, pairs)  9.51 us
    all_gather x3, blocking collectives, exchange(): lax.all_gather(jnp.concatenate([near, far], axis=1), 'band', axis=0, tile...  6.44 us
    ppermute x1, starting transfers between devices, shards(): other = lax.ppermute(mine, 'band', [(0, 1), (1, 0)])  6.05 us
    pallas_call x1, Pallas kernels, finish(): pl.pallas_call(lambda *refs: finish_body(scale, *refs), out_shape=(jax.Sh...  5.85 us
  transfers between devices with their start and end apart: 6, of which 0 were waited for; matrix products, arithmetic and copies ran while one was open for 2% of the time, Pallas kernels for 8%

profile of v6, /device:TPU:1, one launch (start us, length us, event | category | flops | bytes accessed | tf_op | source)
XLA Modules:
  0.0 145.1 jit_solution(17403210680029584599)
XLA Ops:
  0.6 1.8 %send_first.1 = (bf16[80,256]{1,0:T(8,128)(2,1)}, bf16[80,256]{1,0:T(8,128)(2,1)}) custom-call(bf16[64,1024]{1,0:T(8,128)(2,1)} %block_ref.1, s32[2,256]{1,0:T(2,128)} %bitcast.14), custom_call_target="tpu_custom_call" | custom-call | tf_op jit(solution)/shard_map/send_first/pallas_call | solution.py:56
  2.5 4.0 %collective-permute-start = (bf16[80,256]{1,0:T(8,128)(2,1)}, bf16[80,256]{1,0:T(8,128)(2,1)S(1)}, u32[]{:S(2)}, u32[]{:S(2)}) collective-permute-start(bf16[80,256]{1,0:T(8,128)(2,1)} %get-tuple-element.29), channel_id=1, source_target_pairs={{0,2},{2,4},{4,6},{6,8},{8,10},{10,12},{12,14},{14,16},{16,18},{18... | collective-permute-start | bytes 122888 | tf_op jit(solution)/shard_map/ppermute | solution.py:263
  6.5 1.3 collective-permute-start.1
  7.8 0.8 pad_convert_fusion
  8.6 0.7 convert_element_type.4
  9.3 0.1 pad_add_fusion.band_ref.r_0_
  9.4 0.7 select_maximum_fusion.packed_ref
  10.0 0.0 copy-start.2
  10.0 0.0 copy-start
  10.1 0.0 copy-start.1
  10.1 12.3 %build.1.mine_ref.r_1_ = bf16[768,1536]{1,0:T(8,128)(2,1)S(1)} custom-call(s32[3]{0:T(128)S(1)} %pad_add_fusion.band_ref.r_0_, f32[168,128]{1,0:T(8,128)S(1)} %select_maximum_fusion.packed_ref), custom_call_target="tpu_custom_call" | custom-call | flops 9663676416 | bytes 2359296 | tf_op jit(solution)/shard_map/build/pallas_call | solution.py:100
  22.4 0.0 collective-permute-done.r_5_.fl_ref
  22.4 0.0 collective-permute-done.1.r_6_.fr_ref
  22.4 6.0 %collective-permute-start.2 = (bf16[768,1536]{1,0:T(8,128)(2,1)S(1)}, bf16[768,1536]{1,0:T(8,128)(2,1)}, u32[]{:S(2)}, u32[]{:S(2)}) collective-permute-start(bf16[768,1536]{1,0:T(8,128)(2,1)S(1)} %build.1.mine_ref.r_1_), channel_id=1, source_target_pairs={{0,1},{1,0},{2,3},{3,2},{4,5},{5,4},{6,7},{7,6},{8,9},{9,8},{10,11... | collective-permute-start | bytes 7077896 | tf_op jit(solution)/shard_map/ppermute | solution.py:430
  28.5 0.0 copy-done.2
  28.5 4.4 %all_gather.21.x_ref.r_10_ = bf16[128,1536]{1,0:T(8,128)(2,1)S(1)} all-gather(bf16[64,1536]{1,0:T(8,128)(2,1)S(1)} %pad_maximum_fusion), channel_id=1, replica_groups=mesh['dom'=256,'band'=2] {'band'}, dimensions={0}, use_global_device_ids=true | all-gather | bytes 589824 | tf_op jit(solution)/shard_map/all_gather | solution.py:432
  32.9 0.0 collective-permute-done.2.other_hbm
  32.9 0.0 copy-done
  32.9 0.0 copy-done.1
  32.9 3.1 %apply_one.1 = (bf16[768,1536]{1,0:T(8,128)(2,1)S(1)}, f32[128,1024]{1,0:T(8,128)S(1)}, bf16[128,512]{1,0:T(8,128)(2,1)S(1)}, bf16[128,512]{1,0:T(8,128)(2,1)S(1)}, bf16[128,256]{1,0:T(8,128)(2,1)S(1)}) custom-call(s32[3]{0:T(128)S(1)} %pad_add_fusion.band_ref.r_0_, bf16[768,1536]{1,0:T(8,128)(2,1)S(1)} %build.1.mine_ref.r_1_, ...), custom_call_target="tpu_custom_call" | custom-call | tf_op jit(solution)/shard_map/apply_one/pallas_call | solution.py:250
  35.9 4.5 %collective-permute-start.3 = (bf16[128,512]{1,0:T(8,128)(2,1)S(1)}, bf16[128,512]{1,0:T(8,128)(2,1)S(1)}, u32[]{:S(2)}, u32[]{:S(2)}) collective-permute-start(bf16[128,512]{1,0:T(8,128)(2,1)S(1)} %get-tuple-element.37), channel_id=1, source_target_pairs={{1,2},{3,4},{5,6},{7,8},{9,10},{11,12},{13,14},{15,16},{17,18},{19... | collective-permute-start | bytes 393224 | tf_op jit(solution)/shard_map/ppermute | solution.py:270
  40.5 5.9 %all_gather.22 = bf16[256,256]{1,0:T(8,128)(2,1)S(1)} all-gather(bf16[128,256]{1,0:T(8,128)(2,1)S(1)} %get-tuple-element.38), channel_id=1, replica_groups={{1,4},{3,6},{5,8},{7,10},{9,12},{11,14},{13,16},{15,18},{17,20},{19,22}..., dimensions={0}, use_global_device_ids=true | all-gather | bytes 196608 | tf_op jit(solution)/shard_map/all_gather | solution.py:281
  46.4 0.0 collective-permute-done.3
  46.4 2.3 %all_gather.23.r_9_ = bf16[256,768]{1,0:T(8,128)(2,1)S(1)} all-gather(bf16[128,768]{1,0:T(8,128)(2,1)S(1)} %pad_maximum_fusion.1), channel_id=1, replica_groups=mesh['dom'=256,'band'=2] {'band'}, dimensions={0}, use_global_device_ids=true | all-gather | bytes 589824 | tf_op jit(solution)/shard_map/all_gather | solution.py:283
  48.7 2.1 %apply_two.1 = (bf16[128,1536]{1,0:T(8,128)(2,1)S(1)}, f32[128,1024]{1,0:T(8,128)S(1)}, bf16[128,512]{1,0:T(8,128)(2,1)S(1)}, bf16[128,512]{1,0:T(8,128)(2,1)S(1)}, bf16[128,256]{1,0:T(8,128)(2,1)S(1)}) custom-call(s32[3]{0:T(128)S(1)} %pad_add_fusion.band_ref.r_0_, bf16[768,1536]{1,0:T(8,128)(2,1)S(1)} %build.1.mine_ref.r_1_, ...), custom_call_target="tpu_custom_call" | custom-call | tf_op jit(solution)/shard_map/apply_two/pallas_call | solution.py:250
  50.8 2.1 %collective-permute-start.4 = (bf16[128,512]{1,0:T(8,128)(2,1)S(1)}, bf16[128,512]{1,0:T(8,128)(2,1)S(1)}, u32[]{:S(2)}, u32[]{:S(2)}) collective-permute-start(bf16[128,512]{1,0:T(8,128)(2,1)S(1)} %get-tuple-element.41), channel_id=1, source_target_pairs={{1,2},{3,4},{5,6},{7,8},{9,10},{11,12},{13,14},{15,16},{17,18},{19... | collective-permute-start | bytes 393224 | tf_op jit(solution)/shard_map/ppermute | solution.py:270
  52.9 6.5 %all_gather.24 = bf16[256,256]{1,0:T(8,128)(2,1)S(1)} all-gather(bf16[128,256]{1,0:T(8,128)(2,1)S(1)} %get-tuple-element.42), channel_id=1, replica_groups={{1,4},{3,6},{5,8},{7,10},{9,12},{11,14},{13,16},{15,18},{17,20},{19,22}..., dimensions={0}, use_global_device_ids=true | all-gather | bytes 196608 | tf_op jit(solution)/shard_map/all_gather | solution.py:281
  59.4 0.0 collective-permute-done.4
  59.5 2.1 %all_gather.25.r_9_ = bf16[256,768]{1,0:T(8,128)(2,1)S(1)} all-gather(bf16[128,768]{1,0:T(8,128)(2,1)S(1)} %pad_maximum_fusion.2), channel_id=1, replica_groups=mesh['dom'=256,'band'=2] {'band'}, dimensions={0}, use_global_device_ids=true | all-gather | bytes 589824 | tf_op jit(solution)/shard_map/all_gather | solution.py:283
  61.5 2.7 %apply_three.1 = (bf16[128,1536]{1,0:T(8,128)(2,1)}, f32[128,1024]{1,0:T(8,128)S(1)}, bf16[128,512]{1,0:T(8,128)(2,1)S(1)}, bf16[128,512]{1,0:T(8,128)(2,1)S(1)}, bf16[128,256]{1,0:T(8,128)(2,1)S(1)}) custom-call(s32[3]{0:T(128)S(1)} %pad_add_fusion.band_ref.r_0_, bf16[768,1536]{1,0:T(8,128)(2,1)S(1)} %build.1.mine_ref.r_1_, ...), custom_call_target="tpu_custom_call" | custom-call | tf_op jit(solution)/shard_map/apply_three/pallas_call | solution.py:250
  64.3 2.9 %collective-permute-start.5 = (bf16[128,512]{1,0:T(8,128)(2,1)S(1)}, bf16[128,512]{1,0:T(8,128)(2,1)S(1)}, u32[]{:S(2)}, u32[]{:S(2)}) collective-permute-start(bf16[128,512]{1,0:T(8,128)(2,1)S(1)} %get-tuple-element.45), channel_id=1, source_target_pairs={{1,2},{3,4},{5,6},{7,8},{9,10},{11,12},{13,14},{15,16},{17,18},{19... | collective-permute-start | bytes 393224 | tf_op jit(solution)/shard_map/ppermute | solution.py:270
  67.2 6.6 %all_gather.26 = bf16[256,256]{1,0:T(8,128)(2,1)S(1)} all-gather(bf16[128,256]{1,0:T(8,128)(2,1)S(1)} %get-tuple-element.46), channel_id=1, replica_groups={{1,4},{3,6},{5,8},{7,10},{9,12},{11,14},{13,16},{15,18},{17,20},{19,22}..., dimensions={0}, use_global_device_ids=true | all-gather | bytes 196608 | tf_op jit(solution)/shard_map/all_gather | solution.py:281
  73.7 0.0 collective-permute-done.5
  73.8 2.1 %all_gather.27.got_ref = bf16[256,768]{1,0:T(8,128)(2,1)S(1)} all-gather(bf16[128,768]{1,0:T(8,128)(2,1)S(1)} %pad_maximum_fusion.3), channel_id=1, replica_groups=mesh['dom'=256,'band'=2] {'band'}, dimensions={0}, use_global_device_ids=true | all-gather | bytes 589824 | tf_op jit(solution)/shard_map/all_gather | solution.py:283
  75.9 2.0 %apply_four.1 = (bf16[128,512]{1,0:T(8,128)(2,1)S(1)}, f32[256,128]{1,0:T(8,128)S(1)}) custom-call(s32[3]{0:T(128)S(1)} %pad_add_fusion.band_ref.r_0_, bf16[768,1536]{1,0:T(8,128)(2,1)S(1)} %build.1.mine_ref.r_1_, bf16[768,1536]{1,0:T(8,128)(2,1)S(1)} %get-tuple-element.34.r_2_.other_ref, f32[1,1024]{1,0:T(1,128)S(1)} %bitcast.13, s32[2,256]{1,0:T(2,128)S(1)} %bitcast.18, ...), custom_call_target="tpu_custom_call" | custom-call | tf_op jit(solution)/shard_map/apply_four/pallas_call | solution.py:250
  77.8 31.8 %all_to_all.23 = f32[32,8,128]{2,1,0:T(8,128)S(1)} all-to-all(f32[32,8,128]{2,1,0:T(8,128)S(1)} %bitcast.9), channel_id=1, replica_groups={{0,1,2,3,4,5,6,7,128,129,130,131,132,133,134,135,256,257,258,259,260,26..., dimensions={0} | all-to-all | bytes 262144 | tf_op jit(solution)/shard_map/all_to_all | solution.py:299
  109.6 16.8 %all_to_all.24 = f32[16,8,128]{2,1,0:T(8,128)S(1)} all-to-all(f32[16,8,128]{2,1,0:T(8,128)S(1)} %broadcast_in_dim.7), channel_id=1, replica_groups={{0,8,16,24,32,40,48,56,64,72,80,88,96,104,112,120},{1,9,17,25,33,41,49,..., dimensions={0} | all-to-all | bytes 131072 | tf_op jit(solution)/shard_map/all_to_all | solution.py:299
  126.4 12.8 %all_to_all.25 = f32[32,8,128]{2,1,0:T(8,128)S(1)} all-to-all(f32[32,8,128]{2,1,0:T(8,128)S(1)} %broadcast_in_dim.8), channel_id=1, replica_groups={{0,1,2,3,4,5,6,7,128,129,130,131,132,133,134,135,256,257,258,259,260,26..., dimensions={0} | all-to-all | bytes 262144 | tf_op jit(solution)/shard_map/all_to_all | solution.py:299
  139.3 5.9 %finish.1 = (f32[128,512]{1,0:T(8,128)}, f32[128,128]{1,0:T(8,128)}) custom-call(f32[256,128]{1,0:T(8,128)S(1)} %bitcast.8, bf16[128,512]{1,0:T(8,128)(2,1)S(1)} %get-tuple-element.49.refs_1_), custom_call_target="tpu_custom_call" | custom-call | tf_op jit(solution)/shard_map/finish/pallas_call | solution.py:403
  (13 shorter events, 0.2 us)
Async XLA Ops:
  2.5 19.9 %collective-permute-start = (bf16[80,256]{1,0:T(8,128)(2,1)}, bf16[80,256]{1,0:T(8,128)(2,1)S(1)}, u32[]{:S(2)}, u32[]{:S(2)}) collective-permute-start(bf16[80,256]{1,0:T(8,128)(2,1)} %get-tuple-element.29), channel_id=1, source_target_pairs={{0,2},{2,4},{4,6},{6,8},{8,10},{10,12},{12,14},{14,16},{16,18},{18... | collective-permute-start | bytes 122888 | tf_op jit(solution)/shard_map/ppermute | solution.py:263
  6.5 15.9 %collective-permute-start.1 = (bf16[80,256]{1,0:T(8,128)(2,1)}, bf16[80,256]{1,0:T(8,128)(2,1)S(1)}, u32[]{:S(2)}, u32[]{:S(2)}) collective-permute-start(bf16[80,256]{1,0:T(8,128)(2,1)} %get-tuple-element.30), channel_id=1, source_target_pairs={{2,0},{4,2},{6,4},{8,6},{10,8},{12,10},{14,12},{16,14},{18,16},{20... | collective-permute-start | bytes 122888 | tf_op jit(solution)/shard_map/ppermute | solution.py:263
  10.0 18.4 %copy-start.2 = (bf16[64,1024]{1,0:T(8,128)(2,1)S(1)}, bf16[64,1024]{1,0:T(8,128)(2,1)}, u32[]{:S(2)}) copy-start(bf16[64,1024]{1,0:T(8,128)(2,1)} %block_ref.1) | copy-start | bytes 393220
  10.0 22.8 %copy-start = (f32[1024]{0:T(1024)S(1)}, f32[1024]{0:T(1024)}, u32[]{:S(2)}) copy-start(f32[1024]{0:T(1024)} %param.11) | copy-start | bytes 12292
  10.1 22.8 %copy-start.1 = (s32[1,2,256]{2,1,0:T(2,128)S(1)}, s32[1,2,256]{2,1,0:T(2,128)}, u32[]{:S(2)}) copy-start(s32[1,2,256]{2,1,0:T(2,128)} %param.8) | copy-start | bytes 6148
  22.4 10.5 %collective-permute-start.2 = (bf16[768,1536]{1,0:T(8,128)(2,1)S(1)}, bf16[768,1536]{1,0:T(8,128)(2,1)}, u32[]{:S(2)}, u32[]{:S(2)}) collective-permute-start(bf16[768,1536]{1,0:T(8,128)(2,1)S(1)} %build.1.mine_ref.r_1_), channel_id=1, source_target_pairs={{0,1},{1,0},{2,3},{3,2},{4,5},{5,4},{6,7},{7,6},{8,9},{9,8},{10,11... | collective-permute-start | bytes 7077896 | tf_op jit(solution)/shard_map/ppermute | solution.py:430
  35.9 10.4 %collective-permute-start.3 = (bf16[128,512]{1,0:T(8,128)(2,1)S(1)}, bf16[128,512]{1,0:T(8,128)(2,1)S(1)}, u32[]{:S(2)}, u32[]{:S(2)}) collective-permute-start(bf16[128,512]{1,0:T(8,128)(2,1)S(1)} %get-tuple-element.37), channel_id=1, source_target_pairs={{1,2},{3,4},{5,6},{7,8},{9,10},{11,12},{13,14},{15,16},{17,18},{19... | collective-permute-start | bytes 393224 | tf_op jit(solution)/shard_map/ppermute | solution.py:270
  50.8 8.6 %collective-permute-start.4 = (bf16[128,512]{1,0:T(8,128)(2,1)S(1)}, bf16[128,512]{1,0:T(8,128)(2,1)S(1)}, u32[]{:S(2)}, u32[]{:S(2)}) collective-permute-start(bf16[128,512]{1,0:T(8,128)(2,1)S(1)} %get-tuple-element.41), channel_id=1, source_target_pairs={{1,2},{3,4},{5,6},{7,8},{9,10},{11,12},{13,14},{15,16},{17,18},{19... | collective-permute-start | bytes 393224 | tf_op jit(solution)/shard_map/ppermute | solution.py:270
  64.3 9.5 %collective-permute-start.5 = (bf16[128,512]{1,0:T(8,128)(2,1)S(1)}, bf16[128,512]{1,0:T(8,128)(2,1)S(1)}, u32[]{:S(2)}, u32[]{:S(2)}) collective-permute-start(bf16[128,512]{1,0:T(8,128)(2,1)S(1)} %get-tuple-element.45), channel_id=1, source_target_pairs={{1,2},{3,4},{5,6},{7,8},{9,10},{11,12},{13,14},{15,16},{17,18},{19... | collective-permute-start | bytes 393224 | tf_op jit(solution)/shard_map/ppermute | solution.py:270

commit v7 on v6

--- a/solution.py
+++ b/solution.py
@@ -33,16 +33,16 @@
     return (column == row).astype(F32).astype(BF16)
 
 
-def send_body(block_ref, lists_ref, left_ref, right_ref):
+def send_body(parts, part_ref, block_ref, lists_ref, left_ref, right_ref):
     own = block_ref.shape[1]
     states = block_ref.shape[0]
     lists = lists_ref[...]
     slots = lists.shape[1]
     part = lax.broadcasted_iota(jnp.int32, (16, slots), 0)
-    codes = jnp.zeros((16, slots), jnp.int32)
-    for side in (0, 1):
+    codes = jnp.where(part == 4, 1, 0)
+    for side, end in ((0, 0), (1, parts - 1)):
         one = lists[side : side + 1]
-        codes = jnp.where(part == 2 * side, one >> 5, codes)
+        codes = jnp.where(part == 2 * side, (one >> 5) + jnp.where(part_ref[0] == end, 128, 0), codes)
         codes = jnp.where(part == 2 * side + 1, one & 31, codes)
     codes = codes.astype(F32).astype(BF16)
     for side, out in ((0, left_ref), (1, right_ref)):
@@ -50,16 +50,16 @@
         out[states : states + 16, :] = codes
 
 
-def send_first(block, lists):
+def send_first(parts, part, block, lists):
     states, slots = block.shape[0], lists.shape[1]
     shape = jax.ShapeDtypeStruct((states + 16, slots), BF16)
     return pl.pallas_call(
-        send_body,
+        lambda *refs: send_body(parts, *refs),
         out_shape=(shape, shape),
-        in_specs=[spec()] * 2,
+        in_specs=[spec(pltpu.SMEM)] + [spec()] * 2,
         out_specs=(spec(), spec()),
         name="send_first",
-    )(block, lists)
+    )(part, block, lists)
 
 
 def build_body(band_ref, packed_ref, out_ref, hot, left):
@@ -117,11 +117,11 @@
     rows = [codes[2 * s : 2 * s + 1] * 32.0 + codes[2 * s + 1 : 2 * s + 2] for s in (0, 1)]
     part = lax.broadcasted_iota(jnp.int32, (8, slots), 0)
     both = jnp.where(part == 0, rows[0], rows[1])
-    columns = both.T
+    columns = both.T + (1.0 - codes[4:5, 0:1]) * 16384.0
     return rows, [columns[:, 0:1], columns[:, 1:2]]
 
 
-def assemble(band_ref, partial_ref, ghost_ref, got_ref, lists, from_left_ref, from_right_ref, own):
+def assemble(partial_ref, ghost_ref, got_ref, lists, from_left_ref, from_right_ref, own):
     slots = lists.shape[1]
     (left_rows, left_cols), (right_rows, right_cols) = decode(from_left_ref), decode(from_right_ref)
     ghost = ghost_ref[...]
@@ -129,7 +129,6 @@
     states = ghost.shape[0]
     got_left, got_right = got_ref[0:states, :], got_ref[states : 2 * states, :]
     near_left, near_right = got_left[:, 0:slots], got_right[:, 0:slots]
-    gone_left, gone_right = ((1 - band_ref[1 + side]).astype(F32) * 4096.0 for side in (0, 1))
     whole_own = (
         partial_ref[...]
         + nt(near_left, one_hot(own, lists[0:1]))
@@ -137,12 +136,12 @@
     )
     whole_left = (
         got_left[:, slots : 2 * slots].astype(F32)
-        + nn(got_left[:, 2 * slots : 3 * slots], pair_mask(left_cols[0] + gone_left, left_rows[1]))
+        + nn(got_left[:, 2 * slots : 3 * slots], pair_mask(left_cols[0], left_rows[1]))
         + nn(ghost_left, pair_mask(left_cols[1], left_rows[1]))
     )
     whole_right = (
         got_right[:, slots : 2 * slots].astype(F32)
-        + nn(got_right[:, 2 * slots : 3 * slots], pair_mask(right_cols[1] + gone_right, right_rows[0]))
+        + nn(got_right[:, 2 * slots : 3 * slots], pair_mask(right_cols[1], right_rows[0]))
         + nn(ghost_right, pair_mask(right_cols[0], right_rows[0]))
     )
     return whole_own, whole_left, whole_right
@@ -212,7 +211,7 @@
     x_out, *outs = refs[11:] if chebyshev else refs[10:]
     lists = lists_ref[...]
     own = partial_ref.shape[1]
-    new_states(older_ref, x_out, assemble(band_ref, partial_ref, ghost_ref, got_ref, lists, fl_ref, fr_ref, own))
+    new_states(older_ref, x_out, assemble(partial_ref, ghost_ref, got_ref, lists, fl_ref, fr_ref, own))
     apply_body(band_ref, x_out, mine_ref, other_ref, potential_ref, lists, *outs)
 
 
@@ -224,7 +223,7 @@
     own = partial_ref.shape[1]
     states = partial_ref.shape[0]
     slots = lists.shape[1]
-    new_states(older_ref, x_all, assemble(band_ref, partial_ref, ghost_ref, got_ref, lists, fl_ref, fr_ref, own))
+    new_states(older_ref, x_all, assemble(partial_ref, ghost_ref, got_ref, lists, fl_ref, fr_ref, own))
     pot[...] = potential_ref[...]
     half = own // 2
     mine = pl.ds(pl.multiple_of(band_ref[0] * half, 128), half)
@@ -417,11 +416,12 @@
     full = own + 2 * slots
     states_here = block.shape[0]
     states = 2 * states_here
-    core, part = lax.axis_index("band"), lax.axis_index("dom")
-    band = jnp.stack([core, part >= 2, part < lax.axis_size("dom") - 2]).astype(jnp.int32)
+    core = lax.axis_index("band")
+    band = core.astype(jnp.int32).reshape(1)
+    part = lax.axis_index("dom").astype(jnp.int32).reshape(1)
     potential = potential.reshape(1, own)
 
-    to_left, to_right = send_first(block, lists)
+    to_left, to_right = send_first(lax.axis_size("dom"), part, block, lists)
     to_left, to_right, cell_nodes = lax.optimization_barrier((to_left, to_right, cell_nodes))
     from_left = shift(to_right, "dom", 1)
     from_right = shift(to_left, "dom", -1)

time: 146 us -> 143 us (0.979)
  Pallas kernels: 29.9 us -> 27.2 us
    pallas_call x4, Pallas kernels: 9.89 us -> 7.74 us  [stage_call(): pl.pallas_call(body, out_shape=tuple(shapes), in_specs=[spec(pltpu.SMEM)]...]
where the time goes in v7:
time: 143 us; the launch traced here: 142 us
  blocking collectives  91.1 us (64%)
  Pallas kernels  27.2 us (19%)
  starting transfers between devices  20.9 us (15%)
  other arithmetic  2.26 us (2%)
    all_to_all x3, blocking collectives, swap_pieces(): return lax.all_to_all(x, BOTH, 0, 0, axis_index_groups=groups, tiled=True)  61.4 us
    all_gather x3, blocking collectives, exchange(): lax.all_gather(far, BOTH, axis_index_groups=far_groups(lax.axis_size('dom...  19 us
    pallas_call x1, Pallas kernels, build(): pl.pallas_call(build_body, out_shape=jax.ShapeDtypeStruct((half, full), B...  11.7 us
    ppermute x3, starting transfers between devices, across(): return lax.ppermute(x, BOTH, pairs)  9.5 us
    pallas_call x4, Pallas kernels, stage_call(): pl.pallas_call(body, out_shape=tuple(shapes), in_specs=[spec(pltpu.SMEM)]...  7.74 us
    all_gather x3, blocking collectives, exchange(): lax.all_gather(jnp.concatenate([near, far], axis=1), 'band', axis=0, tile...  6.44 us
    ppermute x1, starting transfers between devices, shards(): other = lax.ppermute(mine, 'band', [(0, 1), (1, 0)])  6.05 us
    pallas_call x1, Pallas kernels, finish(): pl.pallas_call(lambda *refs: finish_body(scale, *refs), out_shape=(jax.Sh...  5.86 us
  transfers between devices with their start and end apart: 6, of which 0 were waited for; matrix products, arithmetic and copies ran while one was open for 2% of the time, Pallas kernels for 8%

profile of v7, /device:TPU:1, one launch (start us, length us, event | category | flops | bytes accessed | tf_op | source)
XLA Modules:
  0.0 142.4 jit_solution(7958753015545862241)
XLA Ops:
  0.6 1.8 %send_first.1 = (bf16[80,256]{1,0:T(8,128)(2,1)}, bf16[80,256]{1,0:T(8,128)(2,1)}) custom-call(s32[1]{0:T(128)} %bitcast.1.refs_0_, bf16[64,1024]{1,0:T(8,128)(2,1)} %refs_1_.1, s32[2,256]{1,0:T(2,128)} %bitcast.13), custom_call_target="tpu_custom_call" | custom-call | tf_op jit(solution)/shard_map/send_first/pallas_call | solution.py:56
  2.5 4.0 %collective-permute-start = (bf16[80,256]{1,0:T(8,128)(2,1)}, bf16[80,256]{1,0:T(8,128)(2,1)S(1)}, u32[]{:S(2)}, u32[]{:S(2)}) collective-permute-start(bf16[80,256]{1,0:T(8,128)(2,1)} %get-tuple-element.29), channel_id=1, source_target_pairs={{0,2},{2,4},{4,6},{6,8},{8,10},{10,12},{12,14},{14,16},{16,18},{18... | collective-permute-start | bytes 122888 | tf_op jit(solution)/shard_map/ppermute | solution.py:262
  6.5 1.3 collective-permute-start.1
  7.8 0.7 convert_element_type.8
  8.5 0.8 pad_convert_fusion
  9.3 0.7 select_maximum_fusion.packed_ref
  10.0 0.0 copy-start.2
  10.0 0.0 copy-start
  10.0 0.0 copy-start.1
  10.0 11.7 %build.1.mine_ref.r_1_ = bf16[768,1536]{1,0:T(8,128)(2,1)S(1)} custom-call(s32[1]{0:T(128)} %bitcast.band_ref.r_0_, f32[168,128]{1,0:T(8,128)S(1)} %select_maximum_fusion.packed_ref), custom_call_target="tpu_custom_call" | custom-call | flops 9663676416 | bytes 2359296 | tf_op jit(solution)/shard_map/build/pallas_call | solution.py:100
  21.7 0.0 collective-permute-done.r_5_.fl_ref
  21.7 0.0 collective-permute-done.1.r_6_.fr_ref
  21.8 6.0 %collective-permute-start.2 = (bf16[768,1536]{1,0:T(8,128)(2,1)S(1)}, bf16[768,1536]{1,0:T(8,128)(2,1)}, u32[]{:S(2)}, u32[]{:S(2)}) collective-permute-start(bf16[768,1536]{1,0:T(8,128)(2,1)S(1)} %build.1.mine_ref.r_1_), channel_id=1, source_target_pairs={{0,1},{1,0},{2,3},{3,2},{4,5},{5,4},{6,7},{7,6},{8,9},{9,8},{10,11... | collective-permute-start | bytes 7077896 | tf_op jit(solution)/shard_map/ppermute | solution.py:430
  27.8 0.0 copy-done.2
  27.9 4.4 %all_gather.21.x_ref.r_10_ = bf16[128,1536]{1,0:T(8,128)(2,1)S(1)} all-gather(bf16[64,1536]{1,0:T(8,128)(2,1)S(1)} %pad_maximum_fusion), channel_id=1, replica_groups=mesh['dom'=256,'band'=2] {'band'}, dimensions={0}, use_global_device_ids=true | all-gather | bytes 589824 | tf_op jit(solution)/shard_map/all_gather | solution.py:432
  32.2 0.0 collective-permute-done.2.other_hbm
  32.2 0.0 copy-done
  32.2 0.0 copy-done.1
  32.2 2.5 %apply_one.1 = (bf16[768,1536]{1,0:T(8,128)(2,1)S(1)}, f32[128,1024]{1,0:T(8,128)S(1)}, bf16[128,512]{1,0:T(8,128)(2,1)S(1)}, bf16[128,512]{1,0:T(8,128)(2,1)S(1)}, bf16[128,256]{1,0:T(8,128)(2,1)S(1)}) custom-call(s32[1]{0:T(128)} %bitcast.band_ref.r_0_, bf16[768,1536]{1,0:T(8,128)(2,1)S(1)} %build.1.mine_ref.r_1_, ...), custom_call_target="tpu_custom_call" | custom-call | tf_op jit(solution)/shard_map/apply_one/pallas_call | solution.py:249
  34.8 4.5 %collective-permute-start.3 = (bf16[128,512]{1,0:T(8,128)(2,1)S(1)}, bf16[128,512]{1,0:T(8,128)(2,1)S(1)}, u32[]{:S(2)}, u32[]{:S(2)}) collective-permute-start(bf16[128,512]{1,0:T(8,128)(2,1)S(1)} %get-tuple-element.37), channel_id=1, source_target_pairs={{1,2},{3,4},{5,6},{7,8},{9,10},{11,12},{13,14},{15,16},{17,18},{19... | collective-permute-start | bytes 393224 | tf_op jit(solution)/shard_map/ppermute | solution.py:269
  39.3 5.9 %all_gather.22 = bf16[256,256]{1,0:T(8,128)(2,1)S(1)} all-gather(bf16[128,256]{1,0:T(8,128)(2,1)S(1)} %get-tuple-element.38), channel_id=1, replica_groups={{1,4},{3,6},{5,8},{7,10},{9,12},{11,14},{13,16},{15,18},{17,20},{19,22}..., dimensions={0}, use_global_device_ids=true | all-gather | bytes 196608 | tf_op jit(solution)/shard_map/all_gather | solution.py:280
  45.2 0.0 collective-permute-done.3
  45.2 2.3 %all_gather.23.r_9_ = bf16[256,768]{1,0:T(8,128)(2,1)S(1)} all-gather(bf16[128,768]{1,0:T(8,128)(2,1)S(1)} %pad_maximum_fusion.1), channel_id=1, replica_groups=mesh['dom'=256,'band'=2] {'band'}, dimensions={0}, use_global_device_ids=true | all-gather | bytes 589824 | tf_op jit(solution)/shard_map/all_gather | solution.py:282
  47.5 1.6 %apply_two.1 = (bf16[128,1536]{1,0:T(8,128)(2,1)S(1)}, f32[128,1024]{1,0:T(8,128)S(1)}, bf16[128,512]{1,0:T(8,128)(2,1)S(1)}, bf16[128,512]{1,0:T(8,128)(2,1)S(1)}, bf16[128,256]{1,0:T(8,128)(2,1)S(1)}) custom-call(s32[1]{0:T(128)} %bitcast.band_ref.r_0_, bf16[768,1536]{1,0:T(8,128)(2,1)S(1)} %build.1.mine_ref.r_1_, ...), custom_call_target="tpu_custom_call" | custom-call | tf_op jit(solution)/shard_map/apply_two/pallas_call | solution.py:249
  49.1 2.1 %collective-permute-start.4 = (bf16[128,512]{1,0:T(8,128)(2,1)S(1)}, bf16[128,512]{1,0:T(8,128)(2,1)S(1)}, u32[]{:S(2)}, u32[]{:S(2)}) collective-permute-start(bf16[128,512]{1,0:T(8,128)(2,1)S(1)} %get-tuple-element.41), channel_id=1, source_target_pairs={{1,2},{3,4},{5,6},{7,8},{9,10},{11,12},{13,14},{15,16},{17,18},{19... | collective-permute-start | bytes 393224 | tf_op jit(solution)/shard_map/ppermute | solution.py:269
  51.2 6.5 %all_gather.24 = bf16[256,256]{1,0:T(8,128)(2,1)S(1)} all-gather(bf16[128,256]{1,0:T(8,128)(2,1)S(1)} %get-tuple-element.42), channel_id=1, replica_groups={{1,4},{3,6},{5,8},{7,10},{9,12},{11,14},{13,16},{15,18},{17,20},{19,22}..., dimensions={0}, use_global_device_ids=true | all-gather | bytes 196608 | tf_op jit(solution)/shard_map/all_gather | solution.py:280
  57.7 0.0 collective-permute-done.4
  57.8 2.1 %all_gather.25.r_9_ = bf16[256,768]{1,0:T(8,128)(2,1)S(1)} all-gather(bf16[128,768]{1,0:T(8,128)(2,1)S(1)} %pad_maximum_fusion.2), channel_id=1, replica_groups=mesh['dom'=256,'band'=2] {'band'}, dimensions={0}, use_global_device_ids=true | all-gather | bytes 589824 | tf_op jit(solution)/shard_map/all_gather | solution.py:282
  59.9 2.2 %apply_three.1 = (bf16[128,1536]{1,0:T(8,128)(2,1)}, f32[128,1024]{1,0:T(8,128)S(1)}, bf16[128,512]{1,0:T(8,128)(2,1)S(1)}, bf16[128,512]{1,0:T(8,128)(2,1)S(1)}, bf16[128,256]{1,0:T(8,128)(2,1)S(1)}) custom-call(s32[1]{0:T(128)} %bitcast.band_ref.r_0_, bf16[768,1536]{1,0:T(8,128)(2,1)S(1)} %build.1.mine_ref.r_1_, ...), custom_call_target="tpu_custom_call" | custom-call | tf_op jit(solution)/shard_map/apply_three/pallas_call | solution.py:249
  62.1 2.9 %collective-permute-start.5 = (bf16[128,512]{1,0:T(8,128)(2,1)S(1)}, bf16[128,512]{1,0:T(8,128)(2,1)S(1)}, u32[]{:S(2)}, u32[]{:S(2)}) collective-permute-start(bf16[128,512]{1,0:T(8,128)(2,1)S(1)} %get-tuple-element.45), channel_id=1, source_target_pairs={{1,2},{3,4},{5,6},{7,8},{9,10},{11,12},{13,14},{15,16},{17,18},{19... | collective-permute-start | bytes 393224 | tf_op jit(solution)/shard_map/ppermute | solution.py:269
  64.9 6.6 %all_gather.26 = bf16[256,256]{1,0:T(8,128)(2,1)S(1)} all-gather(bf16[128,256]{1,0:T(8,128)(2,1)S(1)} %get-tuple-element.46), channel_id=1, replica_groups={{1,4},{3,6},{5,8},{7,10},{9,12},{11,14},{13,16},{15,18},{17,20},{19,22}..., dimensions={0}, use_global_device_ids=true | all-gather | bytes 196608 | tf_op jit(solution)/shard_map/all_gather | solution.py:280
  71.5 0.0 collective-permute-done.5
  71.5 2.1 %all_gather.27.got_ref = bf16[256,768]{1,0:T(8,128)(2,1)S(1)} all-gather(bf16[128,768]{1,0:T(8,128)(2,1)S(1)} %pad_maximum_fusion.3), channel_id=1, replica_groups=mesh['dom'=256,'band'=2] {'band'}, dimensions={0}, use_global_device_ids=true | all-gather | bytes 589824 | tf_op jit(solution)/shard_map/all_gather | solution.py:282
  73.6 1.4 apply_four.1
  75.1 31.8 %all_to_all.23 = f32[32,8,128]{2,1,0:T(8,128)S(1)} all-to-all(f32[32,8,128]{2,1,0:T(8,128)S(1)} %bitcast.8), channel_id=1, replica_groups={{0,1,2,3,4,5,6,7,128,129,130,131,132,133,134,135,256,257,258,259,260,26..., dimensions={0} | all-to-all | bytes 262144 | tf_op jit(solution)/shard_map/all_to_all | solution.py:298
  106.9 16.8 %all_to_all.24 = f32[16,8,128]{2,1,0:T(8,128)S(1)} all-to-all(f32[16,8,128]{2,1,0:T(8,128)S(1)} %broadcast_in_dim.7), channel_id=1, replica_groups={{0,8,16,24,32,40,48,56,64,72,80,88,96,104,112,120},{1,9,17,25,33,41,49,..., dimensions={0} | all-to-all | bytes 131072 | tf_op jit(solution)/shard_map/all_to_all | solution.py:298
  123.7 12.8 %all_to_all.25 = f32[32,8,128]{2,1,0:T(8,128)S(1)} all-to-all(f32[32,8,128]{2,1,0:T(8,128)S(1)} %broadcast_in_dim.8), channel_id=1, replica_groups={{0,1,2,3,4,5,6,7,128,129,130,131,132,133,134,135,256,257,258,259,260,26..., dimensions={0} | all-to-all | bytes 262144 | tf_op jit(solution)/shard_map/all_to_all | solution.py:298
  136.5 5.9 %finish.1 = (f32[128,512]{1,0:T(8,128)}, f32[128,128]{1,0:T(8,128)}) custom-call(f32[256,128]{1,0:T(8,128)S(1)} %bitcast.7, bf16[128,512]{1,0:T(8,128)(2,1)S(1)} %get-tuple-element.49.refs_1_), custom_call_target="tpu_custom_call" | custom-call | tf_op jit(solution)/shard_map/finish/pallas_call | solution.py:402
  (13 shorter events, 0.2 us)
Async XLA Ops:
  2.5 19.3 %collective-permute-start = (bf16[80,256]{1,0:T(8,128)(2,1)}, bf16[80,256]{1,0:T(8,128)(2,1)S(1)}, u32[]{:S(2)}, u32[]{:S(2)}) collective-permute-start(bf16[80,256]{1,0:T(8,128)(2,1)} %get-tuple-element.29), channel_id=1, source_target_pairs={{0,2},{2,4},{4,6},{6,8},{8,10},{10,12},{12,14},{14,16},{16,18},{18... | collective-permute-start | bytes 122888 | tf_op jit(solution)/shard_map/ppermute | solution.py:262
  6.5 15.2 %collective-permute-start.1 = (bf16[80,256]{1,0:T(8,128)(2,1)}, bf16[80,256]{1,0:T(8,128)(2,1)S(1)}, u32[]{:S(2)}, u32[]{:S(2)}) collective-permute-start(bf16[80,256]{1,0:T(8,128)(2,1)} %get-tuple-element.30), channel_id=1, source_target_pairs={{2,0},{4,2},{6,4},{8,6},{10,8},{12,10},{14,12},{16,14},{18,16},{20... | collective-permute-start | bytes 122888 | tf_op jit(solution)/shard_map/ppermute | solution.py:262
  10.0 17.9 %copy-start.2 = (bf16[64,1024]{1,0:T(8,128)(2,1)S(1)}, bf16[64,1024]{1,0:T(8,128)(2,1)}, u32[]{:S(2)}) copy-start(bf16[64,1024]{1,0:T(8,128)(2,1)} %refs_1_.1) | copy-start | bytes 393220
  10.0 22.3 %copy-start = (f32[1024]{0:T(1024)S(1)}, f32[1024]{0:T(1024)}, u32[]{:S(2)}) copy-start(f32[1024]{0:T(1024)} %param.11) | copy-start | bytes 12292
  10.0 22.3 %copy-start.1 = (s32[1,2,256]{2,1,0:T(2,128)S(1)}, s32[1,2,256]{2,1,0:T(2,128)}, u32[]{:S(2)}) copy-start(s32[1,2,256]{2,1,0:T(2,128)} %param.8) | copy-start | bytes 6148
  21.8 10.5 %collective-permute-start.2 = (bf16[768,1536]{1,0:T(8,128)(2,1)S(1)}, bf16[768,1536]{1,0:T(8,128)(2,1)}, u32[]{:S(2)}, u32[]{:S(2)}) collective-permute-start(bf16[768,1536]{1,0:T(8,128)(2,1)S(1)} %build.1.mine_ref.r_1_), channel_id=1, source_target_pairs={{0,1},{1,0},{2,3},{3,2},{4,5},{5,4},{6,7},{7,6},{8,9},{9,8},{10,11... | collective-permute-start | bytes 7077896 | tf_op jit(solution)/shard_map/ppermute | solution.py:430
  34.8 10.4 %collective-permute-start.3 = (bf16[128,512]{1,0:T(8,128)(2,1)S(1)}, bf16[128,512]{1,0:T(8,128)(2,1)S(1)}, u32[]{:S(2)}, u32[]{:S(2)}) collective-permute-start(bf16[128,512]{1,0:T(8,128)(2,1)S(1)} %get-tuple-element.37), channel_id=1, source_target_pairs={{1,2},{3,4},{5,6},{7,8},{9,10},{11,12},{13,14},{15,16},{17,18},{19... | collective-permute-start | bytes 393224 | tf_op jit(solution)/shard_map/ppermute | solution.py:269
  49.1 8.6 %collective-permute-start.4 = (bf16[128,512]{1,0:T(8,128)(2,1)S(1)}, bf16[128,512]{1,0:T(8,128)(2,1)S(1)}, u32[]{:S(2)}, u32[]{:S(2)}) collective-permute-start(bf16[128,512]{1,0:T(8,128)(2,1)S(1)} %get-tuple-element.41), channel_id=1, source_target_pairs={{1,2},{3,4},{5,6},{7,8},{9,10},{11,12},{13,14},{15,16},{17,18},{19... | collective-permute-start | bytes 393224 | tf_op jit(solution)/shard_map/ppermute | solution.py:269
  62.1 9.4 %collective-permute-start.5 = (bf16[128,512]{1,0:T(8,128)(2,1)S(1)}, bf16[128,512]{1,0:T(8,128)(2,1)S(1)}, u32[]{:S(2)}, u32[]{:S(2)}) collective-permute-start(bf16[128,512]{1,0:T(8,128)(2,1)S(1)} %get-tuple-element.45), channel_id=1, source_target_pairs={{1,2},{3,4},{5,6},{7,8},{9,10},{11,12},{13,14},{15,16},{17,18},{19... | collective-permute-start | bytes 393224 | tf_op jit(solution)/shard_map/ppermute | solution.py:269

commit v8 on v7

--- a/solution.py
+++ b/solution.py
@@ -208,7 +208,8 @@
 def next_body(chebyshev, *refs):
     band_ref, mine_ref, other_ref, potential_ref, lists_ref, fl_ref, fr_ref, partial_ref, ghost_ref, got_ref = refs[:10]
     older_ref = refs[10] if chebyshev else None
-    x_out, *outs = refs[11:] if chebyshev else refs[10:]
+    rest = refs[11:] if chebyshev else refs[10:]
+    x_out, outs = (rest[-1], rest[:-1]) if chebyshev else (rest[0], rest[1:])
     lists = lists_ref[...]
     own = partial_ref.shape[1]
     new_states(older_ref, x_out, assemble(partial_ref, ghost_ref, got_ref, lists, fl_ref, fr_ref, own))
@@ -446,8 +447,12 @@
         lambda *r: next_body(False, *r), ends + (partial, ghost, got), (x_shape,) + shapes, "apply_two"
     )
     got = exchange(core, near, far)
-    x2, partial, ghost, near, far = stage_call(
-        lambda *r: next_body(True, *r), ends + (partial, ghost, got, x0), (x_shape,) + shapes, "apply_three"
+    partial, ghost, near, far = stage_call(
+        lambda *r: next_body(True, *r),
+        ends + (partial, ghost, got, x0),
+        shapes,
+        "apply_three",
+        (pltpu.VMEM((states, full), BF16),),
     )
     got = exchange(core, near, far)
     own_part, sums = stage_call(

time: 143 us -> 142 us (level)
  no operation moved by 1% of the time
where the time goes in v8:
time: 142 us
  blocking collectives  91.1 us (64%)
  Pallas kernels  26.6 us (19%)
  starting transfers between devices  20.9 us (15%)
  other arithmetic  2.26 us (2%)
    all_to_all x3, blocking collectives, swap_pieces(): return lax.all_to_all(x, BOTH, 0, 0, axis_index_groups=groups, tiled=True)  61.4 us
    all_gather x3, blocking collectives, exchange(): lax.all_gather(far, BOTH, axis_index_groups=far_groups(lax.axis_size('dom...  19 us
    pallas_call x1, Pallas kernels, build(): pl.pallas_call(build_body, out_shape=jax.ShapeDtypeStruct((half, full), B...  11.7 us
    ppermute x3, starting transfers between devices, across(): return lax.ppermute(x, BOTH, pairs)  9.53 us
    pallas_call x4, Pallas kernels, stage_call(): pl.pallas_call(body, out_shape=tuple(shapes), in_specs=[spec(pltpu.SMEM)]...  7.11 us
    all_gather x3, blocking collectives, exchange(): lax.all_gather(jnp.concatenate([near, far], axis=1), 'band', axis=0, tile...  6.44 us
    ppermute x1, starting transfers between devices, shards(): other = lax.ppermute(mine, 'band', [(0, 1), (1, 0)])  6.05 us
    pallas_call x1, Pallas kernels, finish(): pl.pallas_call(lambda *refs: finish_body(scale, *refs), out_shape=(jax.Sh...  5.86 us
  transfers between devices with their start and end apart: 6, of which 0 were waited for; matrix products, arithmetic and copies ran while one was open for 2% of the time, Pallas kernels for 8%

profile of v8, /device:TPU:1, one launch (start us, length us, event | category | flops | bytes accessed | tf_op | source)
XLA Modules:
  0.0 141.8 jit_solution(3157756911439362688)
XLA Ops:
  0.6 1.8 %send_first.1 = (bf16[80,256]{1,0:T(8,128)(2,1)}, bf16[80,256]{1,0:T(8,128)(2,1)}) custom-call(s32[1]{0:T(128)} %bitcast.1.refs_0_, bf16[64,1024]{1,0:T(8,128)(2,1)} %refs_1_.1, s32[2,256]{1,0:T(2,128)} %bitcast.13), custom_call_target="tpu_custom_call" | custom-call | tf_op jit(solution)/shard_map/send_first/pallas_call | solution.py:56
  2.5 4.0 %collective-permute-start = (bf16[80,256]{1,0:T(8,128)(2,1)}, bf16[80,256]{1,0:T(8,128)(2,1)S(1)}, u32[]{:S(2)}, u32[]{:S(2)}) collective-permute-start(bf16[80,256]{1,0:T(8,128)(2,1)} %get-tuple-element.29), channel_id=1, source_target_pairs={{0,2},{2,4},{4,6},{6,8},{8,10},{10,12},{12,14},{14,16},{16,18},{18... | collective-permute-start | bytes 122888 | tf_op jit(solution)/shard_map/ppermute | solution.py:263
  6.5 1.3 collective-permute-start.1
  7.8 0.7 convert_element_type.8
  8.5 0.8 pad_convert_fusion
  9.3 0.7 select_maximum_fusion.packed_ref
  10.0 0.0 copy-start.2
  10.0 0.0 copy-start
  10.0 0.0 copy-start.1
  10.0 11.7 %build.1.mine_ref.r_1_ = bf16[768,1536]{1,0:T(8,128)(2,1)S(1)} custom-call(s32[1]{0:T(128)} %bitcast.band_ref.r_0_, f32[168,128]{1,0:T(8,128)S(1)} %select_maximum_fusion.packed_ref), custom_call_target="tpu_custom_call" | custom-call | flops 9663676416 | bytes 2359296 | tf_op jit(solution)/shard_map/build/pallas_call | solution.py:100
  21.7 0.0 collective-permute-done.r_5_.fl_ref
  21.7 0.0 collective-permute-done.1.r_6_.fr_ref
  21.8 6.0 %collective-permute-start.2 = (bf16[768,1536]{1,0:T(8,128)(2,1)S(1)}, bf16[768,1536]{1,0:T(8,128)(2,1)}, u32[]{:S(2)}, u32[]{:S(2)}) collective-permute-start(bf16[768,1536]{1,0:T(8,128)(2,1)S(1)} %build.1.mine_ref.r_1_), channel_id=1, source_target_pairs={{0,1},{1,0},{2,3},{3,2},{4,5},{5,4},{6,7},{7,6},{8,9},{9,8},{10,11... | collective-permute-start | bytes 7077896 | tf_op jit(solution)/shard_map/ppermute | solution.py:431
  27.8 0.0 copy-done.2
  27.9 4.4 %all_gather.21.x_ref.r_10_ = bf16[128,1536]{1,0:T(8,128)(2,1)S(1)} all-gather(bf16[64,1536]{1,0:T(8,128)(2,1)S(1)} %pad_maximum_fusion), channel_id=1, replica_groups=mesh['dom'=256,'band'=2] {'band'}, dimensions={0}, use_global_device_ids=true | all-gather | bytes 589824 | tf_op jit(solution)/shard_map/all_gather | solution.py:433
  32.2 0.0 collective-permute-done.2.other_hbm
  32.2 0.0 copy-done
  32.2 0.0 copy-done.1
  32.2 2.5 %apply_one.1 = (bf16[768,1536]{1,0:T(8,128)(2,1)S(1)}, f32[128,1024]{1,0:T(8,128)S(1)}, bf16[128,512]{1,0:T(8,128)(2,1)S(1)}, bf16[128,512]{1,0:T(8,128)(2,1)S(1)}, bf16[128,256]{1,0:T(8,128)(2,1)S(1)}) custom-call(s32[1]{0:T(128)} %bitcast.band_ref.r_0_, bf16[768,1536]{1,0:T(8,128)(2,1)S(1)} %build.1.mine_ref.r_1_, ...), custom_call_target="tpu_custom_call" | custom-call | tf_op jit(solution)/shard_map/apply_one/pallas_call | solution.py:250
  34.8 4.5 %collective-permute-start.3 = (bf16[128,512]{1,0:T(8,128)(2,1)S(1)}, bf16[128,512]{1,0:T(8,128)(2,1)S(1)}, u32[]{:S(2)}, u32[]{:S(2)}) collective-permute-start(bf16[128,512]{1,0:T(8,128)(2,1)S(1)} %get-tuple-element.37), channel_id=1, source_target_pairs={{1,2},{3,4},{5,6},{7,8},{9,10},{11,12},{13,14},{15,16},{17,18},{19... | collective-permute-start | bytes 393224 | tf_op jit(solution)/shard_map/ppermute | solution.py:270
  39.3 5.9 %all_gather.22 = bf16[256,256]{1,0:T(8,128)(2,1)S(1)} all-gather(bf16[128,256]{1,0:T(8,128)(2,1)S(1)} %get-tuple-element.38), channel_id=1, replica_groups={{1,4},{3,6},{5,8},{7,10},{9,12},{11,14},{13,16},{15,18},{17,20},{19,22}..., dimensions={0}, use_global_device_ids=true | all-gather | bytes 196608 | tf_op jit(solution)/shard_map/all_gather | solution.py:281
  45.2 0.0 collective-permute-done.3
  45.2 2.3 %all_gather.23.r_9_ = bf16[256,768]{1,0:T(8,128)(2,1)S(1)} all-gather(bf16[128,768]{1,0:T(8,128)(2,1)S(1)} %pad_maximum_fusion.1), channel_id=1, replica_groups=mesh['dom'=256,'band'=2] {'band'}, dimensions={0}, use_global_device_ids=true | all-gather | bytes 589824 | tf_op jit(solution)/shard_map/all_gather | solution.py:283
  47.5 1.6 %apply_two.1 = (bf16[128,1536]{1,0:T(8,128)(2,1)S(1)}, f32[128,1024]{1,0:T(8,128)S(1)}, bf16[128,512]{1,0:T(8,128)(2,1)S(1)}, bf16[128,512]{1,0:T(8,128)(2,1)S(1)}, bf16[128,256]{1,0:T(8,128)(2,1)S(1)}) custom-call(s32[1]{0:T(128)} %bitcast.band_ref.r_0_, bf16[768,1536]{1,0:T(8,128)(2,1)S(1)} %build.1.mine_ref.r_1_, ...), custom_call_target="tpu_custom_call" | custom-call | tf_op jit(solution)/shard_map/apply_two/pallas_call | solution.py:250
  49.1 2.1 %collective-permute-start.4 = (bf16[128,512]{1,0:T(8,128)(2,1)S(1)}, bf16[128,512]{1,0:T(8,128)(2,1)S(1)}, u32[]{:S(2)}, u32[]{:S(2)}) collective-permute-start(bf16[128,512]{1,0:T(8,128)(2,1)S(1)} %get-tuple-element.41), channel_id=1, source_target_pairs={{1,2},{3,4},{5,6},{7,8},{9,10},{11,12},{13,14},{15,16},{17,18},{19... | collective-permute-start | bytes 393224 | tf_op jit(solution)/shard_map/ppermute | solution.py:270
  51.2 6.5 %all_gather.24 = bf16[256,256]{1,0:T(8,128)(2,1)S(1)} all-gather(bf16[128,256]{1,0:T(8,128)(2,1)S(1)} %get-tuple-element.42), channel_id=1, replica_groups={{1,4},{3,6},{5,8},{7,10},{9,12},{11,14},{13,16},{15,18},{17,20},{19,22}..., dimensions={0}, use_global_device_ids=true | all-gather | bytes 196608 | tf_op jit(solution)/shard_map/all_gather | solution.py:281
  57.7 0.0 collective-permute-done.4
  57.8 2.1 %all_gather.25.r_9_ = bf16[256,768]{1,0:T(8,128)(2,1)S(1)} all-gather(bf16[128,768]{1,0:T(8,128)(2,1)S(1)} %pad_maximum_fusion.2), channel_id=1, replica_groups=mesh['dom'=256,'band'=2] {'band'}, dimensions={0}, use_global_device_ids=true | all-gather | bytes 589824 | tf_op jit(solution)/shard_map/all_gather | solution.py:283
  59.9 1.6 %apply_three.1 = (f32[128,1024]{1,0:T(8,128)S(1)}, bf16[128,512]{1,0:T(8,128)(2,1)S(1)}, bf16[128,512]{1,0:T(8,128)(2,1)S(1)}, bf16[128,256]{1,0:T(8,128)(2,1)S(1)}) custom-call(s32[1]{0:T(128)} %bitcast.band_ref.r_0_, bf16[768,1536]{1,0:T(8,128)(2,1)S(1)} %build.1.mine_ref.r_1_, bf16[768,1536]{1,0:T(8,128)(2,1)S(1)} %get-tuple-element.34.r_2_.other_ref, ...), custom_call_target="tpu_custom_call" | custom-call | tf_op jit(solution)/shard_map/apply_three/pallas_call | solution.py:250
  61.4 2.9 %collective-permute-start.5 = (bf16[128,512]{1,0:T(8,128)(2,1)S(1)}, bf16[128,512]{1,0:T(8,128)(2,1)S(1)}, u32[]{:S(2)}, u32[]{:S(2)}) collective-permute-start(bf16[128,512]{1,0:T(8,128)(2,1)S(1)} %get-tuple-element.45), channel_id=1, source_target_pairs={{1,2},{3,4},{5,6},{7,8},{9,10},{11,12},{13,14},{15,16},{17,18},{19... | collective-permute-start | bytes 393224 | tf_op jit(solution)/shard_map/ppermute | solution.py:270
  64.3 6.6 %all_gather.26 = bf16[256,256]{1,0:T(8,128)(2,1)S(1)} all-gather(bf16[128,256]{1,0:T(8,128)(2,1)S(1)} %get-tuple-element.46), channel_id=1, replica_groups={{1,4},{3,6},{5,8},{7,10},{9,12},{11,14},{13,16},{15,18},{17,20},{19,22}..., dimensions={0}, use_global_device_ids=true | all-gather | bytes 196608 | tf_op jit(solution)/shard_map/all_gather | solution.py:281
  70.9 0.0 collective-permute-done.5
  70.9 2.1 %all_gather.27.got_ref = bf16[256,768]{1,0:T(8,128)(2,1)S(1)} all-gather(bf16[128,768]{1,0:T(8,128)(2,1)S(1)} %pad_maximum_fusion.3), channel_id=1, replica_groups=mesh['dom'=256,'band'=2] {'band'}, dimensions={0}, use_global_device_ids=true | all-gather | bytes 589824 | tf_op jit(solution)/shard_map/all_gather | solution.py:283
  73.0 1.4 apply_four.1
  74.5 31.8 %all_to_all.23 = f32[32,8,128]{2,1,0:T(8,128)S(1)} all-to-all(f32[32,8,128]{2,1,0:T(8,128)S(1)} %bitcast.8), channel_id=1, replica_groups={{0,1,2,3,4,5,6,7,128,129,130,131,132,133,134,135,256,257,258,259,260,26..., dimensions={0} | all-to-all | bytes 262144 | tf_op jit(solution)/shard_map/all_to_all | solution.py:299
  106.3 16.8 %all_to_all.24 = f32[16,8,128]{2,1,0:T(8,128)S(1)} all-to-all(f32[16,8,128]{2,1,0:T(8,128)S(1)} %broadcast_in_dim.7), channel_id=1, replica_groups={{0,8,16,24,32,40,48,56,64,72,80,88,96,104,112,120},{1,9,17,25,33,41,49,..., dimensions={0} | all-to-all | bytes 131072 | tf_op jit(solution)/shard_map/all_to_all | solution.py:299
  123.1 12.8 %all_to_all.25 = f32[32,8,128]{2,1,0:T(8,128)S(1)} all-to-all(f32[32,8,128]{2,1,0:T(8,128)S(1)} %broadcast_in_dim.8), channel_id=1, replica_groups={{0,1,2,3,4,5,6,7,128,129,130,131,132,133,134,135,256,257,258,259,260,26..., dimensions={0} | all-to-all | bytes 262144 | tf_op jit(solution)/shard_map/all_to_all | solution.py:299
  135.9 5.9 %finish.1 = (f32[128,512]{1,0:T(8,128)}, f32[128,128]{1,0:T(8,128)}) custom-call(f32[256,128]{1,0:T(8,128)S(1)} %bitcast.7, bf16[128,512]{1,0:T(8,128)(2,1)S(1)} %get-tuple-element.49.refs_1_), custom_call_target="tpu_custom_call" | custom-call | tf_op jit(solution)/shard_map/finish/pallas_call | solution.py:403
  (13 shorter events, 0.2 us)
Async XLA Ops:
  2.5 19.3 %collective-permute-start = (bf16[80,256]{1,0:T(8,128)(2,1)}, bf16[80,256]{1,0:T(8,128)(2,1)S(1)}, u32[]{:S(2)}, u32[]{:S(2)}) collective-permute-start(bf16[80,256]{1,0:T(8,128)(2,1)} %get-tuple-element.29), channel_id=1, source_target_pairs={{0,2},{2,4},{4,6},{6,8},{8,10},{10,12},{12,14},{14,16},{16,18},{18... | collective-permute-start | bytes 122888 | tf_op jit(solution)/shard_map/ppermute | solution.py:263
  6.5 15.2 %collective-permute-start.1 = (bf16[80,256]{1,0:T(8,128)(2,1)}, bf16[80,256]{1,0:T(8,128)(2,1)S(1)}, u32[]{:S(2)}, u32[]{:S(2)}) collective-permute-start(bf16[80,256]{1,0:T(8,128)(2,1)} %get-tuple-element.30), channel_id=1, source_target_pairs={{2,0},{4,2},{6,4},{8,6},{10,8},{12,10},{14,12},{16,14},{18,16},{20... | collective-permute-start | bytes 122888 | tf_op jit(solution)/shard_map/ppermute | solution.py:263
  10.0 17.9 %copy-start.2 = (bf16[64,1024]{1,0:T(8,128)(2,1)S(1)}, bf16[64,1024]{1,0:T(8,128)(2,1)}, u32[]{:S(2)}) copy-start(bf16[64,1024]{1,0:T(8,128)(2,1)} %refs_1_.1) | copy-start | bytes 393220
  10.0 22.3 %copy-start = (f32[1024]{0:T(1024)S(1)}, f32[1024]{0:T(1024)}, u32[]{:S(2)}) copy-start(f32[1024]{0:T(1024)} %param.11) | copy-start | bytes 12292
  10.0 22.3 %copy-start.1 = (s32[1,2,256]{2,1,0:T(2,128)S(1)}, s32[1,2,256]{2,1,0:T(2,128)}, u32[]{:S(2)}) copy-start(s32[1,2,256]{2,1,0:T(2,128)} %param.8) | copy-start | bytes 6148
  21.8 10.5 %collective-permute-start.2 = (bf16[768,1536]{1,0:T(8,128)(2,1)S(1)}, bf16[768,1536]{1,0:T(8,128)(2,1)}, u32[]{:S(2)}, u32[]{:S(2)}) collective-permute-start(bf16[768,1536]{1,0:T(8,128)(2,1)S(1)} %build.1.mine_ref.r_1_), channel_id=1, source_target_pairs={{0,1},{1,0},{2,3},{3,2},{4,5},{5,4},{6,7},{7,6},{8,9},{9,8},{10,11... | collective-permute-start | bytes 7077896 | tf_op jit(solution)/shard_map/ppermute | solution.py:431
  34.8 10.4 %collective-permute-start.3 = (bf16[128,512]{1,0:T(8,128)(2,1)S(1)}, bf16[128,512]{1,0:T(8,128)(2,1)S(1)}, u32[]{:S(2)}, u32[]{:S(2)}) collective-permute-start(bf16[128,512]{1,0:T(8,128)(2,1)S(1)} %get-tuple-element.37), channel_id=1, source_target_pairs={{1,2},{3,4},{5,6},{7,8},{9,10},{11,12},{13,14},{15,16},{17,18},{19... | collective-permute-start | bytes 393224 | tf_op jit(solution)/shard_map/ppermute | solution.py:270
  49.1 8.6 %collective-permute-start.4 = (bf16[128,512]{1,0:T(8,128)(2,1)S(1)}, bf16[128,512]{1,0:T(8,128)(2,1)S(1)}, u32[]{:S(2)}, u32[]{:S(2)}) collective-permute-start(bf16[128,512]{1,0:T(8,128)(2,1)S(1)} %get-tuple-element.41), channel_id=1, source_target_pairs={{1,2},{3,4},{5,6},{7,8},{9,10},{11,12},{13,14},{15,16},{17,18},{19... | collective-permute-start | bytes 393224 | tf_op jit(solution)/shard_map/ppermute | solution.py:270
  61.4 9.5 %collective-permute-start.5 = (bf16[128,512]{1,0:T(8,128)(2,1)S(1)}, bf16[128,512]{1,0:T(8,128)(2,1)S(1)}, u32[]{:S(2)}, u32[]{:S(2)}) collective-permute-start(bf16[128,512]{1,0:T(8,128)(2,1)S(1)} %get-tuple-element.45), channel_id=1, source_target_pairs={{1,2},{3,4},{5,6},{7,8},{9,10},{11,12},{13,14},{15,16},{17,18},{19... | collective-permute-start | bytes 393224 | tf_op jit(solution)/shard_map/ppermute | solution.py:270
